TPU v7x, 32 devices: a whole 2x2x4 slice. The times are simulated.
32 devices in a mesh: seq: 8 (over z, y), fsdp: 4 (over x, core).
Axes of the slice: x: 2, y: 2, z: 4, core: 2. Of those that a mesh axis runs over, the one named last changes fastest.
Arguments:
- queries: bfloat16 [4, 1024, 2048], P('fsdp', 'seq'), may hold values from -160 to 160
- key_rows: bfloat16 [4, 1024, 2048], P('fsdp', 'seq'), may hold values from -4.5 to 4.5
- value_rows: bfloat16 [4, 1024, 2048], P('fsdp', 'seq'), may hold values from -6 to 6
- out_grad: bfloat16 [4, 1024, 2048], P('fsdp', 'seq'), may hold values from -6 to 6
- inputs: bfloat16 [4, 1024, 4096], P('fsdp', 'seq'), may hold values from -6 to 6
- router_weight: bfloat16 [4096], P('fsdp'), may hold values from -0.09375 to 0.09375
- counts: int32 [4, 8], P('fsdp', 'seq'), may hold values from 0 to 128, as said below
- picked_pos: int32 [4, 1024], P('fsdp', 'seq'), may hold values from -1 to 511, as said below
Outputs:
- grad_queries: bfloat16 [4, 1024, 2048], P('fsdp', 'seq')
- grad_keys: bfloat16 [4, 1024, 2048], P('fsdp', 'seq')
- grad_values: bfloat16 [4, 1024, 2048], P('fsdp', 'seq')
- grad_router: float32 [4096], P(('seq', 'fsdp'))
Inputs may be any that keep to these rules, and one draw needn't show every extreme that they name: `counts`: devices 2i and 2i + 1 of a sequence together hold 128 picked tokens; some device of every sequence holds 128 and its partner none. `picked_pos`: the first counts slots of a device hold the local positions of its picked tokens in increasing order, the other slots -1.
All inputs are finite; a program needn't handle non-finite values.
Results may differ from a plain program's by a relative error of at most 0.015.
Values may be sent and summed in bfloat16 or wider, within the bound.
No kernel may reach another device: no remote copies, remote signals or barrier semaphores. Data moves between devices by JAX's collectives and lax.ppermute only.
A program may use at most 128 MiB of HBM per device.

v0:
```python
import math

import jax
import jax.numpy as jnp
from jax import lax
from jax.sharding import PartitionSpec as P

HEADS = 16
HEAD_DIM = 128
TOK_DEV = 512


THETA = 500000.0
NEG = -1e30
BLOCK_ROWS = 512


def swapped(array, axis, apart):
    return lax.ppermute(array, axis, [(i, i ^ 1 << apart) for i in range(lax.axis_size(axis))])


def angle_table(positions):
    half_dim = HEAD_DIM // 2
    inverse_freq = THETA ** (-(jnp.arange(half_dim, dtype=jnp.float32) * 2.0 / HEAD_DIM))
    angles = positions.astype(jnp.float32)[:, None] * inverse_freq[None, :]
    return (jnp.cos(angles), jnp.sin(angles))


def rotate(vectors, cosine, sine, direction):
    row_count = vectors.shape[0]
    parted = vectors.reshape(row_count, HEADS, HEAD_DIM)
    half_dim = HEAD_DIM // 2
    lower_half = parted[:, :, :half_dim]
    upper_half = parted[:, :, half_dim:]
    cos_b = cosine[:, None, :]
    sin_b = direction * sine[:, None, :]
    joined = jnp.concatenate(
        [lower_half * cos_b - upper_half * sin_b, upper_half * cos_b + lower_half * sin_b], axis=2
    )
    return joined.reshape(row_count, HEADS * HEAD_DIM)


def each_block(stepper, state_now, arrays, start_row):
    all_rows = arrays[0].shape[0]
    block_len = math.gcd(all_rows, BLOCK_ROWS)
    for offset in range(0, all_rows, block_len):
        pieces = tuple(
            (lax.slice_in_dim(member, offset, offset + block_len, axis=0) for member in arrays)
        )
        state_now = stepper(state_now, pieces, start_row + offset)
    return state_now


def masked_scores(query_part, key_part, query_start, key_start):
    query_len = query_part.shape[0]
    key_len = key_part.shape[0]
    query_heads = query_part.reshape(query_len, HEADS, HEAD_DIM)
    key_heads = key_part.reshape(key_len, HEADS, HEAD_DIM)
    scores = jnp.einsum(
        "qhd,khd->hqk", query_heads, key_heads, preferred_element_type=jnp.float32
    ) * HEAD_DIM ** (-0.5)
    causal = (query_start + jnp.arange(query_len))[:, None] >= (key_start + jnp.arange(key_len))[
        None, :
    ]
    return (scores, causal[None])


def per_device(queries, key_rows, value_rows, out_grad, inputs, router_weight, counts, picked_pos):
    query_own = queries[0]
    key_own = key_rows[0]
    value_own = value_rows[0]
    grad_own = out_grad[0]
    input_own = inputs[0]
    own_count = counts[0, 0]
    slot_pos = picked_pos[0]
    capacity = query_own.shape[0]
    share = capacity // 2
    width = query_own.shape[1]
    score_scale = HEAD_DIM ** (-0.5)
    router_full = lax.all_gather(router_weight, "fsdp", axis=0, tiled=True)
    gate = jax.nn.sigmoid(jnp.dot(input_own, router_full, preferred_element_type=jnp.float32))
    seq_index = lax.axis_index("seq")
    positions = seq_index * TOK_DEV + slot_pos
    cosine, sine = angle_table(positions)
    query_rot = rotate(query_own.astype(jnp.float32), cosine, sine, 1.0).astype(jnp.bfloat16)
    key_rot = rotate(key_own.astype(jnp.float32), cosine, sine, 1.0).astype(jnp.bfloat16)
    grad_scaled = (gate[:, None] * grad_own.astype(jnp.float32)).astype(jnp.bfloat16)
    stacked = jnp.stack([query_rot, key_rot, value_own, grad_scaled])
    parity = seq_index % 2
    outgoing = jnp.where(parity == 0, stacked[:, share:], stacked[:, :share])
    incoming = swapped(outgoing, "seq", 0)
    even_count = jnp.where(parity == 0, own_count, capacity - own_count)
    surplus = even_count - share
    row_ids = jnp.arange(share)
    source = jnp.where(
        parity == 0,
        jnp.where(row_ids < even_count, row_ids, capacity + row_ids - even_count),
        jnp.where(row_ids < surplus, capacity + row_ids, row_ids - surplus),
    )
    joined = jnp.concatenate([stacked, incoming], axis=1)
    balanced = jnp.take(joined, source, axis=1)
    query_bal = balanced[0]
    key_bal = balanced[1]
    value_bal = balanced[2]
    grad_bal = balanced[3]
    query_start = seq_index * share
    grad_heads = grad_bal.reshape(share, HEADS, HEAD_DIM)
    value_heads = value_bal.reshape(share, HEADS, HEAD_DIM)

    def stats_step(state_now, pieces, start_row):
        key_piece, value_piece = pieces
        row_top, row_sum, weighted = state_now
        scores, causal = masked_scores(query_bal, key_piece, query_start, start_row)
        scores = jnp.where(causal, scores, NEG)
        new_top = jnp.maximum(row_top, jnp.max(scores, axis=-1))
        factor = jnp.exp(row_top - new_top)
        expo = jnp.where(causal, jnp.exp(scores - new_top[..., None]), 0.0)
        row_sum = row_sum * factor + jnp.sum(expo, axis=-1)
        piece_heads = value_piece.reshape(value_piece.shape[0], HEADS, HEAD_DIM)
        update = jnp.einsum(
            "hqk,khd->hqd",
            expo.astype(jnp.bfloat16),
            piece_heads,
            preferred_element_type=jnp.float32,
        )
        return (new_top, row_sum, weighted * factor[..., None] + update)

    stats_init = (
        jnp.full((HEADS, share), NEG, jnp.float32),
        jnp.zeros((HEADS, share), jnp.float32),
        jnp.zeros((HEADS, share, HEAD_DIM), jnp.float32),
    )

    def make_query_step(log_total, delta):

        def query_step(grad_query, pieces, start_row):
            key_piece, value_piece = pieces
            piece_len = key_piece.shape[0]
            scores, causal = masked_scores(query_bal, key_piece, query_start, start_row)
            weights_bf = jnp.where(causal, jnp.exp(scores - log_total[..., None]), 0.0).astype(
                jnp.bfloat16
            )
            piece_values = value_piece.reshape(piece_len, HEADS, HEAD_DIM)
            piece_keys = key_piece.reshape(piece_len, HEADS, HEAD_DIM)
            grad_probs = jnp.einsum(
                "qhd,khd->hqk", grad_heads, piece_values, preferred_element_type=jnp.float32
            )
            grad_scores = (
                score_scale * weights_bf.astype(jnp.float32) * (grad_probs - delta[..., None])
            ).astype(jnp.bfloat16)
            return grad_query + jnp.einsum(
                "hqk,khd->qhd", grad_scores, piece_keys, preferred_element_type=jnp.float32
            )

        return query_step

    query_zero = jnp.zeros((share, HEADS, HEAD_DIM), jnp.float32)
    row_top, row_sum, weighted = each_block(
        stats_step,
        stats_init,
        (
            lax.all_gather(key_bal, "seq", axis=0, tiled=True),
            lax.all_gather(value_bal, "seq", axis=0, tiled=True),
        ),
        jnp.int32(0),
    )
    log_total = row_top + jnp.log(row_sum)
    attended = weighted / row_sum[..., None]
    delta = jnp.sum(grad_heads.astype(jnp.float32).transpose(1, 0, 2) * attended, axis=-1)
    log_total, delta = (log_total, delta)
    query_step = make_query_step(log_total, delta)
    grad_query = each_block(
        query_step,
        query_zero,
        (
            lax.all_gather(key_bal, "seq", axis=0, tiled=True),
            lax.all_gather(value_bal, "seq", axis=0, tiled=True),
        ),
        jnp.int32(0),
    )
    row_stats = lax.all_gather(jnp.stack([log_total.T, delta.T]), "seq", axis=1, tiled=True)

    def key_step(state_now, pieces, start_row):
        grad_key, grad_value = state_now
        query_piece, grad_piece = pieces
        piece_len = query_piece.shape[0]
        total_piece = lax.dynamic_slice_in_dim(row_stats[0], start_row, piece_len, 0).T
        delta_piece = lax.dynamic_slice_in_dim(row_stats[1], start_row, piece_len, 0).T
        scores, causal = masked_scores(query_piece, key_bal, start_row, query_start)
        weights_bf = jnp.where(causal, jnp.exp(scores - total_piece[..., None]), 0.0).astype(
            jnp.bfloat16
        )
        piece_grads = grad_piece.reshape(piece_len, HEADS, HEAD_DIM)
        piece_queries = query_piece.reshape(piece_len, HEADS, HEAD_DIM)
        grad_value = grad_value + jnp.einsum(
            "hqk,qhd->khd", weights_bf, piece_grads, preferred_element_type=jnp.float32
        )
        grad_probs = jnp.einsum(
            "qhd,khd->hqk", piece_grads, value_heads, preferred_element_type=jnp.float32
        )
        grad_scores = (
            score_scale * weights_bf.astype(jnp.float32) * (grad_probs - delta_piece[..., None])
        ).astype(jnp.bfloat16)
        grad_key = grad_key + jnp.einsum(
            "hqk,qhd->khd", grad_scores, piece_queries, preferred_element_type=jnp.float32
        )
        return (grad_key, grad_value)

    grad_key, grad_value = each_block(
        key_step,
        (query_zero, query_zero),
        (
            lax.all_gather(query_bal, "seq", axis=0, tiled=True),
            lax.all_gather(grad_bal, "seq", axis=0, tiled=True),
        ),
        jnp.int32(0),
    )
    delta_sum = jnp.sum(delta, axis=0)
    slot_ids = jnp.arange(capacity)
    source_back = jnp.where(
        parity == 0,
        slot_ids,
        jnp.where(slot_ids + surplus >= 0, slot_ids + surplus, share + even_count + slot_ids),
    )
    source_back = jnp.clip(source_back, 0, capacity - 1)
    is_valid = slot_ids < own_count
    payload = jnp.stack(
        [
            grad_query.reshape(share, width),
            grad_key.reshape(share, width),
            grad_value.reshape(share, width),
        ]
    )
    payload_back, delta_back = (
        swapped(payload.astype(jnp.bfloat16), "seq", 0).astype(payload.dtype),
        swapped(delta_sum.astype(jnp.bfloat16), "seq", 0).astype(delta_sum.dtype),
    )
    joined_grads = jnp.concatenate([payload, payload_back], axis=1)
    gathered = jnp.where(is_valid[None, :, None], jnp.take(joined_grads, source_back, axis=1), 0.0)
    grad_q = rotate(gathered[0], cosine, sine, -1.0).astype(jnp.bfloat16)
    grad_k = rotate(gathered[1], cosine, sine, -1.0).astype(jnp.bfloat16)
    grad_v = gathered[2].astype(jnp.bfloat16)
    joined_delta = jnp.concatenate([delta_sum, delta_back])
    router_term = jnp.where(is_valid, (1.0 - gate) * jnp.take(joined_delta, source_back), 0.0)
    partial_value = jnp.dot(
        router_term, input_own.astype(jnp.float32), precision=lax.Precision.HIGHEST
    )
    grad_router = lax.psum_scatter(partial_value, ("seq", "fsdp"), scatter_dimension=0, tiled=True)
    return (grad_q[None], grad_k[None], grad_v[None], grad_router)


def solution(mesh):
    placed = (
        P("fsdp", "seq", None),
        P("fsdp", "seq", None),
        P("fsdp", "seq", None),
        P("fsdp", "seq", None),
        P("fsdp", "seq", None),
        P("fsdp"),
        P("fsdp", "seq"),
        P("fsdp", "seq"),
    )
    return jax.shard_map(
        per_device,
        mesh=mesh,
        in_specs=placed,
        out_specs=(
            P("fsdp", "seq", None),
            P("fsdp", "seq", None),
            P("fsdp", "seq", None),
            P(("seq", "fsdp")),
        ),
        check_vma=False,
    )
```

profile of v0, /device:TPU:0, one launch (start us, length us, event | category | flops | bytes accessed | tf_op | source)
XLA Modules:
  0.0 389.8 jit_solution(5234456993486226784)
XLA Ops:
  7.3 6.4 %all_gather.20 = bf16[4096]{0:T(1024)(128)(2,1)S(1)} all-gather(bf16[1024]{0:T(1024)(128)(2,1)} %param.13), channel_id=1, replica_groups=mesh['seq'=8,'fsdp'=4] {'fsdp'}, dimensions={0}, use_global_device_ids=true | all-gather | bytes 10240 | tf_op jit(solution)/shard_map/all_gather | solution.py:80
  23.0 23.2 %collective-permute-done = bf16[4,64,2048]{2,1,0:T(8,128)(2,1)} collective-permute-done((bf16[4,64,2048]{2,1,0:T(8,128)(2,1)}, bf16[4,64,2048]{2,1,0:T(8,128)(2,1)}, u32[]{:S(2)}, u32[]{:S(2)}) %collective-permute-start) | collective-permute-done | bytes 1048608 | tf_op jit(solution)/shard_map/ppermute | solution.py:19
  47.5 4.1 %copy.168 = bf16[4,192,2048]{2,0,1:T(4,128)(2,1)} copy(bf16[4,192,2048]{2,1,0:T(8,128)(2,1)S(1)} %pad_maximum_fusion) | data formatting | bytes 6291456 | tf_op jit(solution)/shard_map/concatenate | solution.py:100
  51.6 3.3 gather_fusion
  55.5 6.6 %slice_reduce_fusion = (bf16[64,2048]{1,0:T(8,128)(2,1)S(1)}, bf16[64,2048]{1,0:T(8,128)(2,1)}, bf16[64,2048]{1,0:T(8,128)(2,1)}, bf16[64,2048]{1,0:T(8,128)(2,1...) fusion(bf16[4,64,2048]{2,0,1:T(4,128)(2,1)S(1)} %select_bitcast, ...), kind=kLoop, calls=%fused_computation.132 | loop fusion | bytes 3145728 | tf_op jit(solution)/shard_map/slice | solution.py:104
  66.8 47.1 %all-gather.9.cloned.1.call-done = bf16[1,512,2048]{2,1,0:T(8,128)(2,1)} async-done(((bf16[1,64,2048]{2,1,0:T(8,128)(2,1)}), bf16[1,512,2048]{2,1,0:T(8,128)(2,1)}) %all-gather.9.cloned.1.call-update) | async-done | bytes 2097168 | tf_op jit(solution)/shard_map/all_gather | solution.py:176
  113.9 2.9 copy.170
  116.8 47.1 %all-gather.11.cloned.1.call-done = bf16[1,512,2048]{2,1,0:T(8,128)(2,1)} async-done(((bf16[1,64,2048]{2,1,0:T(8,128)(2,1)}), bf16[1,512,2048]{2,1,0:T(8,128)(2,1)}) %all-gather.11.cloned.1.call-update) | async-done | bytes 2097168 | tf_op jit(solution)/shard_map/all_gather | solution.py:177
  163.8 4.0 %copy.174 = bf16[1,512,2048]{1,2,0:T(8,128)(2,1)} copy(bf16[1,512,2048]{2,1,0:T(8,128)(2,1)} %all-gather.11.cloned.1.call-done) | data formatting | bytes 4194304 | tf_op jit(solution)/shard_map/all_gather | solution.py:177
  173.4 4.6 %fusion.6 = f32[64,16,128]{2,0,1:T(8,128)} fusion(bf16[512,16,128]{0,2,1:T(8,128)(2,1)S(1)} %bitcast.136, bf16[512,16,128]{0,2,1:T(8,128)(2,1)} %bitcast.139, f32[16,64,512]{2,1,0:T(8,128)} %copy-done.3, f32[16,64]{1,0:T(8,128)S(1)} %get-tuple-element.29, f32[16,64]{1,0:T(8,128)S(1)} %get-tuple-element.54, pred[64,512]{1,0:T(8,128)(4,1)S(1)} %iota_compare_fusion.1, ...), kind=kOutput, calls=%fused_computation.20 | convolution fusion | flops 273154048 | bytes 7118848 | tf_op jit(solution)/shard_map/hqk,khd->qhd/dot_general | solution.py:151
  180.3 32.2 %all_gather.24 = f32[2,512,16]{2,0,1:T(2,128)S(1)} all-gather(f32[2,64,16]{2,0,1:T(2,128)S(1)} %copy.185), channel_id=1, replica_groups=mesh['seq'=8,'fsdp'=4] {'seq'}, dimensions={1}, use_global_device_ids=true | all-gather | bytes 73728 | tf_op jit(solution)/shard_map/all_gather | solution.py:181
  213.1 5.8 %all-gather.13.cloned.1.call-done = bf16[1,512,2048]{2,1,0:T(8,128)(2,1)} async-done(((bf16[1,64,2048]{2,1,0:T(8,128)(2,1)}), bf16[1,512,2048]{2,1,0:T(8,128)(2,1)}) %all-gather.13.cloned.1.call-update) | async-done | bytes 2097168 | tf_op jit(solution)/shard_map/all_gather | solution.py:213
  218.9 2.9 copy.182
  224.1 2.6 select_convert_fusion
  226.7 42.8 %all-gather.15.cloned.1.call-done = bf16[1,512,2048]{2,1,0:T(8,128)(2,1)} async-done(((bf16[1,64,2048]{2,1,0:T(8,128)(2,1)}), bf16[1,512,2048]{2,1,0:T(8,128)(2,1)}) %all-gather.15.cloned.1.call-update) | async-done | bytes 2097168 | tf_op jit(solution)/shard_map/all_gather | solution.py:214
  269.5 2.9 copy.188
  272.4 2.8 convolution_bitcast_fusion
  275.2 3.8 fusion.5
  289.8 16.3 %collective-permute-done.2 = bf16[64]{0:T(256)(128)(2,1)S(1)} collective-permute-done((bf16[64]{0:T(256)(128)(2,1)S(1)}, bf16[64]{0:T(256)(128)(2,1)S(1)}, u32[]{:S(2)}, u32[]{:S(2)}) %collective-permute-start.2) | collective-permute-done | bytes 160 | tf_op jit(solution)/shard_map/ppermute | solution.py:19
  307.9 39.7 %all-reduce = f32[4096]{0:T(1024)S(1)} all-reduce(f32[4096]{0:T(1024)S(1)} %bitcast.147), channel_id=6, replica_groups=mesh['seq'=8,'fsdp'=4] {'seq','fsdp'}, use_global_device_ids=true, to_apply=%region_4.5.clone | all-reduce | flops 4096 | bytes 32768
  348.7 4.1 %copy.196 = f32[3,128,2048]{2,0,1:T(4,128)} copy(f32[3,128,2048]{2,1,0:T(8,128)S(1)} %pad_maximum_fusion.1) | data formatting | bytes 6291456 | tf_op jit(solution)/shard_map/concatenate | solution.py:238
  352.8 6.9 %gather_fusion.1 = f32[128,3,2048]{2,1,0:T(4,128)} fusion(f32[3,128,2048]{2,0,1:T(4,128)} %copy.196, s32[1024]{0:T(1024)S(1)} %pad_clamp_fusion), kind=kCustom, calls=%fused_computation.1 | custom fusion | bytes 6291968 | tf_op jit(solution)/shard_map/jit(_take)/gather | solution.py:239
  359.8 4.0 %select_bitcast_fusion = f32[3,128,2048]{2,0,1:T(4,128)S(1)} fusion(f32[128,3,2048]{2,1,0:T(4,128)} %gather_fusion.1, pred[128]{0:T(512)(128)(4,1)S(1)} %iota_compare_fusion.2, pred[128]{0:T(512)(128)(4,1)S(1)} %compare_and_fusion.1), kind=kLoop, calls=%fused_computation.3 | loop fusion | flops 1572864 | bytes 6291712 | tf_op jit(solution)/shard_map/jit(_where)/select_n | solution.py:239
  374.6 2.5 copy.212
  (104 shorter events, 56.4 us)
Async XLA Ops:
  7.2 10.1 %copy-start = (bf16[1,128,4096]{2,1,0:T(8,128)(2,1)S(1)}, bf16[1,128,4096]{2,1,0:T(8,128)(2,1)}, u32[]{:S(2)}) copy-start(bf16[1,128,4096]{2,1,0:T(8,128)(2,1)} %param.12) | copy-start | bytes 3145732
  7.2 9.0 %copy-start.9 = (s32[1,128]{1,0:T(1,128)S(1)}, s32[1,128]{1,0:T(1,128)}, u32[]{:S(2)}) copy-start(s32[1,128]{1,0:T(1,128)} %param.15) | copy-start | bytes 1540
  7.2 106.7 %all-gather.9.cloned.1.call-start = ((), (), s32[]{:S(2)}) async-start(), calls=%async_computation | async-start | bytes 2359296 | tf_op jit(solution)/shard_map/all_gather | solution.py:176
  16.8 2.1 copy-start.7
  20.2 25.9 %collective-permute-start = (bf16[4,64,2048]{2,1,0:T(8,128)(2,1)}, bf16[4,64,2048]{2,1,0:T(8,128)(2,1)}, u32[]{:S(2)}, u32[]{:S(2)}) collective-permute-start(bf16[4,64,2048]{2,1,0:T(8,128)(2,1)} %slice_select_fusion), channel_id=1, source_target_pairs={{0,4},{4,0},{8,12},{12,8},{16,20},{20,16},{24,28},{28,24},{1,5},{5... | collective-permute-start | bytes 3145736 | tf_op jit(solution)/shard_map/ppermute | solution.py:19
  63.0 100.9 %all-gather.11.cloned.1.call-start = ((), (), s32[]{:S(2)}) async-start(), calls=%async_computation.1 | async-start | bytes 2359296 | tf_op jit(solution)/shard_map/all_gather | solution.py:177
  63.9 155.0 %all-gather.13.cloned.1.call-start = ((), (), s32[]{:S(2)}) async-start(), calls=%async_computation.2 | async-start | bytes 2359296 | tf_op jit(solution)/shard_map/all_gather | solution.py:213
  64.9 204.7 %all-gather.15.cloned.1.call-start = ((), (), s32[]{:S(2)}) async-start(), calls=%async_computation.3 | async-start | bytes 2359296 | tf_op jit(solution)/shard_map/all_gather | solution.py:214
  167.8 2.4 copy-start.8
  169.4 3.9 %copy-start.3 = (f32[16,64,512]{2,1,0:T(8,128)}, f32[16,64,512]{2,1,0:T(8,128)S(1)}, u32[]{:S(2)}) copy-start(f32[16,64,512]{2,1,0:T(8,128)S(1)} %get-tuple-element.61) | copy-start | bytes 6291460
  169.4 2.4 copy-start.6
  221.8 4.9 %copy-start.2 = (bf16[1,512,2048]{1,2,0:T(8,128)(2,1)}, bf16[1,512,2048]{1,2,0:T(8,128)(2,1)S(1)}, u32[]{:S(2)}) copy-start(bf16[1,512,2048]{1,2,0:T(8,128)(2,1)S(1)} %copy.182) | copy-start | bytes 6291460
  279.1 4.2 %copy-start.5 = (f32[64,16,128]{2,0,1:T(8,128)S(1)}, f32[64,16,128]{2,0,1:T(8,128)}, u32[]{:S(2)}) copy-start(f32[64,16,128]{2,0,1:T(8,128)} %convolution_bitcast_fusion) | copy-start | bytes 1572868
  279.1 6.4 %copy-start.1 = (f32[3,64,2048]{2,1,0:T(8,128)S(1)}, f32[3,64,2048]{2,1,0:T(8,128)}, u32[]{:S(2)}) copy-start(f32[3,64,2048]{2,1,0:T(8,128)} %constant_dynamic-update-slice_fusion.2) | copy-start | bytes 4718596
  287.6 60.6 %collective-permute-start.1 = (bf16[3,64,2048]{2,1,0:T(8,128)(2,1)}, bf16[3,64,2048]{2,1,0:T(8,128)(2,1)S(1)}, u32[]{:S(2)}, u32[]{:S(2)}) collective-permute-start(bf16[3,64,2048]{2,1,0:T(8,128)(2,1)} %convert_element_type.130), channel_id=1, source_target_pairs={{0,4},{4,0},{8,12},{12,8},{16,20},{20,16},{24,28},{28,24},{1,5},{5... | collective-permute-start | bytes 2359304 | tf_op jit(solution)/shard_map/ppermute | solution.py:19
  288.2 17.8 %collective-permute-start.2 = (bf16[64]{0:T(256)(128)(2,1)S(1)}, bf16[64]{0:T(256)(128)(2,1)S(1)}, u32[]{:S(2)}, u32[]{:S(2)}) collective-permute-start(bf16[64]{0:T(256)(128)(2,1)S(1)} %convert_element_type.134), channel_id=1, source_target_pairs={{0,4},{4,0},{8,12},{12,8},{16,20},{20,16},{24,28},{28,24},{1,5},{5... | collective-permute-start | bytes 392 | tf_op jit(solution)/shard_map/ppermute | solution.py:19
  374.6 2.5 copy-start.4
Sparse Core Ops, SparseCore 0:
  63.1 50.7 all-gather.8
  116.0 47.7 all-gather.10
  166.0 52.9 all-gather.12
  220.9 48.5 all-gather.14
where the time goes:
time: 391 us; the launch traced here: 390 us
  waiting for transfers between devices  182 us (47%)
  blocking collectives  78.3 us (20%)
  local copies, waits for them, and re-layouts  77.9 us (20%)
  matrix products  17.9 us (5%)
  between operations  14.9 us (4%)
  other arithmetic  14 us (4%)
  starting transfers between devices  4.43 us (1%)
    all_gather x1, waiting for transfers between devices, per_device(): lax.all_gather(key_bal, 'seq', axis=0, tiled=True)  47.1 us
    all_gather x1, waiting for transfers between devices, per_device(): lax.all_gather(value_bal, 'seq', axis=0, tiled=True)  47.1 us
    all_gather x1, waiting for transfers between devices, per_device(): lax.all_gather(grad_bal, 'seq', axis=0, tiled=True)  42.8 us
    unnamed x1, blocking collectives  39.7 us
    ppermute x3, waiting for transfers between devices, swapped(): lax.ppermute(array, axis, [(i, i ^ 1 << apart) for i in range(lax.axis_si...  39.5 us
    all_gather x1, blocking collectives, per_device(): lax.all_gather(jnp.stack([log_total.T, delta.T]), 'seq', axis=1, tiled=True)  32.2 us
    unnamed x30, local copies, waits for them, and re-layouts  17.3 us
  transfers between devices with their start and end apart: 7, of which 6 were waited for; matrix products, arithmetic and copies ran while one was open for 8% of the time, Pallas kernels for 0%

commit v1 on v0

v1 whole, which is shorter than its diff:
```python
import functools

import jax
import jax.numpy as jnp
import numpy as np
from jax import lax
from jax.experimental import pallas as pl
from jax.experimental.pallas import tpu as pltpu
from jax.sharding import PartitionSpec as P

HEADS = 16
HEAD_DIM = 128
HALF_DIM = HEAD_DIM // 2
TOK_DEV = 512
THETA = 500000.0
NEG = -1e30
SCALE = HEAD_DIM ** -0.5
BF16 = jnp.bfloat16
F32 = jnp.float32
PARAMS = pltpu.CompilerParams(vmem_limit_bytes=40 * 1024 * 1024)
VMEM = pl.BlockSpec(memory_space=pltpu.VMEM)
SMEM = pl.BlockSpec(memory_space=pltpu.SMEM)


def swapped(array, apart):
    return lax.ppermute(array, "seq", [(i, i ^ apart) for i in range(lax.axis_size("seq"))])


def dot(a, b, contract):
    return lax.dot_general(a, b, ((contract[0], contract[1]), ((), ())), preferred_element_type=F32)


def pack_matrices(place, cap):
    parity, first = place[0], place[2]
    row = lax.broadcasted_iota(jnp.int32, (cap, cap), 0)
    slot = lax.broadcasted_iota(jnp.int32, (cap, cap), 1)
    even = jnp.where((row == slot) & (row < first), 1.0, 0.0)
    odd = jnp.where((row == slot + first) & (row >= first), 1.0, 0.0)
    is_even = parity == 0
    own = jnp.where(is_even, even, odd).astype(BF16)
    other = jnp.where(is_even, odd, even).astype(BF16)
    return own, other


def rolled(vectors):
    return pltpu.roll(vectors, HALF_DIM, 1)


def pack_kernel(groups, chunk, place, freq_ref, note_own, note_in, *refs):
    if chunk == 0:
        q_ref, k_ref, v_ref, g_ref, in_ref, *outs, table_ref = refs
    else:
        q_ref, k_ref, v_ref, g_ref, in_ref, table_ref, *outs = refs
    cap = q_ref.shape[0]
    group, first = place[1], place[2]
    own_hot, in_hot = pack_matrices(place, cap)
    row = lax.broadcasted_iota(jnp.int32, (cap, HEAD_DIM), 0)
    lane = lax.broadcasted_iota(jnp.int32, (cap, HEAD_DIM), 1)
    if chunk == 0:
        is_even = place[0] == 0
        note_a = jnp.where(is_even, note_own[...], note_in[...])
        note_b = jnp.where(is_even, note_in[...], note_own[...])
        note = jnp.where(row < first, note_a, pltpu.roll(note_b, first, 0))
        turned = rolled(note)
        position = jnp.where(lane < HALF_DIM, note, turned)
        gate = jnp.where(lane < HALF_DIM, turned, note)
        angle = position * freq_ref[0:1, :]
        cosine = jnp.cos(angle)
        sine = jnp.where(lane < HALF_DIM, -1.0, 1.0) * jnp.sin(angle)
        table_ref[0] = cosine
        table_ref[1] = sine
        table_ref[2] = gate
    else:
        cosine, sine, gate = table_ref[0], table_ref[1], table_ref[2]

    for m in range(groups):
        columns = pl.ds(pl.multiple_of((group ^ m) * HEAD_DIM, HEAD_DIM), HEAD_DIM)
        for t, ref in enumerate((q_ref, k_ref, v_ref, g_ref)):
            rows = dot(own_hot, ref[:, columns], ((1,), (0,)))
            rows += dot(in_hot, in_ref[t, :, columns], ((1,), (0,)))
            if t < 2:
                rows = rows * cosine + rolled(rows) * sine
            elif t == 3:
                rows = rows * gate
            outs[m][t] = rows.astype(BF16)


def attention_kernel(groups, place, *refs):
    ins, outs, delta_ref, rows_ref, dk_ref, dv_ref = (
        refs[:groups], refs[groups:2 * groups], refs[2 * groups], refs[2 * groups + 1], refs[2 * groups + 2],
        refs[2 * groups + 3],
    )
    cap = ins[0].shape[1]
    group = place[1]
    for m in range(groups):
        start = pl.multiple_of((group ^ m) * cap, cap)
        for t in range(4):
            rows_ref[t, pl.ds(start, cap), :] = ins[m][t]
    dk_ref[...] = jnp.zeros_like(dk_ref)
    dv_ref[...] = jnp.zeros_like(dv_ref)
    key = lax.broadcasted_iota(jnp.int32, (cap, cap), 0)
    query = lax.broadcasted_iota(jnp.int32, (cap, cap), 1)
    kept = query >= key
    for i in range(groups):
        here = pl.ds(i * cap, cap)
        q, g = rows_ref[0, here, :], rows_ref[3, here, :]
        upto = (i + 1) * cap
        k, v = rows_ref[1, :upto, :], rows_ref[2, :upto, :]
        s = dot(k, q, ((1,), (1,))) * SCALE
        last = jnp.where(kept, s[i * cap:], NEG)
        s = last if i == 0 else jnp.concatenate([s[:i * cap], last], axis=0)
        top = jnp.max(s, axis=0, keepdims=True)
        e = jnp.exp(s - top)
        p = e * (1.0 / jnp.sum(e, axis=0, keepdims=True))
        dp = dot(v, g, ((1,), (1,)))
        delta = jnp.sum(p * dp, axis=0, keepdims=True)
        delta_ref[:, i * cap:upto] = jnp.broadcast_to(delta, (8, cap))
        p16 = p.astype(BF16)
        ds = (p16.astype(F32) * (dp - delta) * SCALE).astype(BF16)
        dv_ref[:upto, :] += dot(p16, g, ((1,), (0,)))
        dk_ref[:upto, :] += dot(ds, q, ((1,), (0,)))
        rows_ref[0, here, :] = dot(ds, k, ((0,), (0,))).astype(BF16)
    for m in range(groups):
        block = pl.ds(pl.multiple_of((group ^ m) * cap, cap), cap)
        outs[m][0] = rows_ref[0, block, :]
        outs[m][1] = dk_ref[block, :].astype(BF16)
        outs[m][2] = dv_ref[block, :].astype(BF16)


def unpack_kernel(groups, place, table_ref, *refs):
    ins, own_ref, send_ref = refs[:groups], refs[groups], refs[groups + 1]
    cap = ins[0].shape[1]
    group = place[1]
    own_hot, in_hot = pack_matrices(place, cap)
    cosine, sine = table_ref[0], table_ref[1]
    for m in range(groups):
        columns = pl.ds(pl.multiple_of((group ^ m) * HEAD_DIM, HEAD_DIM), HEAD_DIM)
        for t in range(3):
            rows = ins[m][t]
            if t < 2:
                rows = rows.astype(F32)
                rows = (rows * cosine - rolled(rows) * sine).astype(BF16)
            own_ref[t, :, columns] = dot(own_hot, rows, ((0,), (0,))).astype(BF16)
            send_ref[t, :, columns] = dot(in_hot, rows, ((0,), (0,))).astype(BF16)


def place_kernel(chunks, place, *refs):
    owns, others, outs = refs[:chunks], refs[chunks:2 * chunks], refs[2 * chunks:]
    parity = place[0]
    wide = owns[0].shape[2]
    for c in range(chunks):
        own = pl.ds(pl.multiple_of((parity * chunks + c) * wide, wide), wide)
        other = pl.ds(pl.multiple_of(((1 - parity) * chunks + c) * wide, wide), wide)
        for t in range(3):
            outs[t][:, own] = owns[c][t]
            outs[t][:, other] = others[c][t]


def per_device(queries, key_rows, value_rows, out_grad, inputs, router_weight, counts, picked_pos):
    arrays = (queries[0], key_rows[0], value_rows[0], out_grad[0])
    input_own = inputs[0]
    own_count = counts[0, 0]
    cap, width = arrays[0].shape
    seq_size = lax.axis_size("seq")
    groups = seq_size // 2
    chunks = HEADS // seq_size
    wide = groups * HEAD_DIM
    seq_index = lax.axis_index("seq")
    parity, group = seq_index % 2, seq_index // 2
    first = jnp.where(parity == 0, own_count, cap - own_count)
    place = jnp.stack([parity, group, first]).astype(jnp.int32)

    arrived = []
    for c in range(chunks):
        begin = ((1 - parity) * chunks + c) * wide
        arrived.append(swapped(jnp.stack([lax.dynamic_slice_in_dim(a, begin, wide, 1) for a in arrays]), 1))

    router_full = lax.all_gather(router_weight, "fsdp", axis=0, tiled=True)
    gate = jax.nn.sigmoid(jnp.dot(input_own, router_full, preferred_element_type=F32))
    position = (seq_index * TOK_DEV + picked_pos[0]).astype(F32)
    note = jnp.where(jnp.arange(HEAD_DIM)[None, :] < HALF_DIM, position[:, None], gate[:, None])
    note_in = swapped(note, 1)

    power = THETA ** (-(np.arange(HALF_DIM) * 2.0 / HEAD_DIM))
    freq = jnp.asarray(np.broadcast_to(np.tile(power, 2).astype(np.float32), (8, HEAD_DIM)))

    piece = jax.ShapeDtypeStruct((4, cap, HEAD_DIM), BF16)
    table = None
    grads, deltas = [], []
    for c in range(chunks):
        block = pl.BlockSpec((cap, wide), lambda i, at, c=c: (0, at[0] * chunks + c))
        outs = pl.pallas_call(
            functools.partial(pack_kernel, groups, c),
            grid_spec=pltpu.PrefetchScalarGridSpec(
                num_scalar_prefetch=1,
                grid=(1,),
                in_specs=[VMEM] * 3 + [block] * 4 + [VMEM] + ([] if c == 0 else [VMEM]),
                out_specs=[VMEM] * (groups + (1 if c == 0 else 0)),
            ),
            out_shape=[piece] * groups + ([jax.ShapeDtypeStruct((3, cap, HEAD_DIM), F32)] if c == 0 else []),
            compiler_params=PARAMS,
            name=f"pack_{c}",
        )(place, freq, note, note_in, *arrays, arrived[c], *([] if c == 0 else [table]))
        if c == 0:
            table = outs[groups]
        pieces = [outs[0]] + [swapped(outs[m], 2 * m) for m in range(1, groups)]
        total = groups * cap
        outs = pl.pallas_call(
            functools.partial(attention_kernel, groups),
            in_specs=[SMEM] + [VMEM] * groups,
            out_specs=[VMEM] * (groups + 1),
            out_shape=[jax.ShapeDtypeStruct((3, cap, HEAD_DIM), BF16)] * groups
            + [jax.ShapeDtypeStruct((8, total), F32)],
            scratch_shapes=[
                pltpu.VMEM((4, total, HEAD_DIM), BF16),
                pltpu.VMEM((total, HEAD_DIM), F32),
                pltpu.VMEM((total, HEAD_DIM), F32),
            ],
            compiler_params=PARAMS,
            name=f"attention_{c}",
        )(place, *pieces)
        grads.append(outs[:groups])
        deltas.append(outs[groups][0])

    owns, others = [], []
    for c in range(chunks):
        pieces = [grads[c][0]] + [swapped(grads[c][m], 2 * m) for m in range(1, groups)]
        slots = jax.ShapeDtypeStruct((3, cap, wide), BF16)
        own, send = pl.pallas_call(
            functools.partial(unpack_kernel, groups),
            in_specs=[SMEM] + [VMEM] * (groups + 1),
            out_specs=[VMEM] * 2,
            out_shape=[slots] * 2,
            compiler_params=PARAMS,
            name=f"unpack_{c}",
        )(place, table, *pieces)
        owns.append(own)
        others.append(swapped(send, 1))
    grad_q, grad_k, grad_v = pl.pallas_call(
        functools.partial(place_kernel, chunks),
        in_specs=[SMEM] + [VMEM] * (2 * chunks),
        out_specs=[VMEM] * 3,
        out_shape=[jax.ShapeDtypeStruct((cap, width), BF16)] * 3,
        compiler_params=PARAMS,
        name="place",
    )(place, *owns, *others)

    delta = functools.reduce(jnp.add, deltas).reshape(groups, 1, cap)
    to_pair = jnp.broadcast_to(delta, (groups, 2, cap)).reshape(seq_size, cap)
    delta = jnp.sum(lax.all_to_all(to_pair, "seq", 0, 0), axis=0)
    slot = jnp.arange(cap)
    is_valid = slot < own_count
    start = jnp.where(parity == 0, 0, first)
    padded = jnp.concatenate([delta, jnp.zeros_like(delta)])
    own_delta = lax.dynamic_slice_in_dim(padded, start, cap, 0)
    router_term = jnp.where(is_valid, (1.0 - gate) * own_delta, 0.0)
    partial_value = jnp.dot(router_term, input_own.astype(F32), precision=lax.Precision.HIGHEST)
    devices = seq_size * lax.axis_size("fsdp")
    shares = lax.all_to_all(partial_value.reshape(devices, -1), ("seq", "fsdp"), 0, 0)
    grad_router = jnp.sum(shares, axis=0)
    return grad_q[None], grad_k[None], grad_v[None], grad_router


def solution(mesh):
    rows = P("fsdp", "seq", None)
    placed = (rows, rows, rows, rows, rows, P("fsdp"), P("fsdp", "seq"), P("fsdp", "seq"))
    return jax.shard_map(
        per_device,
        mesh=mesh,
        in_specs=placed,
        out_specs=(rows, rows, rows, P(("seq", "fsdp"))),
        check_vma=False,
    )
```

time: 391 us -> 107 us (0.27)
  waiting for transfers between devices: 182 us -> 29.6 us
  local copies, waits for them, and re-layouts: 77.9 us -> 3.09 us
  blocking collectives: 78.3 us -> 17.6 us
  starting transfers between devices: 4.43 us -> 38.2 us
  matrix products: 17.9 us -> 0.96 us
  between operations: 14.9 us -> 1.46 us
  Pallas kernels: 0 us -> 13.2 us
  other arithmetic: 14 us -> 2.49 us
    all_gather x4 -> x0, waiting for transfers between devices: 143 us -> none  [the longest x1 47.1 us: per_device(): lax.all_gather(key_bal, 'seq', axis=0, tiled=True)]
    unnamed x1 -> x0, blocking collectives: 39.7 us -> none
    all_gather x1 -> x0, blocking collectives: 32.2 us -> none  [per_device(): lax.all_gather(jnp.stack([log_total.T, delta.T]), 'seq', axis=1, tiled=True)]
    ppermute x3 -> x17, starting transfers between devices: 4.09 us -> 34.5 us  [swapped(): lax.ppermute(array, 'seq', [(i, i ^ apart) for i in range(lax.axis_size('...]
    dot_general x8 -> x2, matrix products: 17.9 us -> 0.96 us  [the longest x1 0.58 us: per_device(): jnp.dot(router_term, input_own.astype(F32), precision=lax.Precision.HIGHEST)]
    slice x10 -> x0, local copies, waits for them, and re-layouts: 16.5 us -> none  [the longest x2 7.47 us: per_device(): value_bal = balanced[2]]
    ppermute x3 -> x17, waiting for transfers between devices: 39.5 us -> 23.3 us  [swapped(): lax.ppermute(array, 'seq', [(i, i ^ apart) for i in range(lax.axis_size('...]
    unnamed x30 -> x16, local copies, waits for them, and re-layouts: 17.3 us -> 1.17 us
  transfers between devices with their start and end apart: 7 -> 18, of which waited for: 6 -> 4; matrix products, arithmetic and copies ran while one was open for 8% -> 3% of each run, Pallas kernels for 0% -> 11%
where the time goes in v1:
time: 107 us
  starting transfers between devices  38.2 us (36%)
  waiting for transfers between devices  29.6 us (28%)
  blocking collectives  17.6 us (16%)
  Pallas kernels  13.2 us (12%)
  local copies, waits for them, and re-layouts  3.09 us (3%)
  other arithmetic  2.49 us (2%)
  between operations  1.46 us (1%)
    ppermute x17, starting transfers between devices, swapped(): lax.ppermute(array, 'seq', [(i, i ^ apart) for i in range(lax.axis_size('...  34.5 us
    ppermute x17, waiting for transfers between devices, swapped(): lax.ppermute(array, 'seq', [(i, i ^ apart) for i in range(lax.axis_size('...  23.3 us
    all_to_all x1, blocking collectives, per_device(): lax.all_to_all(partial_value.reshape(devices, -1), ('seq', 'fsdp'), 0, 0)  12.4 us
    all_to_all x1, waiting for transfers between devices, per_device(): delta = jnp.sum(lax.all_to_all(to_pair, 'seq', 0, 0), axis=0)  6.39 us
    all_gather x1, blocking collectives, per_device(): router_full = lax.all_gather(router_weight, 'fsdp', axis=0, tiled=True)  5.15 us
    pallas_call x2, Pallas kernels, per_device(): pl.pallas_call(functools.partial(attention_kernel, groups), in_specs=[SME...  4.39 us
    pallas_call x2, Pallas kernels, per_device(): pl.pallas_call(functools.partial(pack_kernel, groups, c), grid_spec=pltpu...  4.32 us
    all_to_all x1, starting transfers between devices, per_device(): delta = jnp.sum(lax.all_to_all(to_pair, 'seq', 0, 0), axis=0)  3.65 us
  transfers between devices with their start and end apart: 18, of which 4 were waited for; matrix products, arithmetic and copies ran while one was open for 3% of the time, Pallas kernels for 11%

profile of v1, /device:TPU:0, one launch (start us, length us, event | category | flops | bytes accessed | tf_op | source)
XLA Modules:
  0.0 106.6 jit_solution(14191362477540867498)
XLA Ops:
  3.1 3.0 %collective-permute-start.1 = (bf16[4,128,512]{2,1,0:T(8,128)(2,1)}, bf16[4,128,512]{2,1,0:T(8,128)(2,1)}, u32[]{:S(2)}, u32[]{:S(2)}) collective-permute-start(bf16[4,128,512]{2,1,0:T(8,128)(2,1)} %pad_maximum_fusion), channel_id=1, source_target_pairs={{0,4},{4,0},{8,12},{12,8},{16,20},{20,16},{24,28},{28,24},{1,5},{5... | collective-permute-start | bytes 1572872 | tf_op jit(solution)/shard_map/ppermute | solution.py:26
  6.9 5.2 %all_gather.3 = bf16[4096]{0:T(1024)(128)(2,1)S(1)} all-gather(bf16[1024]{0:T(1024)(128)(2,1)S(1)} %copy-done.5), channel_id=1, replica_groups=mesh['seq'=8,'fsdp'=4] {'fsdp'}, dimensions={0}, use_global_device_ids=true | all-gather | bytes 10240 | tf_op jit(solution)/shard_map/all_gather | solution.py:178
  12.9 2.1 %collective-permute-start = (f32[128,128]{1,0:T(8,128)S(1)}, f32[128,128]{1,0:T(8,128)S(1)}, u32[]{:S(2)}, u32[]{:S(2)}) collective-permute-start(f32[128,128]{1,0:T(8,128)S(1)} %broadcast_select_fusion.note_own), channel_id=1, source_target_pairs={{0,4},{4,0},{8,12},{12,8},{16,20},{20,16},{24,28},{28,24},{1,5},{5... | collective-permute-start | bytes 196616 | tf_op jit(solution)/shard_map/ppermute | solution.py:26
  15.7 15.1 %collective-permute-done.note_in = f32[128,128]{1,0:T(8,128)S(1)} collective-permute-done((f32[128,128]{1,0:T(8,128)S(1)}, f32[128,128]{1,0:T(8,128)S(1)}, u32[]{:S(2)}, u32[]{:S(2)}) %collective-permute-start) | collective-permute-done | bytes 65568 | tf_op jit(solution)/shard_map/ppermute | solution.py:26
  31.5 2.2 %pack_0.1 = (bf16[4,128,128]{2,1,0:T(8,128)(2,1)S(1)}, bf16[4,128,128]{2,1,0:T(8,128)(2,1)S(1)}, bf16[4,128,128]{2,1,0:T(8,128)(2,1)S(1)}, bf16[4,128,128]{2,1,0:T(8,128)(2,1)S(1)}, f32[3,128,128]{2,1,0:T(8,128)S(1)}) custom-call(s32[3]{0:T(128)S(1)} %pad_add_fusion.place, f32[8,128]{1,0:T(8,128)S(1)} %jit_solution_.3.freq_ref, ...), custom_call_target="tpu_custom_call" | custom-call | tf_op jit(solution)/shard_map/pack_0/pallas_call | solution.py:192
  33.8 1.9 %collective-permute-start.2 = (bf16[4,128,128]{2,1,0:T(8,128)(2,1)S(1)}, bf16[4,128,128]{2,1,0:T(8,128)(2,1)S(1)}, u32[]{:S(2)}, u32[]{:S(2)}) collective-permute-start(bf16[4,128,128]{2,1,0:T(8,128)(2,1)S(1)} %get-tuple-element.32), channel_id=1, source_target_pairs={{0,8},{4,12},{8,0},{12,4},{16,24},{20,28},{24,16},{28,20},{1,9},{5... | collective-permute-start | bytes 393224 | tf_op jit(solution)/shard_map/ppermute | solution.py:26
  35.6 2.6 %collective-permute-start.3 = (bf16[4,128,128]{2,1,0:T(8,128)(2,1)S(1)}, bf16[4,128,128]{2,1,0:T(8,128)(2,1)S(1)}, u32[]{:S(2)}, u32[]{:S(2)}) collective-permute-start(bf16[4,128,128]{2,1,0:T(8,128)(2,1)S(1)} %get-tuple-element.33), channel_id=1, source_target_pairs={{0,16},{4,20},{8,24},{12,28},{16,0},{20,4},{24,8},{28,12},{1,17},{... | collective-permute-start | bytes 393224 | tf_op jit(solution)/shard_map/ppermute | solution.py:26
  38.2 2.1 %pack_1.1 = (bf16[4,128,128]{2,1,0:T(8,128)(2,1)S(1)}, bf16[4,128,128]{2,1,0:T(8,128)(2,1)S(1)}, bf16[4,128,128]{2,1,0:T(8,128)(2,1)S(1)}, bf16[4,128,128]{2,1,0:T(8,128)(2,1)S(1)}) custom-call(s32[3]{0:T(128)S(1)} %pad_add_fusion.place, f32[8,128]{1,0:T(8,128)S(1)} %jit_solution_.3.freq_ref, f32[128,128]{1,0:T(8,128)S(1)} %broadcast_select_fusion.note_own, ...), custom_call_target="tpu_custom_call" | custom-call | tf_op jit(solution)/shard_map/pack_1/pallas_call | solution.py:192
  41.3 3.5 %collective-permute-start.10 = (bf16[4,128,128]{2,1,0:T(8,128)(2,1)S(1)}, bf16[4,128,128]{2,1,0:T(8,128)(2,1)S(1)}, u32[]{:S(2)}, u32[]{:S(2)}) collective-permute-start(bf16[4,128,128]{2,1,0:T(8,128)(2,1)S(1)} %get-tuple-element.42), channel_id=1, source_target_pairs={{0,16},{4,20},{8,24},{12,28},{16,0},{20,4},{24,8},{28,12},{1,17},{... | collective-permute-start | bytes 393224 | tf_op jit(solution)/shard_map/ppermute | solution.py:26
  44.8 3.9 %collective-permute-done.3.refs_2_ = bf16[4,128,128]{2,1,0:T(8,128)(2,1)S(1)} collective-permute-done((bf16[4,128,128]{2,1,0:T(8,128)(2,1)S(1)}, bf16[4,128,128]{2,1,0:T(8,128)(2,1)S(1)}, u32[]{:S(2)}, u32[]{:S(2)}) %collective-permute-start.3) | collective-permute-done | bytes 131104 | tf_op jit(solution)/shard_map/ppermute | solution.py:26
  48.6 2.2 %attention_0.1 = (bf16[3,128,128]{2,1,0:T(8,128)(2,1)S(1)}, bf16[3,128,128]{2,1,0:T(8,128)(2,1)S(1)}, bf16[3,128,128]{2,1,0:T(8,128)(2,1)S(1)}, bf16[3,128,128]{2,1,0:T(8,128)(2,1)S(1)}, f32[8,512]{1,0:T(8,128)S(1)}) custom-call(s32[3]{0:T(128)S(1)} %pad_add_fusion.place, bf16[4,128,128]{2,1,0:T(8,128)(2,1)S(1)} %get-tuple-element.31.refs_0_, ...), custom_call_target="tpu_custom_call" | custom-call | tf_op jit(solution)/shard_map/attention_0/pallas_call | solution.py:208
  50.8 10.4 %collective-permute-start.5 = (bf16[3,128,128]{2,1,0:T(8,128)(2,1)S(1)}, bf16[3,128,128]{2,1,0:T(8,128)(2,1)S(1)}, u32[]{:S(2)}, u32[]{:S(2)}) collective-permute-start(bf16[3,128,128]{2,1,0:T(8,128)(2,1)S(1)} %get-tuple-element.36), channel_id=1, source_target_pairs={{0,8},{4,12},{8,0},{12,4},{16,24},{20,28},{24,16},{28,20},{1,9},{5... | collective-permute-start | bytes 294920 | tf_op jit(solution)/shard_map/ppermute | solution.py:26
  62.4 1.4 %collective-permute-start.7 = (bf16[3,128,128]{2,1,0:T(8,128)(2,1)S(1)}, bf16[3,128,128]{2,1,0:T(8,128)(2,1)S(1)}, u32[]{:S(2)}, u32[]{:S(2)}) collective-permute-start(bf16[3,128,128]{2,1,0:T(8,128)(2,1)S(1)} %get-tuple-element.38), channel_id=1, source_target_pairs={{0,24},{4,28},{8,16},{12,20},{16,8},{20,12},{24,0},{28,4},{1,25},{... | collective-permute-start | bytes 294920 | tf_op jit(solution)/shard_map/ppermute | solution.py:26
  63.8 2.2 %attention_1.1 = (bf16[3,128,128]{2,1,0:T(8,128)(2,1)S(1)}, bf16[3,128,128]{2,1,0:T(8,128)(2,1)S(1)}, bf16[3,128,128]{2,1,0:T(8,128)(2,1)S(1)}, bf16[3,128,128]{2,1,0:T(8,128)(2,1)S(1)}, f32[8,512]{1,0:T(8,128)S(1)}) custom-call(s32[3]{0:T(128)S(1)} %pad_add_fusion.place, bf16[4,128,128]{2,1,0:T(8,128)(2,1)S(1)} %get-tuple-element.40.refs_0_, ...), custom_call_target="tpu_custom_call" | custom-call | tf_op jit(solution)/shard_map/attention_1/pallas_call | solution.py:208
  67.0 2.1 %collective-permute-start.13 = (bf16[3,128,128]{2,1,0:T(8,128)(2,1)S(1)}, bf16[3,128,128]{2,1,0:T(8,128)(2,1)S(1)}, u32[]{:S(2)}, u32[]{:S(2)}) collective-permute-start(bf16[3,128,128]{2,1,0:T(8,128)(2,1)S(1)} %get-tuple-element.46), channel_id=1, source_target_pairs={{0,16},{4,20},{8,24},{12,28},{16,0},{20,4},{24,8},{28,12},{1,17},{... | collective-permute-start | bytes 294920 | tf_op jit(solution)/shard_map/ppermute | solution.py:26
  69.1 1.4 %collective-permute-start.14 = (bf16[3,128,128]{2,1,0:T(8,128)(2,1)S(1)}, bf16[3,128,128]{2,1,0:T(8,128)(2,1)S(1)}, u32[]{:S(2)}, u32[]{:S(2)}) collective-permute-start(bf16[3,128,128]{2,1,0:T(8,128)(2,1)S(1)} %get-tuple-element.47), channel_id=1, source_target_pairs={{0,24},{4,28},{8,16},{12,20},{16,8},{20,12},{24,0},{28,4},{1,25},{... | collective-permute-start | bytes 294920 | tf_op jit(solution)/shard_map/ppermute | solution.py:26
  71.5 1.6 %collective-permute-start.15 = (bf16[3,128,512]{2,1,0:T(8,128)(2,1)S(1)}, bf16[3,128,512]{2,1,0:T(8,128)(2,1)S(1)}, u32[]{:S(2)}, u32[]{:S(2)}) collective-permute-start(bf16[3,128,512]{2,1,0:T(8,128)(2,1)S(1)} %get-tuple-element.49), channel_id=1, source_target_pairs={{0,4},{4,0},{8,12},{12,8},{16,20},{20,16},{24,28},{28,24},{1,5},{5... | collective-permute-start | bytes 1179656 | tf_op jit(solution)/shard_map/ppermute | solution.py:26
  73.1 4.2 %collective-permute-done.13.refs_2_ = bf16[3,128,128]{2,1,0:T(8,128)(2,1)S(1)} collective-permute-done((bf16[3,128,128]{2,1,0:T(8,128)(2,1)S(1)}, bf16[3,128,128]{2,1,0:T(8,128)(2,1)S(1)}, u32[]{:S(2)}, u32[]{:S(2)}) %collective-permute-start.13) | collective-permute-done | bytes 98336 | tf_op jit(solution)/shard_map/ppermute | solution.py:26
  77.3 1.7 %unpack_1.1 = (bf16[3,128,512]{2,1,0:T(8,128)(2,1)S(1)}, bf16[3,128,512]{2,1,0:T(8,128)(2,1)}) custom-call(s32[3]{0:T(128)S(1)} %pad_add_fusion.place, f32[3,128,128]{2,1,0:T(8,128)S(1)} %get-tuple-element.30.table_ref.refs_5_, bf16[3,128,128]{2,1,0:T(8,128)(2,1)S(1)} %get-tuple-element.44.refs_0_, bf16[3,128,128]{2,1,0:T(8,128)(2,1)S(1)} %collective-permute-done.12.refs_1_, ...), custom_call_target="tpu_custom_call" | custom-call | tf_op jit(solution)/shard_map/unpack_1/pallas_call | solution.py:229
  79.0 1.5 %collective-permute-start.16 = (bf16[3,128,512]{2,1,0:T(8,128)(2,1)}, bf16[3,128,512]{2,1,0:T(8,128)(2,1)S(1)}, u32[]{:S(2)}, u32[]{:S(2)}) collective-permute-start(bf16[3,128,512]{2,1,0:T(8,128)(2,1)} %get-tuple-element.50), channel_id=1, source_target_pairs={{0,4},{4,0},{8,12},{12,8},{16,20},{20,16},{24,28},{28,24},{1,5},{5... | collective-permute-start | bytes 1179656 | tf_op jit(solution)/shard_map/ppermute | solution.py:26
  81.1 3.6 %all-to-all-start = ((f32[8,1,128]{2,1,0:T(1,128)}), f32[8,1,128]{2,1,0:T(1,128)S(1)}, u32[]{:S(2)}, u32[]{:S(2)}) async-start(f32[8,1,128]{2,1,0:T(1,128)} %bitcast.15), calls=%async_computation | async-start | bytes 8192 | tf_op jit(solution)/shard_map/all_to_all | solution.py:250
  84.8 6.4 %all-to-all-done = f32[8,1,128]{2,1,0:T(1,128)S(1)} async-done(((f32[8,1,128]{2,1,0:T(1,128)}), f32[8,1,128]{2,1,0:T(1,128)S(1)}, u32[]{:S(2)}, u32[]{:S(2)}) %all-to-all-start) | async-done | bytes 4128 | tf_op jit(solution)/shard_map/all_to_all | solution.py:250
  91.8 12.4 %all_to_all.18 = f32[32,1,128]{2,1,0:T(1,128)S(1)} all-to-all(f32[32,1,128]{2,1,0:T(1,128)S(1)} %convolution_bitcast_fusion), channel_id=1, replica_groups=mesh['seq'=8,'fsdp'=4] {'seq','fsdp'}, dimensions={0} | all-to-all | bytes 32768 | tf_op jit(solution)/shard_map/all_to_all | solution.py:259
  104.8 1.8 %place.1 = (bf16[128,2048]{1,0:T(8,128)(2,1)}, bf16[128,2048]{1,0:T(8,128)(2,1)}, bf16[128,2048]{1,0:T(8,128)(2,1)}) custom-call(s32[3]{0:T(128)S(1)} %pad_add_fusion.place, bf16[3,128,512]{2,1,0:T(8,128)(2,1)S(1)} %get-tuple-element.39.refs_0_, bf16[3,128,512]{2,1,0:T(8,128)(2,1)S(1)} %get-tuple-element.48.refs_1_, ...), custom_call_target="tpu_custom_call" | custom-call | tf_op jit(solution)/shard_map/place/pallas_call | solution.py:239
  (53 shorter events, 10.7 us)
Async XLA Ops:
  0.6 11.5 %copy-start = (bf16[1,128,4096]{2,1,0:T(8,128)(2,1)S(1)}, bf16[1,128,4096]{2,1,0:T(8,128)(2,1)}, u32[]{:S(2)}) copy-start(bf16[1,128,4096]{2,1,0:T(8,128)(2,1)} %param.13) | copy-start | bytes 3145732
  0.7 1.4 %copy-start.3 = (bf16[1,128,2048]{2,1,0:T(8,128)(2,1)S(1)}, bf16[1,128,2048]{2,1,0:T(8,128)(2,1)}, u32[]{:S(2)}) copy-start(bf16[1,128,2048]{2,1,0:T(8,128)(2,1)} %param.11) | copy-start | bytes 1572868
  0.7 1.5 %copy-start.4 = (bf16[1,128,2048]{2,1,0:T(8,128)(2,1)S(1)}, bf16[1,128,2048]{2,1,0:T(8,128)(2,1)}, u32[]{:S(2)}) copy-start(bf16[1,128,2048]{2,1,0:T(8,128)(2,1)} %param.12) | copy-start | bytes 1572868
  3.1 27.7 %collective-permute-start.1 = (bf16[4,128,512]{2,1,0:T(8,128)(2,1)}, bf16[4,128,512]{2,1,0:T(8,128)(2,1)}, u32[]{:S(2)}, u32[]{:S(2)}) collective-permute-start(bf16[4,128,512]{2,1,0:T(8,128)(2,1)} %pad_maximum_fusion), channel_id=1, source_target_pairs={{0,4},{4,0},{8,12},{12,8},{16,20},{20,16},{24,28},{28,24},{1,5},{5... | collective-permute-start | bytes 1572872 | tf_op jit(solution)/shard_map/ppermute | solution.py:26
  6.1 0.9 copy-start.5
  6.9 31.3 %collective-permute-start.8 = (bf16[4,128,512]{2,1,0:T(8,128)(2,1)}, bf16[4,128,512]{2,1,0:T(8,128)(2,1)}, u32[]{:S(2)}, u32[]{:S(2)}) collective-permute-start(bf16[4,128,512]{2,1,0:T(8,128)(2,1)} %pad_maximum_fusion.1), channel_id=1, source_target_pairs={{0,4},{4,0},{8,12},{12,8},{16,20},{20,16},{24,28},{28,24},{1,5},{5... | collective-permute-start | bytes 1572872 | tf_op jit(solution)/shard_map/ppermute | solution.py:26
  12.1 19.4 %copy-start.1 = (bf16[1,128,2048]{2,1,0:T(8,128)(2,1)S(1)}, bf16[1,128,2048]{2,1,0:T(8,128)(2,1)}, u32[]{:S(2)}) copy-start(bf16[1,128,2048]{2,1,0:T(8,128)(2,1)} %param.9) | copy-start | bytes 1572868
  12.1 19.4 %copy-start.2 = (bf16[1,128,2048]{2,1,0:T(8,128)(2,1)S(1)}, bf16[1,128,2048]{2,1,0:T(8,128)(2,1)}, u32[]{:S(2)}) copy-start(bf16[1,128,2048]{2,1,0:T(8,128)(2,1)} %param.10) | copy-start | bytes 1572868
  12.9 18.0 %collective-permute-start = (f32[128,128]{1,0:T(8,128)S(1)}, f32[128,128]{1,0:T(8,128)S(1)}, u32[]{:S(2)}, u32[]{:S(2)}) collective-permute-start(f32[128,128]{1,0:T(8,128)S(1)} %broadcast_select_fusion.note_own), channel_id=1, source_target_pairs={{0,4},{4,0},{8,12},{12,8},{16,20},{20,16},{24,28},{28,24},{1,5},{5... | collective-permute-start | bytes 196616 | tf_op jit(solution)/shard_map/ppermute | solution.py:26
  33.8 11.0 %collective-permute-start.2 = (bf16[4,128,128]{2,1,0:T(8,128)(2,1)S(1)}, bf16[4,128,128]{2,1,0:T(8,128)(2,1)S(1)}, u32[]{:S(2)}, u32[]{:S(2)}) collective-permute-start(bf16[4,128,128]{2,1,0:T(8,128)(2,1)S(1)} %get-tuple-element.32), channel_id=1, source_target_pairs={{0,8},{4,12},{8,0},{12,4},{16,24},{20,28},{24,16},{28,20},{1,9},{5... | collective-permute-start | bytes 393224 | tf_op jit(solution)/shard_map/ppermute | solution.py:26
  35.6 13.0 %collective-permute-start.3 = (bf16[4,128,128]{2,1,0:T(8,128)(2,1)S(1)}, bf16[4,128,128]{2,1,0:T(8,128)(2,1)S(1)}, u32[]{:S(2)}, u32[]{:S(2)}) collective-permute-start(bf16[4,128,128]{2,1,0:T(8,128)(2,1)S(1)} %get-tuple-element.33), channel_id=1, source_target_pairs={{0,16},{4,20},{8,24},{12,28},{16,0},{20,4},{24,8},{28,12},{1,17},{... | collective-permute-start | bytes 393224 | tf_op jit(solution)/shard_map/ppermute | solution.py:26
  38.2 10.4 %collective-permute-start.4 = (bf16[4,128,128]{2,1,0:T(8,128)(2,1)S(1)}, bf16[4,128,128]{2,1,0:T(8,128)(2,1)S(1)}, u32[]{:S(2)}, u32[]{:S(2)}) collective-permute-start(bf16[4,128,128]{2,1,0:T(8,128)(2,1)S(1)} %get-tuple-element.34), channel_id=1, source_target_pairs={{0,24},{4,28},{8,16},{12,20},{16,8},{20,12},{24,0},{28,4},{1,25},{... | collective-permute-start | bytes 393224 | tf_op jit(solution)/shard_map/ppermute | solution.py:26
  40.3 22.1 %collective-permute-start.9 = (bf16[4,128,128]{2,1,0:T(8,128)(2,1)S(1)}, bf16[4,128,128]{2,1,0:T(8,128)(2,1)S(1)}, u32[]{:S(2)}, u32[]{:S(2)}) collective-permute-start(bf16[4,128,128]{2,1,0:T(8,128)(2,1)S(1)} %get-tuple-element.41), channel_id=1, source_target_pairs={{0,8},{4,12},{8,0},{12,4},{16,24},{20,28},{24,16},{28,20},{1,9},{5... | collective-permute-start | bytes 393224 | tf_op jit(solution)/shard_map/ppermute | solution.py:26
  41.3 22.6 %collective-permute-start.10 = (bf16[4,128,128]{2,1,0:T(8,128)(2,1)S(1)}, bf16[4,128,128]{2,1,0:T(8,128)(2,1)S(1)}, u32[]{:S(2)}, u32[]{:S(2)}) collective-permute-start(bf16[4,128,128]{2,1,0:T(8,128)(2,1)S(1)} %get-tuple-element.42), channel_id=1, source_target_pairs={{0,16},{4,20},{8,24},{12,28},{16,0},{20,4},{24,8},{28,12},{1,17},{... | collective-permute-start | bytes 393224 | tf_op jit(solution)/shard_map/ppermute | solution.py:26
  44.8 19.1 %collective-permute-start.11 = (bf16[4,128,128]{2,1,0:T(8,128)(2,1)S(1)}, bf16[4,128,128]{2,1,0:T(8,128)(2,1)S(1)}, u32[]{:S(2)}, u32[]{:S(2)}) collective-permute-start(bf16[4,128,128]{2,1,0:T(8,128)(2,1)S(1)} %get-tuple-element.43), channel_id=1, source_target_pairs={{0,24},{4,28},{8,16},{12,20},{16,8},{20,12},{24,0},{28,4},{1,25},{... | collective-permute-start | bytes 393224 | tf_op jit(solution)/shard_map/ppermute | solution.py:26
  50.8 18.3 %collective-permute-start.5 = (bf16[3,128,128]{2,1,0:T(8,128)(2,1)S(1)}, bf16[3,128,128]{2,1,0:T(8,128)(2,1)S(1)}, u32[]{:S(2)}, u32[]{:S(2)}) collective-permute-start(bf16[3,128,128]{2,1,0:T(8,128)(2,1)S(1)} %get-tuple-element.36), channel_id=1, source_target_pairs={{0,8},{4,12},{8,0},{12,4},{16,24},{20,28},{24,16},{28,20},{1,9},{5... | collective-permute-start | bytes 294920 | tf_op jit(solution)/shard_map/ppermute | solution.py:26
  61.2 9.3 %collective-permute-start.6 = (bf16[3,128,128]{2,1,0:T(8,128)(2,1)S(1)}, bf16[3,128,128]{2,1,0:T(8,128)(2,1)S(1)}, u32[]{:S(2)}, u32[]{:S(2)}) collective-permute-start(bf16[3,128,128]{2,1,0:T(8,128)(2,1)S(1)} %get-tuple-element.37), channel_id=1, source_target_pairs={{0,16},{4,20},{8,24},{12,28},{16,0},{20,4},{24,8},{28,12},{1,17},{... | collective-permute-start | bytes 294920 | tf_op jit(solution)/shard_map/ppermute | solution.py:26
  62.4 8.1 %collective-permute-start.7 = (bf16[3,128,128]{2,1,0:T(8,128)(2,1)S(1)}, bf16[3,128,128]{2,1,0:T(8,128)(2,1)S(1)}, u32[]{:S(2)}, u32[]{:S(2)}) collective-permute-start(bf16[3,128,128]{2,1,0:T(8,128)(2,1)S(1)} %get-tuple-element.38), channel_id=1, source_target_pairs={{0,24},{4,28},{8,16},{12,20},{16,8},{20,12},{24,0},{28,4},{1,25},{... | collective-permute-start | bytes 294920 | tf_op jit(solution)/shard_map/ppermute | solution.py:26
  66.0 7.0 %collective-permute-start.12 = (bf16[3,128,128]{2,1,0:T(8,128)(2,1)S(1)}, bf16[3,128,128]{2,1,0:T(8,128)(2,1)S(1)}, u32[]{:S(2)}, u32[]{:S(2)}) collective-permute-start(bf16[3,128,128]{2,1,0:T(8,128)(2,1)S(1)} %get-tuple-element.45), channel_id=1, source_target_pairs={{0,8},{4,12},{8,0},{12,4},{16,24},{20,28},{24,16},{28,20},{1,9},{5... | collective-permute-start | bytes 294920 | tf_op jit(solution)/shard_map/ppermute | solution.py:26
  67.0 10.3 %collective-permute-start.13 = (bf16[3,128,128]{2,1,0:T(8,128)(2,1)S(1)}, bf16[3,128,128]{2,1,0:T(8,128)(2,1)S(1)}, u32[]{:S(2)}, u32[]{:S(2)}) collective-permute-start(bf16[3,128,128]{2,1,0:T(8,128)(2,1)S(1)} %get-tuple-element.46), channel_id=1, source_target_pairs={{0,16},{4,20},{8,24},{12,28},{16,0},{20,4},{24,8},{28,12},{1,17},{... | collective-permute-start | bytes 294920 | tf_op jit(solution)/shard_map/ppermute | solution.py:26
  69.1 8.2 %collective-permute-start.14 = (bf16[3,128,128]{2,1,0:T(8,128)(2,1)S(1)}, bf16[3,128,128]{2,1,0:T(8,128)(2,1)S(1)}, u32[]{:S(2)}, u32[]{:S(2)}) collective-permute-start(bf16[3,128,128]{2,1,0:T(8,128)(2,1)S(1)} %get-tuple-element.47), channel_id=1, source_target_pairs={{0,24},{4,28},{8,16},{12,20},{16,8},{20,12},{24,0},{28,4},{1,25},{... | collective-permute-start | bytes 294920 | tf_op jit(solution)/shard_map/ppermute | solution.py:26
  71.5 33.3 %collective-permute-start.15 = (bf16[3,128,512]{2,1,0:T(8,128)(2,1)S(1)}, bf16[3,128,512]{2,1,0:T(8,128)(2,1)S(1)}, u32[]{:S(2)}, u32[]{:S(2)}) collective-permute-start(bf16[3,128,512]{2,1,0:T(8,128)(2,1)S(1)} %get-tuple-element.49), channel_id=1, source_target_pairs={{0,4},{4,0},{8,12},{12,8},{16,20},{20,16},{24,28},{28,24},{1,5},{5... | collective-permute-start | bytes 1179656 | tf_op jit(solution)/shard_map/ppermute | solution.py:26
  79.0 25.7 %collective-permute-start.16 = (bf16[3,128,512]{2,1,0:T(8,128)(2,1)}, bf16[3,128,512]{2,1,0:T(8,128)(2,1)S(1)}, u32[]{:S(2)}, u32[]{:S(2)}) collective-permute-start(bf16[3,128,512]{2,1,0:T(8,128)(2,1)} %get-tuple-element.50), channel_id=1, source_target_pairs={{0,4},{4,0},{8,12},{12,8},{16,20},{20,16},{24,28},{28,24},{1,5},{5... | collective-permute-start | bytes 1179656 | tf_op jit(solution)/shard_map/ppermute | solution.py:26
  81.1 10.0 %all-to-all-start = ((f32[8,1,128]{2,1,0:T(1,128)}), f32[8,1,128]{2,1,0:T(1,128)S(1)}, u32[]{:S(2)}, u32[]{:S(2)}) async-start(f32[8,1,128]{2,1,0:T(1,128)} %bitcast.15), calls=%async_computation | async-start | bytes 8192 | tf_op jit(solution)/shard_map/all_to_all | solution.py:250
  (2 other events, 1.3 us)

commit v2 on v1

v2 whole, which is shorter than its diff:
```python
import functools
import math

import jax
import jax.numpy as jnp
from jax import lax
from jax.experimental import pallas as pl
from jax.experimental.pallas import tpu as pltpu
from jax.sharding import PartitionSpec as P

HEADS = 16
HEAD_DIM = 128
HALF_DIM = HEAD_DIM // 2
TOK_DEV = 512
THETA = 500000.0
NEG = -1e30
SCALE = HEAD_DIM ** -0.5
BF16 = jnp.bfloat16
F32 = jnp.float32
PARAMS = pltpu.CompilerParams(vmem_limit_bytes=40 * 1024 * 1024)
FRONT = 63
SMALL = pl.CostEstimate(flops=1 << 20, bytes_accessed=1 << 16, transcendentals=0)
LARGE = pl.CostEstimate(flops=1 << 28, bytes_accessed=1 << 16, transcendentals=0)
VMEM = pl.BlockSpec(memory_space=pltpu.VMEM)
ANY = pl.BlockSpec(memory_space=pl.ANY)
SMEM = pl.BlockSpec(memory_space=pltpu.SMEM)


def swapped(array):
    return lax.ppermute(array, "seq", [(i, i ^ 1) for i in range(lax.axis_size("seq"))])


def spread(pieces):
    size = lax.axis_size("seq")
    arrived = [
        lax.ppermute(pieces[m], "seq", [(i, i ^ (2 * m)) for i in range(size)]) for m in range(len(pieces) - 1, 0, -1)
    ]
    return arrived + [pieces[0]]


def after(value, *done):
    return lax.optimization_barrier((value, *done))[0]


def call(kernel, name, shapes, *operands, scratch_shapes=(), cost_estimate=SMALL):
    return pl.pallas_call(
        kernel,
        in_specs=[SMEM if a.shape == (1, 1) else VMEM for a in operands],
        out_specs=[VMEM] * len(shapes),
        out_shape=[jax.ShapeDtypeStruct(shape, dtype) for shape, dtype in shapes],
        scratch_shapes=scratch_shapes,
        compiler_params=PARAMS,
        cost_estimate=cost_estimate,
        name=name,
    )(*operands)


def dot(a, b, contract):
    return lax.dot_general(a, b, ((contract[0], contract[1]), ((), ())), preferred_element_type=F32)


def lanes(index, width=HEAD_DIM):
    if isinstance(index, int):
        return slice(index * width, (index + 1) * width)
    return pl.ds(pl.multiple_of(index * width, HEAD_DIM), width)


def grid_of(cap):
    row = lax.broadcasted_iota(jnp.int32, (cap, cap), 0)
    column = lax.broadcasted_iota(jnp.int32, (cap, cap), 1)
    return row, column


def own_place(counts):
    index = lax.axis_index("seq")
    return index & 1, index >> 1, counts[0, 0]


def places(counts, cap):
    parity, _, count = own_place(counts)
    first = jnp.where(parity == 0, count, cap - count)
    row, slot = grid_of(cap)
    even = jnp.where((row == slot) & (row < first), 1.0, 0.0)
    odd = jnp.where((row == slot + first) & (row >= first), 1.0, 0.0)
    is_even = parity == 0
    return jnp.where(is_even, even, odd).astype(BF16), jnp.where(is_even, odd, even).astype(BF16)


def rotated(rows, table_ref, direction):
    rows = rows.astype(F32)
    turned = pltpu.roll(rows, HALF_DIM, 1) * table_ref[1]
    rows = rows * table_ref[0]
    return (rows + turned if direction > 0 else rows - turned).astype(BF16)


def put(hot, rows):
    return dot(hot, rows, ((1,), (0,))).astype(BF16)


def taken(hot, rows):
    return dot(hot, rows, ((0,), (0,))).astype(BF16)


def front_kernel(groups, counts, pos_ref, v_ref, k_ref, q_ref, *refs):
    outs, (out_ref, table_ref, v_buffer, kq_buffer, sems) = refs[:groups], refs[groups:]
    cap, half = out_ref.shape[1:]
    wide = outs[0].shape[2]
    heads = half // HEAD_DIM
    parity, group, _ = own_place(counts)
    copies = [pltpu.make_async_copy(v_ref, v_buffer, sems.at[0])]
    for t, ref in enumerate((k_ref, q_ref)):
        copies.append(pltpu.make_async_copy(ref.at[:, lanes(1 - parity, half)], kq_buffer.at[t], sems.at[1 + t]))
    for copy in copies:
        copy.start()
    own_hot, _ = places(counts, cap)
    row, column = grid_of(cap)
    position = (lax.axis_index("seq") * TOK_DEV + pos_ref[0:1, :]).astype(F32)
    position = jnp.sum(jnp.where(row == column, position, 0.0), axis=1, keepdims=True)
    lane = lax.broadcasted_iota(jnp.int32, (cap, HEAD_DIM), 1)
    feature = jnp.where(lane < HALF_DIM, lane, lane - HALF_DIM).astype(F32)
    angle = position * jnp.exp(feature * (-2.0 / HEAD_DIM * math.log(THETA)))
    table_ref[0] = jnp.cos(angle)
    table_ref[1] = jnp.where(lane < HALF_DIM, -1.0, 1.0) * jnp.sin(angle)
    copies[0].wait()
    for m in range(groups):
        for side in range(2):
            block = (parity ^ side) * groups + (group ^ m)
            outs[m][side] = put(own_hot, v_buffer[:, lanes(block, wide)])
    for t in range(2):
        copies[1 + t].wait()
        for h in range(heads):
            out_ref[t, :, lanes(h)] = put(own_hot, rotated(kq_buffer[t, :, lanes(h)], table_ref, 1))


def gate_kernel(counts, weight_ref, input_ref, g_ref, out_ref, gate_ref):
    cap, half = out_ref.shape
    parity = own_place(counts)[0]
    own_hot, _ = places(counts, cap)
    total = jnp.zeros((cap, HEAD_DIM), F32)
    for b in range(input_ref.shape[1] // HEAD_DIM):
        total += input_ref[:, lanes(b)].astype(F32) * weight_ref[0:1, lanes(b)].astype(F32)
    logit = jnp.sum(total, axis=1, keepdims=True)
    gate = jnp.broadcast_to(1.0 / (1.0 + jnp.exp(-logit)), (cap, HEAD_DIM))
    gate_ref[...] = gate
    heads = half // HEAD_DIM
    for h in range(heads):
        rows = g_ref[:, lanes((1 - parity) * heads + h)].astype(F32) * gate
        out_ref[:, lanes(h)] = put(own_hot, rows.astype(BF16))


def pack_kernel(groups, counts, table_ref, k_ref, q_ref, in_ref, *outs):
    cap, half = in_ref.shape[1:]
    parity, group, _ = own_place(counts)
    own_hot, _ = places(counts, cap)
    heads = half // groups // HEAD_DIM
    for m in range(groups):
        for t, ref in enumerate((k_ref, q_ref)):
            for c in range(heads):
                h = (group ^ m) * heads + c
                rows = rotated(ref[:, lanes(parity * groups * heads + h)], table_ref, 1)
                outs[m][t, :, lanes(c)] = put(own_hot, rows) + in_ref[t, :, lanes(h)]


def pack_gated_kernel(groups, counts, gate_ref, g_ref, in_ref, v_own_ref, v_in_ref, *refs):
    outs, v_ref = refs[:groups], refs[groups]
    cap, half = in_ref.shape
    parity, group, _ = own_place(counts)
    own_hot, _ = places(counts, cap)
    heads = half // groups // HEAD_DIM
    for m in range(groups):
        for c in range(heads):
            h = (group ^ m) * heads + c
            rows = g_ref[:, lanes(parity * groups * heads + h)].astype(F32) * gate_ref[...]
            outs[m][:, lanes(c)] = put(own_hot, rows.astype(BF16)) + in_ref[:, lanes(h)]
    v_ref[...] = v_own_ref[...] + v_in_ref[...]


def block_of(m, cap):
    return pl.ds(pl.multiple_of(((lax.axis_index("seq") >> 1) ^ m) * cap, cap), cap)


def gather_values_kernel(groups, counts, *refs):
    own_ref, send_ref = refs[groups:]
    cap = refs[0].shape[1]
    for i in range(groups):
        block = block_of(groups - 1 - i, cap)
        own_ref[block, :] = refs[i][0]
        send_ref[block, :] = refs[i][1]


def gather_kernel(groups, counts, *refs):
    cap = refs[0].shape[1]
    for i in range(groups):
        refs[groups][:, block_of(groups - 1 - i, cap), :] = refs[i][...]


def probabilities_kernel(groups, counts, kq_ref, v_ref, *refs):
    g_refs, (ds_ref, dv_ref, delta_ref, g_ref, sum_ref) = refs[:groups], refs[groups:]
    cap, wide = g_refs[0].shape
    for i in range(groups):
        g_ref[block_of(groups - 1 - i, cap), :] = g_refs[i][...]
    key, query = grid_of(cap)
    kept = query >= key
    for c in range(wide // HEAD_DIM):
        sum_ref[...] = jnp.zeros_like(sum_ref)
        for i in range(groups):
            upto = (i + 1) * cap
            here = slice(i * cap, upto)
            g = g_ref[here, lanes(c)]
            s = dot(kq_ref[0, :upto, lanes(c)], kq_ref[1, here, lanes(c)], ((1,), (1,))) * SCALE
            last = jnp.where(kept, s[i * cap:], NEG)
            s = last if i == 0 else jnp.concatenate([s[:i * cap], last], axis=0)
            e = jnp.exp(s - jnp.max(s, axis=0, keepdims=True))
            p = e * (1.0 / jnp.sum(e, axis=0, keepdims=True))
            dp = dot(v_ref[:upto, lanes(c)], g, ((1,), (1,)))
            delta = jnp.sum(p * dp, axis=0, keepdims=True)
            whole = jnp.broadcast_to(delta, (8, cap))
            delta_ref[i] = whole if c == 0 else delta_ref[i] + whole
            p16 = p.astype(BF16)
            ds_ref[c, i, :upto, :] = (p16.astype(F32) * (dp - delta) * SCALE).astype(BF16)
            sum_ref[:upto, :] += dot(p16, g, ((1,), (0,)))
        dv_ref[:, lanes(c)] = sum_ref[...].astype(BF16)


def gradients_kernel(groups, counts, kq_ref, ds_ref, delta_ref, *refs):
    outs, (dq_ref, dk_ref) = refs[:groups], refs[groups:]
    heads, _, total, cap = ds_ref.shape
    for c in range(heads):
        dk_ref[...] = jnp.zeros_like(dk_ref)
        for i in range(groups):
            upto = (i + 1) * cap
            here = slice(i * cap, upto)
            ds = ds_ref[c, i, :upto, :]
            dk_ref[:upto, :] += dot(ds, kq_ref[1, here, lanes(c)], ((1,), (0,)))
            dq_ref[here, :] = dot(ds, kq_ref[0, :upto, lanes(c)], ((0,), (0,)))
        for m in range(groups):
            block = block_of(m, cap)
            outs[m][0:cap, lanes(c)] = dq_ref[block, :].astype(BF16)
            outs[m][cap:2 * cap, lanes(c)] = dk_ref[block, :].astype(BF16)
    line = lax.broadcasted_iota(jnp.int32, (8, cap), 0)
    for m in range(groups):
        delta = delta_ref[own_place(counts)[1] ^ m]
        coarse = delta.astype(BF16).astype(F32)
        rows = jnp.where(line == 0, coarse, jnp.where(line == 1, delta - coarse, 0.0))
        rows = jnp.concatenate([rows, jnp.zeros_like(rows)], axis=0).astype(BF16)
        for c in range(heads):
            outs[m][2 * cap:, lanes(c)] = rows


def delta_kernel(groups, *refs):
    ins, out_ref = refs[:groups], refs[groups]
    rows = ins[0].shape[0]
    total = ins[0][rows - 16:, 0:HEAD_DIM].astype(F32)
    for ref in ins[1:]:
        total += ref[rows - 16:, 0:HEAD_DIM].astype(F32)
    out_ref[...] = jnp.broadcast_to(total[0:1, :] + total[1:2, :], out_ref.shape)


def unpack_kernel(groups, counts, table_ref, dv_ref, dv_in_ref, *refs):
    ins, own_ref, send_ref, outs = refs[:groups], refs[groups], refs[groups + 1], refs[groups + 2:]
    cap = own_ref.shape[1]
    for m in range(groups):
        block = block_of(m, cap)
        outs[m][0] = dv_ref[block, :]
        outs[m][1] = dv_in_ref[block, :]
    wide = ins[0].shape[1]
    heads = wide // HEAD_DIM
    own_hot, in_hot = places(counts, cap)
    for i in range(groups):
        group = own_place(counts)[1] ^ (groups - 1 - i)
        for t in range(2):
            send_ref[t, :, lanes(group, wide)] = taken(in_hot, ins[i][t * cap:(t + 1) * cap, :])
            for c in range(heads):
                own = dot(own_hot, ins[i][t * cap:(t + 1) * cap, lanes(c)], ((0,), (0,)))
                own_ref[t, :, lanes(group * heads + c)] = rotated(own, table_ref, -1)


def router_kernel(counts, delta_ref, delta_in_ref, gate_ref, input_ref, out_ref):
    cap = input_ref.shape[0]
    parity, _, count = own_place(counts)
    row, column = grid_of(cap)
    start = jnp.where(parity == 0, 0, cap - count)
    delta = delta_ref[0:1, :] + delta_in_ref[0:1, :]
    own = jnp.where((column == row + start) & (row < count), delta, 0.0)
    term = (1.0 - gate_ref[...]) * jnp.sum(own, axis=1, keepdims=True)
    for b in range(out_ref.shape[0]):
        out_ref[b:b + 1, :] = jnp.sum(input_ref[:, lanes(b)].astype(F32) * term, axis=0, keepdims=True)


def place_kernel(groups, counts, table_ref, own_ref, in_ref, *refs):
    ins, outs, (buffer, sems) = refs[:groups], refs[groups:groups + 3], refs[groups + 3:]
    cap, wide = ins[0].shape[1:]
    half = own_ref.shape[2]
    heads = half // HEAD_DIM
    parity, group, _ = own_place(counts)
    own_hot, _ = places(counts, cap)
    copies = [
        pltpu.make_async_copy(own_ref.at[t], outs[t].at[:, lanes(parity, half)], sems.at[t]) for t in range(2)
    ]
    for copy in copies:
        copy.start()
    for t in range(2):
        for h in range(heads):
            buffer[t, :, lanes(h)] = rotated(in_ref[t, :, lanes(h)], table_ref, -1)
        copies.append(pltpu.make_async_copy(buffer.at[t], outs[t].at[:, lanes(1 - parity, half)], sems.at[2 + t]))
        copies[-1].start()
    for side in range(2):
        for i in range(groups):
            buffer[2 + side, :, lanes(group ^ (groups - 1 - i), wide)] = taken(own_hot, ins[i][side])
        copies.append(pltpu.make_async_copy(buffer.at[2 + side], outs[2].at[:, lanes(parity ^ side, half)], sems.at[4 + side]))
        copies[-1].start()
    for copy in copies:
        copy.wait()


def per_device(queries, key_rows, value_rows, out_grad, inputs, router_weight, counts, picked_pos):
    query_own, key_own, value_own, grad_own, input_own = queries[0], key_rows[0], value_rows[0], out_grad[0], inputs[0]
    cap, width = query_own.shape
    half = width // 2
    seq_size = lax.axis_size("seq")
    groups = seq_size // 2
    wide = half // groups
    total = groups * cap
    heads = wide // HEAD_DIM

    def kernel(body):
        return functools.partial(body, groups)

    *values, sent, table = pl.pallas_call(
        kernel(front_kernel),
        in_specs=[SMEM, VMEM] + [ANY] * 3,
        out_specs=[VMEM] * (groups + 2),
        out_shape=[jax.ShapeDtypeStruct((2, cap, wide), BF16)] * groups
        + [jax.ShapeDtypeStruct((2, cap, half), BF16), jax.ShapeDtypeStruct((2, cap, HEAD_DIM), F32)],
        scratch_shapes=[
            pltpu.VMEM((cap, width), BF16), pltpu.VMEM((2, cap, half), BF16), pltpu.SemaphoreType.DMA((3,)),
        ],
        compiler_params=pltpu.CompilerParams(vmem_limit_bytes=FRONT * 1024 * 1024),
        cost_estimate=SMALL,
        name="front",
    )(counts, picked_pos, value_own, key_own, query_own)
    kq_in = swapped(sent)
    values = spread(values)
    router_full = lax.all_gather(after(router_weight, table), "fsdp", axis=0, tiled=True)
    sent, gate = call(
        gate_kernel, "gate", [((cap, half), BF16), ((cap, HEAD_DIM), F32)], counts, router_full[None, :], input_own, grad_own
    )
    g_in = swapped(sent)
    v_own, sent = call(kernel(gather_values_kernel), "gather_values", [((total, wide), BF16)] * 2, counts, *values)
    v_in = swapped(sent)
    kq = spread(call(
        kernel(pack_kernel),
        "pack",
        [((2, cap, wide), BF16)] * groups,
        after(counts, v_own), table, key_own, query_own, kq_in,
    ))
    *gated, v = call(
        kernel(pack_gated_kernel),
        "pack_gated",
        [((cap, wide), BF16)] * groups + [((total, wide), BF16)],
        after(counts, kq[-1]), gate, grad_own, g_in, v_own, v_in,
    )
    gated = spread(gated)
    (kq,) = call(kernel(gather_kernel), "gather", [((2, total, wide), BF16)], counts, *kq, cost_estimate=LARGE)

    ds, dv, delta = call(
        kernel(probabilities_kernel),
        "probabilities",
        [((heads, groups, total, cap), BF16), ((total, wide), BF16), ((groups, 8, cap), F32)],
        counts, kq, v, *gated,
        scratch_shapes=[pltpu.VMEM((total, wide), BF16), pltpu.VMEM((total, HEAD_DIM), F32)],
    )
    dv_in = swapped(dv)
    pieces = spread(call(
        kernel(gradients_kernel),
        "gradients",
        [((2 * cap + 16, wide), BF16)] * groups,
        counts, kq, ds, delta,
        scratch_shapes=[pltpu.VMEM((total, HEAD_DIM), F32)] * 2,
    ))
    (delta,) = call(kernel(delta_kernel), "delta", [((8, cap), F32)], *pieces)
    delta_in = swapped(delta)
    own, sent, *v_pieces = call(
        kernel(unpack_kernel),
        "unpack",
        [((2, cap, half), BF16)] * 2 + [((2, cap, wide), BF16)] * groups,
        after(counts, delta), table, dv, dv_in, *pieces,
    )
    other = swapped(sent)
    (part,) = call(
        router_kernel, "router", [((input_own.shape[1] // HEAD_DIM, HEAD_DIM), F32)],
        after(counts, own), delta, delta_in, gate, input_own,
    )
    devices = seq_size * lax.axis_size("fsdp")
    shares = lax.all_to_all(part.reshape(devices, -1), ("seq", "fsdp"), 0, 0)
    grad_router = jnp.sum(shares, axis=0)
    v_pieces = spread(v_pieces)
    grad_q, grad_k, grad_v = pl.pallas_call(
        kernel(place_kernel),
        in_specs=[SMEM] + [VMEM] * (3 + groups),
        out_specs=[ANY] * 3,
        out_shape=[jax.ShapeDtypeStruct((cap, width), BF16)] * 3,
        scratch_shapes=[pltpu.VMEM((4, cap, half), BF16), pltpu.SemaphoreType.DMA((6,))],
        compiler_params=PARAMS,
        cost_estimate=SMALL,
        name="place",
    )(counts, table, own, other, *v_pieces)
    return grad_q[None], grad_k[None], grad_v[None], grad_router


def solution(mesh):
    rows = P("fsdp", "seq", None)
    placed = (rows, rows, rows, rows, rows, P("fsdp"), P("fsdp", "seq"), P("fsdp", "seq"))
    return jax.shard_map(
        per_device,
        mesh=mesh,
        in_specs=placed,
        out_specs=(rows, rows, rows, P(("seq", "fsdp"))),
        check_vma=False,
    )
```

time: 107 us -> 85.5 us (0.80)
  starting transfers between devices: 38.2 us -> 29.1 us
  Pallas kernels: 13.2 us -> 9.07 us
  other arithmetic: 2.49 us -> 0.56 us
  waiting for transfers between devices: 29.6 us -> 27.7 us
  local copies, waits for them, and re-layouts: 3.09 us -> 1.26 us
  blocking collectives: 17.6 us -> 16.2 us
    all_to_all x1 -> x0, waiting for transfers between devices: 6.39 us -> none  [per_device(): delta = jnp.sum(lax.all_to_all(to_pair, 'seq', 0, 0), axis=0)]
    ppermute x17 -> x21, starting transfers between devices: 34.5 us -> 29.1 us  [the longest x15 22.1 us: spread(): lax.ppermute(pieces[m], 'seq', [(i, i ^ 2 * m) for i in range(size)])]
    ppermute x17 -> x21, waiting for transfers between devices: 23.3 us -> 27.7 us  [the longest x15 16.6 us: spread(): lax.ppermute(pieces[m], 'seq', [(i, i ^ 2 * m) for i in range(size)])]
    pallas_call x7 -> x12, Pallas kernels: 13.2 us -> 9.07 us  [the longest x10 4.25 us: call(): pl.pallas_call(kernel, in_specs=[SMEM if a.shape == (1, 1) else VMEM for...]
    all_to_all x1 -> x0, starting transfers between devices: 3.65 us -> none  [per_device(): delta = jnp.sum(lax.all_to_all(to_pair, 'seq', 0, 0), axis=0)]
    another operation x3 -> x0, other arithmetic: 1.8 us -> none  [the longest x2 1.72 us: per_device(): jnp.stack([lax.dynamic_slice_in_dim(a, begin, wide, 1) for a in arrays])]
    all_to_all x1, blocking collectives: 12.4 us -> 11 us  [per_device(): shares = lax.all_to_all(part.reshape(devices, -1), ('seq', 'fsdp'), 0, 0)]
    dynamic_slice x2 -> x0, local copies, waits for them, and re-layouts: 1.31 us -> none  [per_device(): lax.dynamic_slice_in_dim(a, begin, wide, 1)]
  transfers between devices with their start and end apart: 18 -> 21, of which waited for: 4 -> 9; matrix products, arithmetic and copies ran while one was open for 3% -> 1% of each run, Pallas kernels for 11% -> 3%
where the time goes in v2:
time: 85.5 us; the launch traced here: 85.2 us
  starting transfers between devices  29.1 us (34%)
  waiting for transfers between devices  27.7 us (32%)
  blocking collectives  16.2 us (19%)
  Pallas kernels  9.07 us (11%)
  between operations  1.43 us (2%)
  local copies, waits for them, and re-layouts  1.26 us (1%)
    ppermute x15, starting transfers between devices, spread(): lax.ppermute(pieces[m], 'seq', [(i, i ^ 2 * m) for i in range(size)])  22.1 us
    ppermute x15, waiting for transfers between devices, spread(): lax.ppermute(pieces[m], 'seq', [(i, i ^ 2 * m) for i in range(size)])  16.6 us
    ppermute x6, waiting for transfers between devices, swapped(): lax.ppermute(array, 'seq', [(i, i ^ 1) for i in range(lax.axis_size('seq'...  11.1 us
    all_to_all x1, blocking collectives, per_device(): shares = lax.all_to_all(part.reshape(devices, -1), ('seq', 'fsdp'), 0, 0)  11 us
    ppermute x6, starting transfers between devices, swapped(): lax.ppermute(array, 'seq', [(i, i ^ 1) for i in range(lax.axis_size('seq'...  6.92 us
    all_gather x1, blocking collectives, per_device(): lax.all_gather(after(router_weight, table), 'fsdp', axis=0, tiled=True)  5.15 us
    pallas_call x10, Pallas kernels, call(): pl.pallas_call(kernel, in_specs=[SMEM if a.shape == (1, 1) else VMEM for...  4.25 us
    pallas_call x1, Pallas kernels, per_device(): pl.pallas_call(kernel(front_kernel), in_specs=[SMEM, VMEM] + [ANY] * 3, o...  3.49 us
  transfers between devices with their start and end apart: 21, of which 9 were waited for; matrix products, arithmetic and copies ran while one was open for 1% of the time, Pallas kernels for 3%

profile of v2, /device:TPU:0, one launch (start us, length us, event | category | flops | bytes accessed | tf_op | source)
XLA Modules:
  0.0 85.2 jit_solution(12263568387679776148)
XLA Ops:
  1.3 3.5 %front.1 = (bf16[2,128,256]{2,1,0:T(8,128)(2,1)}, bf16[2,128,256]{2,1,0:T(8,128)(2,1)}, bf16[2,128,256]{2,1,0:T(8,128)(2,1)}, bf16[2,128,256]{2,1,0:T(8,128)(2,1...) custom-call(s32[1,1]{1,0:T(1,128)S(6)} %copy.13.counts, s32[1,128]{1,0:T(1,128)} %pos_ref.1, ...), custom_call_target="tpu_custom_call" | custom-call | flops 1048576 | bytes 65536 | tf_op jit(solution)/shard_map/front/pallas_call | solution.py:329
  4.8 3.0 %collective-permute-start.3 = (bf16[2,128,1024]{2,1,0:T(8,128)(2,1)}, bf16[2,128,1024]{2,1,0:T(8,128)(2,1)S(1)}, u32[]{:S(2)}, u32[]{:S(2)}) collective-permute-start(bf16[2,128,1024]{2,1,0:T(8,128)(2,1)} %get-tuple-element.51), channel_id=1, source_target_pairs={{0,4},{4,0},{8,12},{12,8},{16,20},{20,16},{24,28},{28,24},{1,5},{5... | collective-permute-start | bytes 1572872 | tf_op jit(solution)/shard_map/ppermute | solution.py:30
  7.8 3.6 %collective-permute-start = (bf16[2,128,256]{2,1,0:T(8,128)(2,1)}, bf16[2,128,256]{2,1,0:T(8,128)(2,1)S(1)}, u32[]{:S(2)}, u32[]{:S(2)}) collective-permute-start(bf16[2,128,256]{2,1,0:T(8,128)(2,1)} %get-tuple-element.45), channel_id=1, source_target_pairs={{0,24},{4,28},{8,16},{12,20},{16,8},{20,12},{24,0},{28,4},{1,25},{... | collective-permute-start | bytes 393224 | tf_op jit(solution)/shard_map/ppermute | solution.py:36
  11.4 0.8 collective-permute-start.2
  12.2 5.2 %all_gather.3 = bf16[4096]{0:T(1024)(128)(2,1)S(1)} all-gather(bf16[1024]{0:T(1024)(128)(2,1)S(1)} %copy-done.7), channel_id=1, replica_groups=mesh['seq'=8,'fsdp'=4] {'fsdp'}, dimensions={0}, use_global_device_ids=true | all-gather | bytes 10240 | tf_op jit(solution)/shard_map/all_gather | solution.py:344
  17.4 1.2 %copy-done = bf16[1,128,4096]{2,1,0:T(8,128)(2,1)S(1)} copy-done((bf16[1,128,4096]{2,1,0:T(8,128)(2,1)S(1)}, bf16[1,128,4096]{2,1,0:T(8,128)(2,1)}, u32[]{:S(2)}) %copy-start) | copy-done | bytes 1048600
  19.6 2.8 %collective-permute-done.1.refs_1_ = bf16[2,128,256]{2,1,0:T(8,128)(2,1)S(1)} collective-permute-done((bf16[2,128,256]{2,1,0:T(8,128)(2,1)}, bf16[2,128,256]{2,1,0:T(8,128)(2,1)S(1)}, u32[]{:S(2)}, u32[]{:S(2)}) %collective-permute-start.1) | collective-permute-done | bytes 131104 | tf_op jit(solution)/shard_map/ppermute | solution.py:36
  23.6 2.5 %collective-permute-start.4 = (bf16[2,128,256]{2,1,0:T(8,128)(2,1)S(1)}, bf16[2,128,256]{2,1,0:T(8,128)(2,1)S(1)}, u32[]{:S(2)}, u32[]{:S(2)}) collective-permute-start(bf16[2,128,256]{2,1,0:T(8,128)(2,1)S(1)} %get-tuple-element.52), channel_id=1, source_target_pairs={{0,24},{4,28},{8,16},{12,20},{16,8},{20,12},{24,0},{28,4},{1,25},{... | collective-permute-start | bytes 393224 | tf_op jit(solution)/shard_map/ppermute | solution.py:36
  26.2 1.9 %collective-permute-start.6 = (bf16[2,128,256]{2,1,0:T(8,128)(2,1)S(1)}, bf16[2,128,256]{2,1,0:T(8,128)(2,1)S(1)}, u32[]{:S(2)}, u32[]{:S(2)}) collective-permute-start(bf16[2,128,256]{2,1,0:T(8,128)(2,1)S(1)} %get-tuple-element.54), channel_id=1, source_target_pairs={{0,8},{4,12},{8,0},{12,4},{16,24},{20,28},{24,16},{28,20},{1,9},{5... | collective-permute-start | bytes 393224 | tf_op jit(solution)/shard_map/ppermute | solution.py:36
  28.4 5.0 %collective-permute-done.8.v_in_ref = bf16[512,256]{1,0:T(8,128)(2,1)S(1)} collective-permute-done((bf16[512,256]{1,0:T(8,128)(2,1)S(1)}, bf16[512,256]{1,0:T(8,128)(2,1)S(1)}, u32[]{:S(2)}, u32[]{:S(2)}) %collective-permute-start.8) | collective-permute-done | bytes 262176 | tf_op jit(solution)/shard_map/ppermute | solution.py:30
  33.6 3.7 %collective-permute-start.9 = (bf16[128,256]{1,0:T(8,128)(2,1)S(1)}, bf16[128,256]{1,0:T(8,128)(2,1)S(1)}, u32[]{:S(2)}, u32[]{:S(2)}) collective-permute-start(bf16[128,256]{1,0:T(8,128)(2,1)S(1)} %get-tuple-element.62), channel_id=1, source_target_pairs={{0,24},{4,28},{8,16},{12,20},{16,8},{20,12},{24,0},{28,4},{1,25},{... | collective-permute-start | bytes 196616 | tf_op jit(solution)/shard_map/ppermute | solution.py:36
  38.1 1.9 %collective-permute-done.9.refs_0_ = bf16[128,256]{1,0:T(8,128)(2,1)S(1)} collective-permute-done((bf16[128,256]{1,0:T(8,128)(2,1)S(1)}, bf16[128,256]{1,0:T(8,128)(2,1)S(1)}, u32[]{:S(2)}, u32[]{:S(2)}) %collective-permute-start.9) | collective-permute-done | bytes 65568 | tf_op jit(solution)/shard_map/ppermute | solution.py:36
  40.0 2.6 %collective-permute-done.10.refs_1_ = bf16[128,256]{1,0:T(8,128)(2,1)S(1)} collective-permute-done((bf16[128,256]{1,0:T(8,128)(2,1)S(1)}, bf16[128,256]{1,0:T(8,128)(2,1)S(1)}, u32[]{:S(2)}, u32[]{:S(2)}) %collective-permute-start.10) | collective-permute-done | bytes 65568 | tf_op jit(solution)/shard_map/ppermute | solution.py:36
  42.8 1.3 %probabilities.1 = (bf16[2,4,512,128]{3,2,1,0:T(8,128)(2,1)S(1)}, bf16[512,256]{1,0:T(8,128)(2,1)S(1)}, f32[4,8,128]{2,1,0:T(8,128)S(1)}) custom-call(s32[1,1]{1,0:T(1,128)S(6)} %copy.13.counts, bf16[2,512,256]{2,1,0:T(8,128)(2,1)S(1)} %gather.1.kq_ref, bf16[512,256]{1,0:T(8,128)(2,1)S(1)} %get-tuple-element.61.v_ref, ...), custom_call_target="tpu_custom_call" | custom-call | flops 1048576 | bytes 65536 | tf_op jit(solution)/shard_map/probabilities/pallas_call | solution.py:46
  45.5 2.3 %collective-permute-start.12 = (bf16[272,256]{1,0:T(8,128)(2,1)S(1)}, bf16[272,256]{1,0:T(8,128)(2,1)S(1)}, u32[]{:S(2)}, u32[]{:S(2)}) collective-permute-start(bf16[272,256]{1,0:T(8,128)(2,1)S(1)} %get-tuple-element.68), channel_id=1, source_target_pairs={{0,24},{4,28},{8,16},{12,20},{16,8},{20,12},{24,0},{28,4},{1,25},{... | collective-permute-start | bytes 417800 | tf_op jit(solution)/shard_map/ppermute | solution.py:36
  47.8 2.1 %collective-permute-start.14 = (bf16[272,256]{1,0:T(8,128)(2,1)S(1)}, bf16[272,256]{1,0:T(8,128)(2,1)S(1)}, u32[]{:S(2)}, u32[]{:S(2)}) collective-permute-start(bf16[272,256]{1,0:T(8,128)(2,1)S(1)} %get-tuple-element.70), channel_id=1, source_target_pairs={{0,8},{4,12},{8,0},{12,4},{16,24},{20,28},{24,16},{28,20},{1,9},{5... | collective-permute-start | bytes 417800 | tf_op jit(solution)/shard_map/ppermute | solution.py:36
  50.0 4.0 %collective-permute-done.12.refs_0_ = bf16[272,256]{1,0:T(8,128)(2,1)S(1)} collective-permute-done((bf16[272,256]{1,0:T(8,128)(2,1)S(1)}, bf16[272,256]{1,0:T(8,128)(2,1)S(1)}, u32[]{:S(2)}, u32[]{:S(2)}) %collective-permute-start.12) | collective-permute-done | bytes 139296 | tf_op jit(solution)/shard_map/ppermute | solution.py:36
  54.0 5.1 %collective-permute-done.13.refs_1_ = bf16[272,256]{1,0:T(8,128)(2,1)S(1)} collective-permute-done((bf16[272,256]{1,0:T(8,128)(2,1)S(1)}, bf16[272,256]{1,0:T(8,128)(2,1)S(1)}, u32[]{:S(2)}, u32[]{:S(2)}) %collective-permute-start.13) | collective-permute-done | bytes 139296 | tf_op jit(solution)/shard_map/ppermute | solution.py:36
  59.7 1.7 %collective-permute-start.16 = (bf16[2,128,1024]{2,1,0:T(8,128)(2,1)S(1)}, bf16[2,128,1024]{2,1,0:T(8,128)(2,1)S(1)}, u32[]{:S(2)}, u32[]{:S(2)}) collective-permute-start(bf16[2,128,1024]{2,1,0:T(8,128)(2,1)S(1)} %get-tuple-element.75), channel_id=1, source_target_pairs={{0,4},{4,0},{8,12},{12,8},{16,20},{20,16},{24,28},{28,24},{1,5},{5... | collective-permute-start | bytes 1572872 | tf_op jit(solution)/shard_map/ppermute | solution.py:30
  61.3 1.8 %collective-permute-start.17 = (bf16[2,128,256]{2,1,0:T(8,128)(2,1)S(1)}, bf16[2,128,256]{2,1,0:T(8,128)(2,1)S(1)}, u32[]{:S(2)}, u32[]{:S(2)}) collective-permute-start(bf16[2,128,256]{2,1,0:T(8,128)(2,1)S(1)} %get-tuple-element.76), channel_id=1, source_target_pairs={{0,24},{4,28},{8,16},{12,20},{16,8},{20,12},{24,0},{28,4},{1,25},{... | collective-permute-start | bytes 393224 | tf_op jit(solution)/shard_map/ppermute | solution.py:36
  63.1 2.6 %collective-permute-start.19 = (bf16[2,128,256]{2,1,0:T(8,128)(2,1)S(1)}, bf16[2,128,256]{2,1,0:T(8,128)(2,1)S(1)}, u32[]{:S(2)}, u32[]{:S(2)}) collective-permute-start(bf16[2,128,256]{2,1,0:T(8,128)(2,1)S(1)} %get-tuple-element.78), channel_id=1, source_target_pairs={{0,8},{4,12},{8,0},{12,4},{16,24},{20,28},{24,16},{28,20},{1,9},{5... | collective-permute-start | bytes 393224 | tf_op jit(solution)/shard_map/ppermute | solution.py:36
  66.1 5.8 %collective-permute-done.20.delta_in_ref = f32[8,128]{1,0:T(8,128)S(1)} collective-permute-done((f32[8,128]{1,0:T(8,128)S(1)}, f32[8,128]{1,0:T(8,128)S(1)}, u32[]{:S(2)}, u32[]{:S(2)}) %collective-permute-start.20) | collective-permute-done | bytes 4128 | tf_op jit(solution)/shard_map/ppermute | solution.py:30
  72.3 11.0 %all_to_all.9 = f32[32,1,128]{2,1,0:T(1,128)S(1)} all-to-all(f32[32,1,128]{2,1,0:T(1,128)S(1)} %bitcast.19), channel_id=1, replica_groups=mesh['seq'=8,'fsdp'=4] {'seq','fsdp'}, dimensions={0} | all-to-all | bytes 32768 | tf_op jit(solution)/shard_map/all_to_all | solution.py:395
  83.9 1.3 %place.1 = (bf16[128,2048]{1,0:T(8,128)(2,1)}, bf16[128,2048]{1,0:T(8,128)(2,1)}, bf16[128,2048]{1,0:T(8,128)(2,1)}) custom-call(s32[1,1]{1,0:T(1,128)S(6)} %copy.13.counts, f32[2,128,128]{2,1,0:T(8,128)S(1)} %copy-done.5, bf16[2,128,1024]{2,1,0:T(8,128)(2,1)S(1)} %get-tuple-element.74.own_ref, bf16[2,128,1024]{2,1,0:T(8,128)(2,1)S(1)} %collective-permute-done.16.in_ref, ...), custom_call_target="tpu_custom_call" | custom-call | flops 1048576 | bytes 65536 | tf_op jit(solution)/shard_map/place/pallas_call | solution.py:398
  (50 shorter events, 7.0 us)
Async XLA Ops:
  1.3 16.1 %copy-start.2 = (bf16[1,128,2048]{2,1,0:T(8,128)(2,1)S(1)}, bf16[1,128,2048]{2,1,0:T(8,128)(2,1)}, u32[]{:S(2)}) copy-start(bf16[1,128,2048]{2,1,0:T(8,128)(2,1)} %param.11) | copy-start | bytes 1572868
  4.8 18.3 %collective-permute-start.3 = (bf16[2,128,1024]{2,1,0:T(8,128)(2,1)}, bf16[2,128,1024]{2,1,0:T(8,128)(2,1)S(1)}, u32[]{:S(2)}, u32[]{:S(2)}) collective-permute-start(bf16[2,128,1024]{2,1,0:T(8,128)(2,1)} %get-tuple-element.51), channel_id=1, source_target_pairs={{0,4},{4,0},{8,12},{12,8},{16,20},{20,16},{24,28},{28,24},{1,5},{5... | collective-permute-start | bytes 1572872 | tf_op jit(solution)/shard_map/ppermute | solution.py:30
  7.8 11.8 %collective-permute-start = (bf16[2,128,256]{2,1,0:T(8,128)(2,1)}, bf16[2,128,256]{2,1,0:T(8,128)(2,1)S(1)}, u32[]{:S(2)}, u32[]{:S(2)}) collective-permute-start(bf16[2,128,256]{2,1,0:T(8,128)(2,1)} %get-tuple-element.45), channel_id=1, source_target_pairs={{0,24},{4,28},{8,16},{12,20},{16,8},{20,12},{24,0},{28,4},{1,25},{... | collective-permute-start | bytes 393224 | tf_op jit(solution)/shard_map/ppermute | solution.py:36
  11.4 11.0 %collective-permute-start.1 = (bf16[2,128,256]{2,1,0:T(8,128)(2,1)}, bf16[2,128,256]{2,1,0:T(8,128)(2,1)S(1)}, u32[]{:S(2)}, u32[]{:S(2)}) collective-permute-start(bf16[2,128,256]{2,1,0:T(8,128)(2,1)} %get-tuple-element.46), channel_id=1, source_target_pairs={{0,16},{4,20},{8,24},{12,28},{16,0},{20,4},{24,8},{28,12},{1,17},{... | collective-permute-start | bytes 393224 | tf_op jit(solution)/shard_map/ppermute | solution.py:36
  11.4 11.0 %collective-permute-start.2 = (bf16[2,128,256]{2,1,0:T(8,128)(2,1)}, bf16[2,128,256]{2,1,0:T(8,128)(2,1)S(1)}, u32[]{:S(2)}, u32[]{:S(2)}) collective-permute-start(bf16[2,128,256]{2,1,0:T(8,128)(2,1)} %get-tuple-element.47), channel_id=1, source_target_pairs={{0,8},{4,12},{8,0},{12,4},{16,24},{20,28},{24,16},{28,20},{1,9},{5... | collective-permute-start | bytes 393224 | tf_op jit(solution)/shard_map/ppermute | solution.py:36
  18.6 4.4 %copy-start.5 = (f32[2,128,128]{2,1,0:T(8,128)S(1)}, f32[2,128,128]{2,1,0:T(8,128)}, u32[]{:S(2)}) copy-start(f32[2,128,128]{2,1,0:T(8,128)} %get-tuple-element.44.table_ref) | copy-start | bytes 393220
  19.2 9.2 %collective-permute-start.7 = (bf16[128,1024]{1,0:T(8,128)(2,1)S(1)}, bf16[128,1024]{1,0:T(8,128)(2,1)S(1)}, u32[]{:S(2)}, u32[]{:S(2)}) collective-permute-start(bf16[128,1024]{1,0:T(8,128)(2,1)S(1)} %get-tuple-element.59), channel_id=1, source_target_pairs={{0,4},{4,0},{8,12},{12,8},{16,20},{20,16},{24,28},{28,24},{1,5},{5... | collective-permute-start | bytes 786440 | tf_op jit(solution)/shard_map/ppermute | solution.py:30
  22.5 10.9 %collective-permute-start.8 = (bf16[512,256]{1,0:T(8,128)(2,1)S(1)}, bf16[512,256]{1,0:T(8,128)(2,1)S(1)}, u32[]{:S(2)}, u32[]{:S(2)}) collective-permute-start(bf16[512,256]{1,0:T(8,128)(2,1)S(1)} %get-tuple-element.60), channel_id=1, source_target_pairs={{0,4},{4,0},{8,12},{12,8},{16,20},{20,16},{24,28},{28,24},{1,5},{5... | collective-permute-start | bytes 786440 | tf_op jit(solution)/shard_map/ppermute | solution.py:30
  23.6 13.6 %collective-permute-start.4 = (bf16[2,128,256]{2,1,0:T(8,128)(2,1)S(1)}, bf16[2,128,256]{2,1,0:T(8,128)(2,1)S(1)}, u32[]{:S(2)}, u32[]{:S(2)}) collective-permute-start(bf16[2,128,256]{2,1,0:T(8,128)(2,1)S(1)} %get-tuple-element.52), channel_id=1, source_target_pairs={{0,24},{4,28},{8,16},{12,20},{16,8},{20,12},{24,0},{28,4},{1,25},{... | collective-permute-start | bytes 393224 | tf_op jit(solution)/shard_map/ppermute | solution.py:36
  26.2 11.9 %collective-permute-start.5 = (bf16[2,128,256]{2,1,0:T(8,128)(2,1)S(1)}, bf16[2,128,256]{2,1,0:T(8,128)(2,1)S(1)}, u32[]{:S(2)}, u32[]{:S(2)}) collective-permute-start(bf16[2,128,256]{2,1,0:T(8,128)(2,1)S(1)} %get-tuple-element.53), channel_id=1, source_target_pairs={{0,16},{4,20},{8,24},{12,28},{16,0},{20,4},{24,8},{28,12},{1,17},{... | collective-permute-start | bytes 393224 | tf_op jit(solution)/shard_map/ppermute | solution.py:36
  26.2 11.9 %collective-permute-start.6 = (bf16[2,128,256]{2,1,0:T(8,128)(2,1)S(1)}, bf16[2,128,256]{2,1,0:T(8,128)(2,1)S(1)}, u32[]{:S(2)}, u32[]{:S(2)}) collective-permute-start(bf16[2,128,256]{2,1,0:T(8,128)(2,1)S(1)} %get-tuple-element.54), channel_id=1, source_target_pairs={{0,8},{4,12},{8,0},{12,4},{16,24},{20,28},{24,16},{28,20},{1,9},{5... | collective-permute-start | bytes 393224 | tf_op jit(solution)/shard_map/ppermute | solution.py:36
  33.6 6.4 %collective-permute-start.9 = (bf16[128,256]{1,0:T(8,128)(2,1)S(1)}, bf16[128,256]{1,0:T(8,128)(2,1)S(1)}, u32[]{:S(2)}, u32[]{:S(2)}) collective-permute-start(bf16[128,256]{1,0:T(8,128)(2,1)S(1)} %get-tuple-element.62), channel_id=1, source_target_pairs={{0,24},{4,28},{8,16},{12,20},{16,8},{20,12},{24,0},{28,4},{1,25},{... | collective-permute-start | bytes 196616 | tf_op jit(solution)/shard_map/ppermute | solution.py:36
  37.3 5.4 %collective-permute-start.10 = (bf16[128,256]{1,0:T(8,128)(2,1)S(1)}, bf16[128,256]{1,0:T(8,128)(2,1)S(1)}, u32[]{:S(2)}, u32[]{:S(2)}) collective-permute-start(bf16[128,256]{1,0:T(8,128)(2,1)S(1)} %get-tuple-element.63), channel_id=1, source_target_pairs={{0,16},{4,20},{8,24},{12,28},{16,0},{20,4},{24,8},{28,12},{1,17},{... | collective-permute-start | bytes 196616 | tf_op jit(solution)/shard_map/ppermute | solution.py:36
  37.3 5.5 %collective-permute-start.11 = (bf16[128,256]{1,0:T(8,128)(2,1)S(1)}, bf16[128,256]{1,0:T(8,128)(2,1)S(1)}, u32[]{:S(2)}, u32[]{:S(2)}) collective-permute-start(bf16[128,256]{1,0:T(8,128)(2,1)S(1)} %get-tuple-element.64), channel_id=1, source_target_pairs={{0,8},{4,12},{8,0},{12,4},{16,24},{20,28},{24,16},{28,20},{1,9},{5... | collective-permute-start | bytes 196616 | tf_op jit(solution)/shard_map/ppermute | solution.py:36
  44.1 14.9 %collective-permute-start.15 = (bf16[512,256]{1,0:T(8,128)(2,1)S(1)}, bf16[512,256]{1,0:T(8,128)(2,1)S(1)}, u32[]{:S(2)}, u32[]{:S(2)}) collective-permute-start(bf16[512,256]{1,0:T(8,128)(2,1)S(1)} %get-tuple-element.73.dv_ref), channel_id=1, source_target_pairs={{0,4},{4,0},{8,12},{12,8},{16,20},{20,16},{24,28},{28,24},{1,5},{5... | collective-permute-start | bytes 786440 | tf_op jit(solution)/shard_map/ppermute | solution.py:30
  45.5 26.5 %copy-start.1 = (bf16[1,128,4096]{2,1,0:T(8,128)(2,1)S(1)}, bf16[1,128,4096]{2,1,0:T(8,128)(2,1)}, u32[]{:S(2)}) copy-start(bf16[1,128,4096]{2,1,0:T(8,128)(2,1)} %param.12) | copy-start | bytes 3145732
  45.5 8.5 %collective-permute-start.12 = (bf16[272,256]{1,0:T(8,128)(2,1)S(1)}, bf16[272,256]{1,0:T(8,128)(2,1)S(1)}, u32[]{:S(2)}, u32[]{:S(2)}) collective-permute-start(bf16[272,256]{1,0:T(8,128)(2,1)S(1)} %get-tuple-element.68), channel_id=1, source_target_pairs={{0,24},{4,28},{8,16},{12,20},{16,8},{20,12},{24,0},{28,4},{1,25},{... | collective-permute-start | bytes 417800 | tf_op jit(solution)/shard_map/ppermute | solution.py:36
  47.8 11.2 %collective-permute-start.13 = (bf16[272,256]{1,0:T(8,128)(2,1)S(1)}, bf16[272,256]{1,0:T(8,128)(2,1)S(1)}, u32[]{:S(2)}, u32[]{:S(2)}) collective-permute-start(bf16[272,256]{1,0:T(8,128)(2,1)S(1)} %get-tuple-element.69), channel_id=1, source_target_pairs={{0,16},{4,20},{8,24},{12,28},{16,0},{20,4},{24,8},{28,12},{1,17},{... | collective-permute-start | bytes 417800 | tf_op jit(solution)/shard_map/ppermute | solution.py:36
  47.8 11.2 %collective-permute-start.14 = (bf16[272,256]{1,0:T(8,128)(2,1)S(1)}, bf16[272,256]{1,0:T(8,128)(2,1)S(1)}, u32[]{:S(2)}, u32[]{:S(2)}) collective-permute-start(bf16[272,256]{1,0:T(8,128)(2,1)S(1)} %get-tuple-element.70), channel_id=1, source_target_pairs={{0,8},{4,12},{8,0},{12,4},{16,24},{20,28},{24,16},{28,20},{1,9},{5... | collective-permute-start | bytes 417800 | tf_op jit(solution)/shard_map/ppermute | solution.py:36
  59.7 24.2 %collective-permute-start.16 = (bf16[2,128,1024]{2,1,0:T(8,128)(2,1)S(1)}, bf16[2,128,1024]{2,1,0:T(8,128)(2,1)S(1)}, u32[]{:S(2)}, u32[]{:S(2)}) collective-permute-start(bf16[2,128,1024]{2,1,0:T(8,128)(2,1)S(1)} %get-tuple-element.75), channel_id=1, source_target_pairs={{0,4},{4,0},{8,12},{12,8},{16,20},{20,16},{24,28},{28,24},{1,5},{5... | collective-permute-start | bytes 1572872 | tf_op jit(solution)/shard_map/ppermute | solution.py:30
  61.3 22.6 %collective-permute-start.17 = (bf16[2,128,256]{2,1,0:T(8,128)(2,1)S(1)}, bf16[2,128,256]{2,1,0:T(8,128)(2,1)S(1)}, u32[]{:S(2)}, u32[]{:S(2)}) collective-permute-start(bf16[2,128,256]{2,1,0:T(8,128)(2,1)S(1)} %get-tuple-element.76), channel_id=1, source_target_pairs={{0,24},{4,28},{8,16},{12,20},{16,8},{20,12},{24,0},{28,4},{1,25},{... | collective-permute-start | bytes 393224 | tf_op jit(solution)/shard_map/ppermute | solution.py:36
  63.1 20.8 %collective-permute-start.18 = (bf16[2,128,256]{2,1,0:T(8,128)(2,1)S(1)}, bf16[2,128,256]{2,1,0:T(8,128)(2,1)S(1)}, u32[]{:S(2)}, u32[]{:S(2)}) collective-permute-start(bf16[2,128,256]{2,1,0:T(8,128)(2,1)S(1)} %get-tuple-element.77), channel_id=1, source_target_pairs={{0,16},{4,20},{8,24},{12,28},{16,0},{20,4},{24,8},{28,12},{1,17},{... | collective-permute-start | bytes 393224 | tf_op jit(solution)/shard_map/ppermute | solution.py:36
  63.1 20.8 %collective-permute-start.19 = (bf16[2,128,256]{2,1,0:T(8,128)(2,1)S(1)}, bf16[2,128,256]{2,1,0:T(8,128)(2,1)S(1)}, u32[]{:S(2)}, u32[]{:S(2)}) collective-permute-start(bf16[2,128,256]{2,1,0:T(8,128)(2,1)S(1)} %get-tuple-element.78), channel_id=1, source_target_pairs={{0,8},{4,12},{8,0},{12,4},{16,24},{20,28},{24,16},{28,20},{1,9},{5... | collective-permute-start | bytes 393224 | tf_op jit(solution)/shard_map/ppermute | solution.py:36
  65.7 6.3 %collective-permute-start.20 = (f32[8,128]{1,0:T(8,128)S(1)}, f32[8,128]{1,0:T(8,128)S(1)}, u32[]{:S(2)}, u32[]{:S(2)}) collective-permute-start(f32[8,128]{1,0:T(8,128)S(1)} %delta.1.delta_ref), channel_id=1, source_target_pairs={{0,4},{4,0},{8,12},{12,8},{16,20},{20,16},{24,28},{28,24},{1,5},{5... | collective-permute-start | bytes 12296 | tf_op jit(solution)/shard_map/ppermute | solution.py:30
  (5 other events, 14.2 us)

commit v3 on v2

v3 whole, which is shorter than its diff:
```python
import functools
import math

import jax
import jax.numpy as jnp
from jax import lax
from jax.experimental import pallas as pl
from jax.experimental.pallas import tpu as pltpu
from jax.sharding import PartitionSpec as P

HEADS = 16
HEAD_DIM = 128
HALF_DIM = HEAD_DIM // 2
TOK_DEV = 512
THETA = 500000.0
NEG = -1e30
SCALE = HEAD_DIM ** -0.5
BF16 = jnp.bfloat16
F32 = jnp.float32
PARAMS = pltpu.CompilerParams(vmem_limit_bytes=40 * 1024 * 1024)
FRONT = 63
COSTS = {"gather": 0.3, "unpack_values": 1, "gate": 1}
VMEM = pl.BlockSpec(memory_space=pltpu.VMEM)
ANY = pl.BlockSpec(memory_space=pl.ANY)
SMEM = pl.BlockSpec(memory_space=pltpu.SMEM)


def swapped(array):
    return lax.ppermute(array, "seq", [(i, i ^ 1) for i in range(lax.axis_size("seq"))])


def spread(pieces):
    size = lax.axis_size("seq")
    arrived = [
        lax.ppermute(pieces[m], "seq", [(i, i ^ (2 * m)) for i in range(size)]) for m in range(len(pieces) - 1, 0, -1)
    ]
    return arrived + [pieces[0]]


def cost(name):
    return pl.CostEstimate(flops=int(COSTS.get(name, 0.001) * 1e9), bytes_accessed=1 << 16, transcendentals=0)


def call(kernel, name, shapes, *operands, wait=(), scratch_shapes=()):
    count = len(operands)

    def body(*refs):
        kernel(*refs[:count], *refs[count + len(wait):])

    return pl.pallas_call(
        body,
        in_specs=[SMEM if a.shape == (1, 1) else VMEM for a in operands] + [ANY] * len(wait),
        out_specs=[VMEM] * len(shapes),
        out_shape=[jax.ShapeDtypeStruct(shape, dtype) for shape, dtype in shapes],
        scratch_shapes=scratch_shapes,
        compiler_params=PARAMS,
        cost_estimate=cost(name),
        name=name,
    )(*operands, *wait)


def dot(a, b, contract):
    return lax.dot_general(a, b, ((contract[0], contract[1]), ((), ())), preferred_element_type=F32)


def lanes(index, width=HEAD_DIM):
    if isinstance(index, int):
        return slice(index * width, (index + 1) * width)
    return pl.ds(pl.multiple_of(index * width, HEAD_DIM), width)


def grid_of(cap):
    row = lax.broadcasted_iota(jnp.int32, (cap, cap), 0)
    column = lax.broadcasted_iota(jnp.int32, (cap, cap), 1)
    return row, column


def own_place(counts):
    index = lax.axis_index("seq")
    return index & 1, index >> 1, counts[0, 0]


def places(counts, cap):
    parity, _, count = own_place(counts)
    first = jnp.where(parity == 0, count, cap - count)
    row, slot = grid_of(cap)
    even = jnp.where((row == slot) & (row < first), 1.0, 0.0)
    odd = jnp.where((row == slot + first) & (row >= first), 1.0, 0.0)
    is_even = parity == 0
    return jnp.where(is_even, even, odd).astype(BF16), jnp.where(is_even, odd, even).astype(BF16)


def rotated(rows, table_ref, direction):
    rows = rows.astype(F32)
    turned = pltpu.roll(rows, HALF_DIM, 1) * table_ref[1]
    rows = rows * table_ref[0]
    return (rows + turned if direction > 0 else rows - turned).astype(BF16)


def put(hot, rows):
    return dot(hot, rows, ((1,), (0,))).astype(BF16)


def taken(hot, rows):
    return dot(hot, rows, ((0,), (0,))).astype(BF16)


def front_kernel(groups, counts, pos_ref, v_ref, k_ref, q_ref, *refs):
    outs, (out_ref, table_ref, v_buffer, kq_buffer, sems) = refs[:groups], refs[groups:]
    cap, half = out_ref.shape[1:]
    wide = outs[0].shape[2]
    heads = half // HEAD_DIM
    parity, group, _ = own_place(counts)
    copies = [pltpu.make_async_copy(v_ref, v_buffer, sems.at[0])]
    for t, ref in enumerate((k_ref, q_ref)):
        copies.append(pltpu.make_async_copy(ref.at[:, lanes(1 - parity, half)], kq_buffer.at[t], sems.at[1 + t]))
    for copy in copies:
        copy.start()
    own_hot, _ = places(counts, cap)
    row, column = grid_of(cap)
    position = (lax.axis_index("seq") * TOK_DEV + pos_ref[0:1, :]).astype(F32)
    position = jnp.sum(jnp.where(row == column, position, 0.0), axis=1, keepdims=True)
    lane = lax.broadcasted_iota(jnp.int32, (cap, HEAD_DIM), 1)
    feature = jnp.where(lane < HALF_DIM, lane, lane - HALF_DIM).astype(F32)
    angle = position * jnp.exp(feature * (-2.0 / HEAD_DIM * math.log(THETA)))
    table_ref[0] = jnp.cos(angle)
    table_ref[1] = jnp.where(lane < HALF_DIM, -1.0, 1.0) * jnp.sin(angle)
    copies[0].wait()
    for m in range(groups):
        for side in range(2):
            block = (parity ^ side) * groups + (group ^ m)
            outs[m][side] = put(own_hot, v_buffer[:, lanes(block, wide)])
    for t in range(2):
        copies[1 + t].wait()
        for h in range(heads):
            out_ref[t, :, lanes(h)] = put(own_hot, rotated(kq_buffer[t, :, lanes(h)], table_ref, 1))


def gate_kernel(counts, weight_ref, input_ref, g_ref, out_ref, gate_ref):
    cap, half = out_ref.shape
    parity = own_place(counts)[0]
    own_hot, _ = places(counts, cap)
    total = jnp.zeros((cap, HEAD_DIM), F32)
    for b in range(input_ref.shape[1] // HEAD_DIM):
        total += input_ref[:, lanes(b)].astype(F32) * weight_ref[0:1, lanes(b)].astype(F32)
    logit = jnp.sum(total, axis=1, keepdims=True)
    gate = jnp.broadcast_to(1.0 / (1.0 + jnp.exp(-logit)), (cap, HEAD_DIM))
    gate_ref[...] = gate
    heads = half // HEAD_DIM
    for h in range(heads):
        rows = g_ref[:, lanes((1 - parity) * heads + h)].astype(F32) * gate
        out_ref[:, lanes(h)] = put(own_hot, rows.astype(BF16))


def pack_kernel(groups, counts, table_ref, k_ref, q_ref, in_ref, *outs):
    cap, half = in_ref.shape[1:]
    parity, group, _ = own_place(counts)
    own_hot, _ = places(counts, cap)
    heads = half // groups // HEAD_DIM
    for m in range(groups):
        for t, ref in enumerate((k_ref, q_ref)):
            for c in range(heads):
                h = (group ^ m) * heads + c
                rows = rotated(ref[:, lanes(parity * groups * heads + h)], table_ref, 1)
                outs[m][t, :, lanes(c)] = put(own_hot, rows) + in_ref[t, :, lanes(h)]


def pack_gated_kernel(groups, counts, gate_ref, g_ref, in_ref, *outs):
    cap, half = in_ref.shape
    parity, group, _ = own_place(counts)
    own_hot, _ = places(counts, cap)
    heads = half // groups // HEAD_DIM
    for m in range(groups):
        for c in range(heads):
            h = (group ^ m) * heads + c
            rows = g_ref[:, lanes(parity * groups * heads + h)].astype(F32) * gate_ref[...]
            outs[m][:, lanes(c)] = put(own_hot, rows.astype(BF16)) + in_ref[:, lanes(h)]


def block_of(m, cap):
    return pl.ds(pl.multiple_of(((lax.axis_index("seq") >> 1) ^ m) * cap, cap), cap)


def gather_values_kernel(groups, counts, *refs):
    own_ref, send_ref = refs[groups:]
    cap = refs[0].shape[1]
    for i in range(groups):
        block = block_of(groups - 1 - i, cap)
        own_ref[block, :] = refs[i][0]
        send_ref[block, :] = refs[i][1]


def gather_kernel(groups, counts, v_own_ref, v_in_ref, *refs):
    cap = refs[0].shape[1]
    for i in range(groups):
        refs[groups][0:2, block_of(groups - 1 - i, cap), :] = refs[i][...]
    refs[groups][2] = v_own_ref[...] + v_in_ref[...]


def probabilities_kernel(groups, counts, kqv_ref, *refs):
    g_refs, outs, (ds_ref, delta_ref, g_ref, sum_ref) = refs[:groups], refs[groups:2 * groups], refs[2 * groups:]
    cap, wide = g_refs[0].shape
    for i in range(groups):
        g_ref[block_of(groups - 1 - i, cap), :] = g_refs[i][...]
    key, query = grid_of(cap)
    kept = query >= key
    for c in range(wide // HEAD_DIM):
        sum_ref[...] = jnp.zeros_like(sum_ref)
        for i in range(groups):
            upto = (i + 1) * cap
            here = slice(i * cap, upto)
            g = g_ref[here, lanes(c)]
            s = dot(kqv_ref[0, :upto, lanes(c)], kqv_ref[1, here, lanes(c)], ((1,), (1,))) * SCALE
            last = jnp.where(kept, s[i * cap:], NEG)
            s = last if i == 0 else jnp.concatenate([s[:i * cap], last], axis=0)
            e = jnp.exp(s - jnp.max(s, axis=0, keepdims=True))
            p = e * (1.0 / jnp.sum(e, axis=0, keepdims=True))
            dp = dot(kqv_ref[2, :upto, lanes(c)], g, ((1,), (1,)))
            delta = jnp.sum(p * dp, axis=0, keepdims=True)
            whole = jnp.broadcast_to(delta, (8, cap))
            delta_ref[i] = whole if c == 0 else delta_ref[i] + whole
            p16 = p.astype(BF16)
            ds_ref[c, i, :upto, :] = (p16.astype(F32) * (dp - delta) * SCALE).astype(BF16)
            sum_ref[:upto, :] += dot(p16, g, ((1,), (0,)))
        for m in range(groups):
            outs[m][:, lanes(c)] = sum_ref[block_of(m, cap), :].astype(BF16)


def grad_keys_kernel(groups, counts, kqv_ref, ds_ref, *refs):
    deltas, outs, sum_ref = refs[:-groups - 1], refs[-groups - 1:-1], refs[-1]
    heads, _, total, cap = ds_ref.shape
    for c in range(heads):
        sum_ref[...] = jnp.zeros_like(sum_ref)
        for i in range(groups):
            upto = (i + 1) * cap
            sum_ref[:upto, :] += dot(ds_ref[c, i, :upto, :], kqv_ref[1, i * cap:upto, lanes(c)], ((1,), (0,)))
        for m in range(groups):
            outs[m][0:cap, lanes(c)] = sum_ref[block_of(m, cap), :].astype(BF16)
    line = lax.broadcasted_iota(jnp.int32, (8, cap), 0)
    for m in range(groups):
        group = own_place(counts)[1] ^ m
        delta = sum(ref[group] for ref in deltas)
        coarse = delta.astype(BF16).astype(F32)
        rows = jnp.where(line == 0, coarse, jnp.where(line == 1, delta - coarse, 0.0))
        rows = jnp.concatenate([rows, jnp.zeros_like(rows)], axis=0).astype(BF16)
        for c in range(heads):
            outs[m][cap:, lanes(c)] = rows


def grad_queries_kernel(groups, counts, kqv_ref, ds_ref, *refs):
    outs, sum_ref = refs[:groups], refs[groups]
    heads, _, total, cap = ds_ref.shape
    for c in range(heads):
        for i in range(groups):
            upto = (i + 1) * cap
            sum_ref[i * cap:upto, :] = dot(ds_ref[c, i, :upto, :], kqv_ref[0, :upto, lanes(c)], ((0,), (0,)))
        for m in range(groups):
            outs[m][:, lanes(c)] = sum_ref[block_of(m, cap), :].astype(BF16)


def unpack_kernel(groups, turned, counts, table_ref, *refs):
    ins, own_ref, send_ref, token_ref = refs[:groups], refs[groups], refs[groups + 1], refs[groups + 2]
    cap = own_ref.shape[0]
    wide = ins[0].shape[1]
    heads = wide // HEAD_DIM
    own_hot, in_hot = places(counts, cap)
    for i in range(groups):
        group = own_place(counts)[1] ^ (groups - 1 - i)
        send_ref[:, lanes(group, wide)] = taken(in_hot, ins[i][0:cap, :])
        for c in range(heads):
            own = dot(own_hot, ins[i][0:cap, lanes(c)], ((0,), (0,)))
            own_ref[:, lanes(group * heads + c)] = rotated(own, table_ref, -1) if turned else own.astype(BF16)
    token_ref[...] = jnp.zeros_like(token_ref)


def delta_kernel(*refs):
    ins, out_ref = refs[:-1], refs[-1]
    rows = ins[0].shape[0]
    total = ins[0][rows - 16:, 0:HEAD_DIM].astype(F32)
    for ref in ins[1:]:
        total += ref[rows - 16:, 0:HEAD_DIM].astype(F32)
    out_ref[...] = jnp.broadcast_to(total[0:1, :] + total[1:2, :], out_ref.shape)


def router_kernel(counts, gate_ref, input_ref, *refs):
    deltas, out_ref = refs[:-1], refs[-1]
    cap = input_ref.shape[0]
    parity, _, count = own_place(counts)
    row, column = grid_of(cap)
    start = jnp.where(parity == 0, 0, cap - count)
    own = jnp.where((column == row + start) & (row < count), sum(ref[0:1, :] for ref in deltas), 0.0)
    term = (1.0 - gate_ref[...]) * jnp.sum(own, axis=1, keepdims=True)
    for b in range(out_ref.shape[0]):
        out_ref[b:b + 1, :] = jnp.sum(input_ref[:, lanes(b)].astype(F32) * term, axis=0, keepdims=True)


def total_kernel(in_ref, out_ref):
    out_ref[...] = jnp.sum(in_ref[...], axis=0, keepdims=True)


def place_kernel(turned, counts, table_ref, own_ref, in_ref, out_ref, token_ref):
    half = own_ref.shape[1]
    heads = half // HEAD_DIM
    parity = own_place(counts)[0]
    out_ref[:, lanes(parity, half)] = own_ref[...]
    token_ref[...] = jnp.zeros_like(token_ref)
    if not turned:
        out_ref[:, lanes(1 - parity, half)] = in_ref[...]
        return
    for h in range(heads):
        out_ref[:, lanes((1 - parity) * heads + h)] = rotated(in_ref[:, lanes(h)], table_ref, -1)


def per_device(queries, key_rows, value_rows, out_grad, inputs, router_weight, counts, picked_pos):
    query_own, key_own, value_own, grad_own, input_own = queries[0], key_rows[0], value_rows[0], out_grad[0], inputs[0]
    cap, width = query_own.shape
    half = width // 2
    seq_size = lax.axis_size("seq")
    groups = seq_size // 2
    wide = half // groups
    total = groups * cap
    heads = wide // HEAD_DIM

    def kernel(body):
        return functools.partial(body, groups)

    *values, sent, table = pl.pallas_call(
        kernel(front_kernel),
        in_specs=[SMEM, VMEM] + [ANY] * 3,
        out_specs=[VMEM] * (groups + 2),
        out_shape=[jax.ShapeDtypeStruct((2, cap, wide), BF16)] * groups
        + [jax.ShapeDtypeStruct((2, cap, half), BF16), jax.ShapeDtypeStruct((2, cap, HEAD_DIM), F32)],
        scratch_shapes=[
            pltpu.VMEM((cap, width), BF16), pltpu.VMEM((2, cap, half), BF16), pltpu.SemaphoreType.DMA((3,)),
        ],
        compiler_params=pltpu.CompilerParams(vmem_limit_bytes=FRONT * 1024 * 1024),
        cost_estimate=cost("front"),
        name="front",
    )(counts, picked_pos, value_own, key_own, query_own)
    kq_in = swapped(sent)
    values = spread(values)
    router_full = lax.all_gather(router_weight, "fsdp", axis=0, tiled=True)
    sent, gate = call(
        gate_kernel, "gate", [((cap, half), BF16), ((cap, HEAD_DIM), F32)], counts, router_full[None, :], input_own, grad_own
    )
    g_in = swapped(sent)
    kq = spread(call(
        kernel(pack_kernel),
        "pack",
        [((2, cap, wide), BF16)] * groups,
        counts, table, key_own, query_own, kq_in,
    ))
    v_own, sent = call(
        kernel(gather_values_kernel), "gather_values", [((total, wide), BF16)] * 2, counts, *values, wait=kq[-1:]
    )
    v_in = swapped(sent)
    gated = spread(call(
        kernel(pack_gated_kernel),
        "pack_gated",
        [((cap, wide), BF16)] * groups,
        counts, gate, grad_own, g_in, wait=[v_own],
    ))
    kqv = call(
        kernel(gather_kernel), "gather", [((3, total, wide), BF16)], counts, v_own, v_in, *kq
    )[0]

    piece = ((cap, wide), BF16)
    *pieces, ds, delta = call(
        kernel(probabilities_kernel),
        "probabilities",
        [piece] * groups + [((heads, groups, total, cap), BF16), ((groups, 8, cap), F32)],
        counts, kqv, *gated,
        scratch_shapes=[pltpu.VMEM((total, wide), BF16), pltpu.VMEM((total, HEAD_DIM), F32)],
    )
    v_pieces = spread(pieces)
    k_pieces = spread(call(
        kernel(grad_keys_kernel),
        "grad_keys",
        [((cap + 16, wide), BF16)] * groups,
        counts, kqv, ds, delta,
        scratch_shapes=[pltpu.VMEM((total, HEAD_DIM), F32)],
    ))

    def unpacked(name, turned, pieces, wait=()):
        shapes = [((cap, half), BF16)] * 2 + [((8, cap), F32)]
        return call(functools.partial(unpack_kernel, groups, turned), name, shapes, counts, table, *pieces, wait=wait)

    def placed(name, turned, own, other, wait):
        body = functools.partial(place_kernel, turned)
        return call(body, name, [((cap, width), BF16), ((8, HEAD_DIM), F32)], counts, table, own, other, wait=wait)

    v_own, sent, token = unpacked("unpack_values", False, v_pieces, k_pieces[-1:])
    v_in = swapped(sent)
    grad_v, token_v = placed("place_values", False, v_own, v_in, [])
    q_pieces = spread(call(
        kernel(grad_queries_kernel),
        "grad_queries",
        [piece] * groups,
        counts, kqv, ds,
        wait=[token],
        scratch_shapes=[pltpu.VMEM((total, HEAD_DIM), F32)],
    ))
    (delta,) = call(delta_kernel, "delta", [((8, cap), F32)], *k_pieces)
    delta_in = swapped(delta)
    k_own, sent, token_k = unpacked("unpack_keys", True, k_pieces, q_pieces[:1])
    k_in = swapped(sent)
    (part,) = call(
        router_kernel, "router", [((input_own.shape[1] // HEAD_DIM, HEAD_DIM), F32)], counts, gate, input_own, delta, delta_in,
        wait=[token_k],
    )
    q_own, sent, _ = unpacked("unpack_queries", True, q_pieces, [part])
    q_in = swapped(sent)
    grad_k, token_k = placed("place_keys", True, k_own, k_in, [token_v])
    grad_q, _ = placed("place_queries", True, q_own, q_in, [token_k])
    devices = seq_size * lax.axis_size("fsdp")
    shares = lax.all_to_all(part.reshape(devices, -1), ("seq", "fsdp"), 0, 0, tiled=True)
    grad_router = call(total_kernel, "total", [((1, shares.shape[1]), F32)], shares, wait=[token_k])[0][0]
    return grad_q[None], grad_k[None], grad_v[None], grad_router


def solution(mesh):
    rows = P("fsdp", "seq", None)
    placed = (rows, rows, rows, rows, rows, P("fsdp"), P("fsdp", "seq"), P("fsdp", "seq"))
    return jax.shard_map(
        per_device,
        mesh=mesh,
        in_specs=placed,
        out_specs=(rows, rows, rows, P(("seq", "fsdp"))),
        check_vma=False,
    )
```

time: 85.5 us -> 80.7 us (0.944)
  starting transfers between devices: 29.1 us -> 44.3 us
  waiting for transfers between devices: 27.7 us -> 15.2 us
  blocking collectives: 16.2 us -> 5.15 us
  Pallas kernels: 9.07 us -> 13.1 us
    all_to_all x1 -> x0, blocking collectives: 11 us -> none  [per_device(): shares = lax.all_to_all(part.reshape(devices, -1), ('seq', 'fsdp'), 0, 0)]
    ppermute x15 -> x18, starting transfers between devices: 22.1 us -> 32.2 us  [spread(): lax.ppermute(pieces[m], 'seq', [(i, i ^ 2 * m) for i in range(size)])]
    ppermute x6 -> x7, waiting for transfers between devices: 11.1 us -> 1.85 us  [swapped(): lax.ppermute(array, 'seq', [(i, i ^ 1) for i in range(lax.axis_size('seq'...]
    ppermute x15 -> x18, waiting for transfers between devices: 16.6 us -> 8.35 us  [spread(): lax.ppermute(pieces[m], 'seq', [(i, i ^ 2 * m) for i in range(size)])]
    all_to_all x0 -> x1, waiting for transfers between devices: none -> 5.01 us  [per_device(): lax.all_to_all(part.reshape(devices, -1), ('seq', 'fsdp'), 0, 0, tiled=True)]
    all_to_all x0 -> x1, starting transfers between devices: none -> 4.23 us  [per_device(): lax.all_to_all(part.reshape(devices, -1), ('seq', 'fsdp'), 0, 0, tiled=True)]
    pallas_call x11 -> x17, Pallas kernels: 5.59 us -> 9.57 us  [call(): pl.pallas_call(body, in_specs=[SMEM if a.shape == (1, 1) else VMEM for a...]
    ppermute x6 -> x7, starting transfers between devices: 6.92 us -> 7.89 us  [swapped(): lax.ppermute(array, 'seq', [(i, i ^ 1) for i in range(lax.axis_size('seq'...]
  transfers between devices with their start and end apart: 21 -> 26, of which waited for: 9 -> 11; matrix products, arithmetic and copies ran while one was open for 1% -> 0% of each run, Pallas kernels for 3% -> 9%
where the time goes in v3:
time: 80.7 us; the launch traced here: 80.4 us
  starting transfers between devices  44.3 us (55%)
  waiting for transfers between devices  15.2 us (19%)
  Pallas kernels  13.1 us (16%)
  blocking collectives  5.15 us (6%)
  between operations  1.47 us (2%)
  local copies, waits for them, and re-layouts  1.26 us (2%)
    ppermute x18, starting transfers between devices, spread(): lax.ppermute(pieces[m], 'seq', [(i, i ^ 2 * m) for i in range(size)])  32.2 us
    pallas_call x17, Pallas kernels, call(): pl.pallas_call(body, in_specs=[SMEM if a.shape == (1, 1) else VMEM for a...  9.57 us
    ppermute x18, waiting for transfers between devices, spread(): lax.ppermute(pieces[m], 'seq', [(i, i ^ 2 * m) for i in range(size)])  8.35 us
    ppermute x7, starting transfers between devices, swapped(): lax.ppermute(array, 'seq', [(i, i ^ 1) for i in range(lax.axis_size('seq'...  7.89 us
    all_gather x1, blocking collectives, per_device(): router_full = lax.all_gather(router_weight, 'fsdp', axis=0, tiled=True)  5.15 us
    all_to_all x1, waiting for transfers between devices, per_device(): lax.all_to_all(part.reshape(devices, -1), ('seq', 'fsdp'), 0, 0, tiled=True)  5.01 us
    all_to_all x1, starting transfers between devices, per_device(): lax.all_to_all(part.reshape(devices, -1), ('seq', 'fsdp'), 0, 0, tiled=True)  4.23 us
    pallas_call x1, Pallas kernels, per_device(): pl.pallas_call(kernel(front_kernel), in_specs=[SMEM, VMEM] + [ANY] * 3, o...  3.49 us
  transfers between devices with their start and end apart: 26, of which 11 were waited for; matrix products, arithmetic and copies ran while one was open for 0% of the time, Pallas kernels for 9%

profile of v3, /device:TPU:0, one launch (start us, length us, event | category | flops | bytes accessed | tf_op | source)
XLA Modules:
  0.0 80.4 jit_solution(15367140377686163022)
XLA Ops:
  1.3 3.5 %front.1 = (bf16[2,128,256]{2,1,0:T(8,128)(2,1)}, bf16[2,128,256]{2,1,0:T(8,128)(2,1)}, bf16[2,128,256]{2,1,0:T(8,128)(2,1)}, bf16[2,128,256]{2,1,0:T(8,128)(2,1...) custom-call(s32[1,1]{1,0:T(1,128)S(6)} %copy.13.counts.refs_0_, s32[1,128]{1,0:T(1,128)} %pos_ref.1, ...), custom_call_target="tpu_custom_call" | custom-call | flops 1000000 | bytes 65536 | tf_op jit(solution)/shard_map/front/pallas_call | solution.py:327
  4.8 3.0 %collective-permute-start.3 = (bf16[2,128,1024]{2,1,0:T(8,128)(2,1)}, bf16[2,128,1024]{2,1,0:T(8,128)(2,1)S(1)}, u32[]{:S(2)}, u32[]{:S(2)}) collective-permute-start(bf16[2,128,1024]{2,1,0:T(8,128)(2,1)} %get-tuple-element.54), channel_id=1, source_target_pairs={{0,4},{4,0},{8,12},{12,8},{16,20},{20,16},{24,28},{28,24},{1,5},{5... | collective-permute-start | bytes 1572872 | tf_op jit(solution)/shard_map/ppermute | solution.py:29
  7.8 3.6 %collective-permute-start = (bf16[2,128,256]{2,1,0:T(8,128)(2,1)}, bf16[2,128,256]{2,1,0:T(8,128)(2,1)S(1)}, u32[]{:S(2)}, u32[]{:S(2)}) collective-permute-start(bf16[2,128,256]{2,1,0:T(8,128)(2,1)} %get-tuple-element.50), channel_id=1, source_target_pairs={{0,24},{4,28},{8,16},{12,20},{16,8},{20,12},{24,0},{28,4},{1,25},{... | collective-permute-start | bytes 393224 | tf_op jit(solution)/shard_map/ppermute | solution.py:35
  12.2 5.2 %all_gather.3 = bf16[4096]{0:T(1024)(128)(2,1)S(1)} all-gather(bf16[1024]{0:T(1024)(128)(2,1)S(1)} %copy-done.7), channel_id=1, replica_groups=mesh['seq'=8,'fsdp'=4] {'fsdp'}, dimensions={0}, use_global_device_ids=true | all-gather | bytes 10240 | tf_op jit(solution)/shard_map/all_gather | solution.py:342
  17.4 1.2 %copy-done.3 = bf16[1,128,4096]{2,1,0:T(8,128)(2,1)S(1)} copy-done((bf16[1,128,4096]{2,1,0:T(8,128)(2,1)S(1)}, bf16[1,128,4096]{2,1,0:T(8,128)(2,1)}, u32[]{:S(2)}) %copy-start.3) | copy-done | bytes 1048600
  20.5 1.9 %collective-permute-done.1.refs_2_ = bf16[2,128,256]{2,1,0:T(8,128)(2,1)S(1)} collective-permute-done((bf16[2,128,256]{2,1,0:T(8,128)(2,1)}, bf16[2,128,256]{2,1,0:T(8,128)(2,1)S(1)}, u32[]{:S(2)}, u32[]{:S(2)}) %collective-permute-start.1) | collective-permute-done | bytes 131104 | tf_op jit(solution)/shard_map/ppermute | solution.py:35
  23.1 3.3 %collective-permute-start.5 = (bf16[2,128,256]{2,1,0:T(8,128)(2,1)S(1)}, bf16[2,128,256]{2,1,0:T(8,128)(2,1)S(1)}, u32[]{:S(2)}, u32[]{:S(2)}) collective-permute-start(bf16[2,128,256]{2,1,0:T(8,128)(2,1)S(1)} %get-tuple-element.58), channel_id=1, source_target_pairs={{0,24},{4,28},{8,16},{12,20},{16,8},{20,12},{24,0},{28,4},{1,25},{... | collective-permute-start | bytes 393224 | tf_op jit(solution)/shard_map/ppermute | solution.py:35
  26.3 1.1 %collective-permute-start.7 = (bf16[2,128,256]{2,1,0:T(8,128)(2,1)S(1)}, bf16[2,128,256]{2,1,0:T(8,128)(2,1)S(1)}, u32[]{:S(2)}, u32[]{:S(2)}) collective-permute-start(bf16[2,128,256]{2,1,0:T(8,128)(2,1)S(1)} %get-tuple-element.60), channel_id=1, source_target_pairs={{0,8},{4,12},{8,0},{12,4},{16,24},{20,28},{24,16},{28,20},{1,9},{5... | collective-permute-start | bytes 393224 | tf_op jit(solution)/shard_map/ppermute | solution.py:35
  28.6 3.7 %collective-permute-start.9 = (bf16[128,256]{1,0:T(8,128)(2,1)S(1)}, bf16[128,256]{1,0:T(8,128)(2,1)S(1)}, u32[]{:S(2)}, u32[]{:S(2)}) collective-permute-start(bf16[128,256]{1,0:T(8,128)(2,1)S(1)} %get-tuple-element.63), channel_id=1, source_target_pairs={{0,24},{4,28},{8,16},{12,20},{16,8},{20,12},{24,0},{28,4},{1,25},{... | collective-permute-start | bytes 196616 | tf_op jit(solution)/shard_map/ppermute | solution.py:35
  32.3 6.3 %collective-permute-start.10 = (bf16[128,256]{1,0:T(8,128)(2,1)S(1)}, bf16[128,256]{1,0:T(8,128)(2,1)S(1)}, u32[]{:S(2)}, u32[]{:S(2)}) collective-permute-start(bf16[128,256]{1,0:T(8,128)(2,1)S(1)} %get-tuple-element.64), channel_id=1, source_target_pairs={{0,16},{4,20},{8,24},{12,28},{16,0},{20,4},{24,8},{28,12},{1,17},{... | collective-permute-start | bytes 196616 | tf_op jit(solution)/shard_map/ppermute | solution.py:35
  38.6 1.4 %collective-permute-done.6.refs_4_ = bf16[2,128,256]{2,1,0:T(8,128)(2,1)S(1)} collective-permute-done((bf16[2,128,256]{2,1,0:T(8,128)(2,1)S(1)}, bf16[2,128,256]{2,1,0:T(8,128)(2,1)S(1)}, u32[]{:S(2)}, u32[]{:S(2)}) %collective-permute-start.6) | collective-permute-done | bytes 131104 | tf_op jit(solution)/shard_map/ppermute | solution.py:35
  40.1 1.4 %collective-permute-done.10.refs_3_ = bf16[128,256]{1,0:T(8,128)(2,1)S(1)} collective-permute-done((bf16[128,256]{1,0:T(8,128)(2,1)S(1)}, bf16[128,256]{1,0:T(8,128)(2,1)S(1)}, u32[]{:S(2)}, u32[]{:S(2)}) %collective-permute-start.10) | collective-permute-done | bytes 65568 | tf_op jit(solution)/shard_map/ppermute | solution.py:35
  41.5 2.8 %collective-permute-done.11.refs_4_ = bf16[128,256]{1,0:T(8,128)(2,1)S(1)} collective-permute-done((bf16[128,256]{1,0:T(8,128)(2,1)S(1)}, bf16[128,256]{1,0:T(8,128)(2,1)S(1)}, u32[]{:S(2)}, u32[]{:S(2)}) %collective-permute-start.11) | collective-permute-done | bytes 65568 | tf_op jit(solution)/shard_map/ppermute | solution.py:35
  44.2 1.3 %probabilities.1 = (bf16[128,256]{1,0:T(8,128)(2,1)S(1)}, bf16[128,256]{1,0:T(8,128)(2,1)S(1)}, bf16[128,256]{1,0:T(8,128)(2,1)S(1)}, bf16[128,256]{1,0:T(8,128)...) custom-call(s32[1,1]{1,0:T(1,128)S(6)} %copy.13.counts.refs_0_, ...), custom_call_target="tpu_custom_call" | custom-call | flops 1000000 | bytes 65536 | tf_op jit(solution)/shard_map/probabilities/pallas_call | solution.py:50
  45.6 2.6 %collective-permute-start.12 = (bf16[128,256]{1,0:T(8,128)(2,1)S(1)}, bf16[128,256]{1,0:T(8,128)(2,1)S(1)}, u32[]{:S(2)}, u32[]{:S(2)}) collective-permute-start(bf16[128,256]{1,0:T(8,128)(2,1)S(1)} %get-tuple-element.68), channel_id=1, source_target_pairs={{0,24},{4,28},{8,16},{12,20},{16,8},{20,12},{24,0},{28,4},{1,25},{... | collective-permute-start | bytes 196616 | tf_op jit(solution)/shard_map/ppermute | solution.py:35
  48.1 1.9 %collective-permute-start.14 = (bf16[128,256]{1,0:T(8,128)(2,1)S(1)}, bf16[128,256]{1,0:T(8,128)(2,1)S(1)}, u32[]{:S(2)}, u32[]{:S(2)}) collective-permute-start(bf16[128,256]{1,0:T(8,128)(2,1)S(1)} %get-tuple-element.70), channel_id=1, source_target_pairs={{0,8},{4,12},{8,0},{12,4},{16,24},{20,28},{24,16},{28,20},{1,9},{5... | collective-permute-start | bytes 196616 | tf_op jit(solution)/shard_map/ppermute | solution.py:35
  50.4 2.6 %collective-permute-start.18 = (bf16[144,256]{1,0:T(8,128)(2,1)S(1)}, bf16[144,256]{1,0:T(8,128)(2,1)S(1)}, u32[]{:S(2)}, u32[]{:S(2)}) collective-permute-start(bf16[144,256]{1,0:T(8,128)(2,1)S(1)} %get-tuple-element.79), channel_id=1, source_target_pairs={{0,24},{4,28},{8,16},{12,20},{16,8},{20,12},{24,0},{28,4},{1,25},{... | collective-permute-start | bytes 221192 | tf_op jit(solution)/shard_map/ppermute | solution.py:35
  53.0 1.9 %collective-permute-start.20 = (bf16[144,256]{1,0:T(8,128)(2,1)S(1)}, bf16[144,256]{1,0:T(8,128)(2,1)S(1)}, u32[]{:S(2)}, u32[]{:S(2)}) collective-permute-start(bf16[144,256]{1,0:T(8,128)(2,1)S(1)} %get-tuple-element.81), channel_id=1, source_target_pairs={{0,8},{4,12},{8,0},{12,4},{16,24},{20,28},{24,16},{28,20},{1,9},{5... | collective-permute-start | bytes 221192 | tf_op jit(solution)/shard_map/ppermute | solution.py:35
  56.0 2.2 %collective-permute-start.15 = (bf16[128,256]{1,0:T(8,128)(2,1)S(1)}, bf16[128,256]{1,0:T(8,128)(2,1)S(1)}, u32[]{:S(2)}, u32[]{:S(2)}) collective-permute-start(bf16[128,256]{1,0:T(8,128)(2,1)S(1)} %get-tuple-element.75), channel_id=1, source_target_pairs={{0,24},{4,28},{8,16},{12,20},{16,8},{20,12},{24,0},{28,4},{1,25},{... | collective-permute-start | bytes 196616 | tf_op jit(solution)/shard_map/ppermute | solution.py:35
  58.3 2.2 %collective-permute-start.17 = (bf16[128,256]{1,0:T(8,128)(2,1)S(1)}, bf16[128,256]{1,0:T(8,128)(2,1)S(1)}, u32[]{:S(2)}, u32[]{:S(2)}) collective-permute-start(bf16[128,256]{1,0:T(8,128)(2,1)S(1)} %get-tuple-element.77), channel_id=1, source_target_pairs={{0,8},{4,12},{8,0},{12,4},{16,24},{20,28},{24,16},{28,20},{1,9},{5... | collective-permute-start | bytes 196616 | tf_op jit(solution)/shard_map/ppermute | solution.py:35
  62.0 1.2 %collective-permute-start.24 = (bf16[128,1024]{1,0:T(8,128)(2,1)S(1)}, bf16[128,1024]{1,0:T(8,128)(2,1)S(1)}, u32[]{:S(2)}, u32[]{:S(2)}) collective-permute-start(bf16[128,1024]{1,0:T(8,128)(2,1)S(1)} %get-tuple-element.88), channel_id=1, source_target_pairs={{0,4},{4,0},{8,12},{12,8},{16,20},{20,16},{24,28},{28,24},{1,5},{5... | collective-permute-start | bytes 786440 | tf_op jit(solution)/shard_map/ppermute | solution.py:29
  67.6 4.2 %all-to-all-start = ((f32[32,1,128]{2,1,0:T(1,128)}), f32[32,1,128]{2,1,0:T(1,128)S(1)}, u32[]{:S(2)}, u32[]{:S(2)}) async-start(f32[32,1,128]{2,1,0:T(1,128)} %bitcast.9), calls=%async_computation | async-start | bytes 32768 | tf_op jit(solution)/shard_map/all_to_all | solution.py:416
  73.9 5.0 %all-to-all-done = f32[32,1,128]{2,1,0:T(1,128)S(1)} async-done(((f32[32,1,128]{2,1,0:T(1,128)}), f32[32,1,128]{2,1,0:T(1,128)S(1)}, u32[]{:S(2)}, u32[]{:S(2)}) %all-to-all-start) | async-done | bytes 16416 | tf_op jit(solution)/shard_map/all_to_all | solution.py:416
  79.4 1.0 %place_queries.1 = (bf16[128,2048]{1,0:T(8,128)(2,1)}, f32[8,128]{1,0:T(8,128)}) custom-call(s32[1,1]{1,0:T(1,128)S(6)} %copy.13.counts.refs_0_, f32[2,128,128]{2,1,0:T(8,128)S(1)} %copy-done, bf16[128,1024]{1,0:T(8,128)(2,1)S(1)} %get-tuple-element.83.refs_2_, bf16[128,1024]{1,0:T(8,128)(2,1)S(1)} %collective-permute-done.22.refs_3_, ...), custom_call_target="tpu_custom_call" | custom-call | flops 1000000 | bytes 65536 | tf_op jit(solution)/shard_map/place_queries/pallas_call | solution.py:50
  (64 shorter events, 14.6 us)
Async XLA Ops:
  4.8 15.2 %collective-permute-start.3 = (bf16[2,128,1024]{2,1,0:T(8,128)(2,1)}, bf16[2,128,1024]{2,1,0:T(8,128)(2,1)S(1)}, u32[]{:S(2)}, u32[]{:S(2)}) collective-permute-start(bf16[2,128,1024]{2,1,0:T(8,128)(2,1)} %get-tuple-element.54), channel_id=1, source_target_pairs={{0,4},{4,0},{8,12},{12,8},{16,20},{20,16},{24,28},{28,24},{1,5},{5... | collective-permute-start | bytes 1572872 | tf_op jit(solution)/shard_map/ppermute | solution.py:29
  7.8 12.7 %collective-permute-start = (bf16[2,128,256]{2,1,0:T(8,128)(2,1)}, bf16[2,128,256]{2,1,0:T(8,128)(2,1)S(1)}, u32[]{:S(2)}, u32[]{:S(2)}) collective-permute-start(bf16[2,128,256]{2,1,0:T(8,128)(2,1)} %get-tuple-element.50), channel_id=1, source_target_pairs={{0,24},{4,28},{8,16},{12,20},{16,8},{20,12},{24,0},{28,4},{1,25},{... | collective-permute-start | bytes 393224 | tf_op jit(solution)/shard_map/ppermute | solution.py:35
  11.4 11.0 %collective-permute-start.1 = (bf16[2,128,256]{2,1,0:T(8,128)(2,1)}, bf16[2,128,256]{2,1,0:T(8,128)(2,1)S(1)}, u32[]{:S(2)}, u32[]{:S(2)}) collective-permute-start(bf16[2,128,256]{2,1,0:T(8,128)(2,1)} %get-tuple-element.51), channel_id=1, source_target_pairs={{0,16},{4,20},{8,24},{12,28},{16,0},{20,4},{24,8},{28,12},{1,17},{... | collective-permute-start | bytes 393224 | tf_op jit(solution)/shard_map/ppermute | solution.py:35
  11.4 11.0 %collective-permute-start.2 = (bf16[2,128,256]{2,1,0:T(8,128)(2,1)}, bf16[2,128,256]{2,1,0:T(8,128)(2,1)S(1)}, u32[]{:S(2)}, u32[]{:S(2)}) collective-permute-start(bf16[2,128,256]{2,1,0:T(8,128)(2,1)} %get-tuple-element.52), channel_id=1, source_target_pairs={{0,8},{4,12},{8,0},{12,4},{16,24},{20,28},{24,16},{28,20},{1,9},{5... | collective-permute-start | bytes 393224 | tf_op jit(solution)/shard_map/ppermute | solution.py:35
  19.1 9.2 %collective-permute-start.8 = (bf16[128,1024]{1,0:T(8,128)(2,1)S(1)}, bf16[128,1024]{1,0:T(8,128)(2,1)S(1)}, u32[]{:S(2)}, u32[]{:S(2)}) collective-permute-start(bf16[128,1024]{1,0:T(8,128)(2,1)S(1)} %get-tuple-element.62), channel_id=1, source_target_pairs={{0,4},{4,0},{8,12},{12,8},{16,20},{20,16},{24,28},{28,24},{1,5},{5... | collective-permute-start | bytes 786440 | tf_op jit(solution)/shard_map/ppermute | solution.py:29
  22.5 17.5 %collective-permute-start.4 = (bf16[512,256]{1,0:T(8,128)(2,1)S(1)}, bf16[512,256]{1,0:T(8,128)(2,1)S(1)}, u32[]{:S(2)}, u32[]{:S(2)}) collective-permute-start(bf16[512,256]{1,0:T(8,128)(2,1)S(1)} %get-tuple-element.57), channel_id=1, source_target_pairs={{0,4},{4,0},{8,12},{12,8},{16,20},{20,16},{24,28},{28,24},{1,5},{5... | collective-permute-start | bytes 786440 | tf_op jit(solution)/shard_map/ppermute | solution.py:29
  23.1 9.2 %collective-permute-start.5 = (bf16[2,128,256]{2,1,0:T(8,128)(2,1)S(1)}, bf16[2,128,256]{2,1,0:T(8,128)(2,1)S(1)}, u32[]{:S(2)}, u32[]{:S(2)}) collective-permute-start(bf16[2,128,256]{2,1,0:T(8,128)(2,1)S(1)} %get-tuple-element.58), channel_id=1, source_target_pairs={{0,24},{4,28},{8,16},{12,20},{16,8},{20,12},{24,0},{28,4},{1,25},{... | collective-permute-start | bytes 393224 | tf_op jit(solution)/shard_map/ppermute | solution.py:35
  26.3 13.7 %collective-permute-start.6 = (bf16[2,128,256]{2,1,0:T(8,128)(2,1)S(1)}, bf16[2,128,256]{2,1,0:T(8,128)(2,1)S(1)}, u32[]{:S(2)}, u32[]{:S(2)}) collective-permute-start(bf16[2,128,256]{2,1,0:T(8,128)(2,1)S(1)} %get-tuple-element.59), channel_id=1, source_target_pairs={{0,16},{4,20},{8,24},{12,28},{16,0},{20,4},{24,8},{28,12},{1,17},{... | collective-permute-start | bytes 393224 | tf_op jit(solution)/shard_map/ppermute | solution.py:35
  26.3 13.7 %collective-permute-start.7 = (bf16[2,128,256]{2,1,0:T(8,128)(2,1)S(1)}, bf16[2,128,256]{2,1,0:T(8,128)(2,1)S(1)}, u32[]{:S(2)}, u32[]{:S(2)}) collective-permute-start(bf16[2,128,256]{2,1,0:T(8,128)(2,1)S(1)} %get-tuple-element.60), channel_id=1, source_target_pairs={{0,8},{4,12},{8,0},{12,4},{16,24},{20,28},{24,16},{28,20},{1,9},{5... | collective-permute-start | bytes 393224 | tf_op jit(solution)/shard_map/ppermute | solution.py:35
  28.6 11.5 %collective-permute-start.9 = (bf16[128,256]{1,0:T(8,128)(2,1)S(1)}, bf16[128,256]{1,0:T(8,128)(2,1)S(1)}, u32[]{:S(2)}, u32[]{:S(2)}) collective-permute-start(bf16[128,256]{1,0:T(8,128)(2,1)S(1)} %get-tuple-element.63), channel_id=1, source_target_pairs={{0,24},{4,28},{8,16},{12,20},{16,8},{20,12},{24,0},{28,4},{1,25},{... | collective-permute-start | bytes 196616 | tf_op jit(solution)/shard_map/ppermute | solution.py:35
  32.3 9.2 %collective-permute-start.10 = (bf16[128,256]{1,0:T(8,128)(2,1)S(1)}, bf16[128,256]{1,0:T(8,128)(2,1)S(1)}, u32[]{:S(2)}, u32[]{:S(2)}) collective-permute-start(bf16[128,256]{1,0:T(8,128)(2,1)S(1)} %get-tuple-element.64), channel_id=1, source_target_pairs={{0,16},{4,20},{8,24},{12,28},{16,0},{20,4},{24,8},{28,12},{1,17},{... | collective-permute-start | bytes 196616 | tf_op jit(solution)/shard_map/ppermute | solution.py:35
  45.6 7.4 %collective-permute-start.12 = (bf16[128,256]{1,0:T(8,128)(2,1)S(1)}, bf16[128,256]{1,0:T(8,128)(2,1)S(1)}, u32[]{:S(2)}, u32[]{:S(2)}) collective-permute-start(bf16[128,256]{1,0:T(8,128)(2,1)S(1)} %get-tuple-element.68), channel_id=1, source_target_pairs={{0,24},{4,28},{8,16},{12,20},{16,8},{20,12},{24,0},{28,4},{1,25},{... | collective-permute-start | bytes 196616 | tf_op jit(solution)/shard_map/ppermute | solution.py:35
  48.1 7.1 %collective-permute-start.13 = (bf16[128,256]{1,0:T(8,128)(2,1)S(1)}, bf16[128,256]{1,0:T(8,128)(2,1)S(1)}, u32[]{:S(2)}, u32[]{:S(2)}) collective-permute-start(bf16[128,256]{1,0:T(8,128)(2,1)S(1)} %get-tuple-element.69), channel_id=1, source_target_pairs={{0,16},{4,20},{8,24},{12,28},{16,0},{20,4},{24,8},{28,12},{1,17},{... | collective-permute-start | bytes 196616 | tf_op jit(solution)/shard_map/ppermute | solution.py:35
  48.1 7.1 %collective-permute-start.14 = (bf16[128,256]{1,0:T(8,128)(2,1)S(1)}, bf16[128,256]{1,0:T(8,128)(2,1)S(1)}, u32[]{:S(2)}, u32[]{:S(2)}) collective-permute-start(bf16[128,256]{1,0:T(8,128)(2,1)S(1)} %get-tuple-element.70), channel_id=1, source_target_pairs={{0,8},{4,12},{8,0},{12,4},{16,24},{20,28},{24,16},{28,20},{1,9},{5... | collective-permute-start | bytes 196616 | tf_op jit(solution)/shard_map/ppermute | solution.py:35
  50.4 7.8 %collective-permute-start.18 = (bf16[144,256]{1,0:T(8,128)(2,1)S(1)}, bf16[144,256]{1,0:T(8,128)(2,1)S(1)}, u32[]{:S(2)}, u32[]{:S(2)}) collective-permute-start(bf16[144,256]{1,0:T(8,128)(2,1)S(1)} %get-tuple-element.79), channel_id=1, source_target_pairs={{0,24},{4,28},{8,16},{12,20},{16,8},{20,12},{24,0},{28,4},{1,25},{... | collective-permute-start | bytes 221192 | tf_op jit(solution)/shard_map/ppermute | solution.py:35
  53.0 8.1 %collective-permute-start.19 = (bf16[144,256]{1,0:T(8,128)(2,1)S(1)}, bf16[144,256]{1,0:T(8,128)(2,1)S(1)}, u32[]{:S(2)}, u32[]{:S(2)}) collective-permute-start(bf16[144,256]{1,0:T(8,128)(2,1)S(1)} %get-tuple-element.80), channel_id=1, source_target_pairs={{0,16},{4,20},{8,24},{12,28},{16,0},{20,4},{24,8},{28,12},{1,17},{... | collective-permute-start | bytes 221192 | tf_op jit(solution)/shard_map/ppermute | solution.py:35
  53.0 8.1 %collective-permute-start.20 = (bf16[144,256]{1,0:T(8,128)(2,1)S(1)}, bf16[144,256]{1,0:T(8,128)(2,1)S(1)}, u32[]{:S(2)}, u32[]{:S(2)}) collective-permute-start(bf16[144,256]{1,0:T(8,128)(2,1)S(1)} %get-tuple-element.81), channel_id=1, source_target_pairs={{0,8},{4,12},{8,0},{12,4},{16,24},{20,28},{24,16},{28,20},{1,9},{5... | collective-permute-start | bytes 221192 | tf_op jit(solution)/shard_map/ppermute | solution.py:35
  56.0 7.1 %collective-permute-start.15 = (bf16[128,256]{1,0:T(8,128)(2,1)S(1)}, bf16[128,256]{1,0:T(8,128)(2,1)S(1)}, u32[]{:S(2)}, u32[]{:S(2)}) collective-permute-start(bf16[128,256]{1,0:T(8,128)(2,1)S(1)} %get-tuple-element.75), channel_id=1, source_target_pairs={{0,24},{4,28},{8,16},{12,20},{16,8},{20,12},{24,0},{28,4},{1,25},{... | collective-permute-start | bytes 196616 | tf_op jit(solution)/shard_map/ppermute | solution.py:35
  58.3 7.5 %collective-permute-start.16 = (bf16[128,256]{1,0:T(8,128)(2,1)S(1)}, bf16[128,256]{1,0:T(8,128)(2,1)S(1)}, u32[]{:S(2)}, u32[]{:S(2)}) collective-permute-start(bf16[128,256]{1,0:T(8,128)(2,1)S(1)} %get-tuple-element.76), channel_id=1, source_target_pairs={{0,16},{4,20},{8,24},{12,28},{16,0},{20,4},{24,8},{28,12},{1,17},{... | collective-permute-start | bytes 196616 | tf_op jit(solution)/shard_map/ppermute | solution.py:35
  58.3 7.5 %collective-permute-start.17 = (bf16[128,256]{1,0:T(8,128)(2,1)S(1)}, bf16[128,256]{1,0:T(8,128)(2,1)S(1)}, u32[]{:S(2)}, u32[]{:S(2)}) collective-permute-start(bf16[128,256]{1,0:T(8,128)(2,1)S(1)} %get-tuple-element.77), channel_id=1, source_target_pairs={{0,8},{4,12},{8,0},{12,4},{16,24},{20,28},{24,16},{28,20},{1,9},{5... | collective-permute-start | bytes 196616 | tf_op jit(solution)/shard_map/ppermute | solution.py:35
  62.0 9.8 %collective-permute-start.24 = (bf16[128,1024]{1,0:T(8,128)(2,1)S(1)}, bf16[128,1024]{1,0:T(8,128)(2,1)S(1)}, u32[]{:S(2)}, u32[]{:S(2)}) collective-permute-start(bf16[128,1024]{1,0:T(8,128)(2,1)S(1)} %get-tuple-element.88), channel_id=1, source_target_pairs={{0,4},{4,0},{8,12},{12,8},{16,20},{20,16},{24,28},{28,24},{1,5},{5... | collective-permute-start | bytes 786440 | tf_op jit(solution)/shard_map/ppermute | solution.py:29
  63.6 9.3 %collective-permute-start.23 = (bf16[128,1024]{1,0:T(8,128)(2,1)S(1)}, bf16[128,1024]{1,0:T(8,128)(2,1)S(1)}, u32[]{:S(2)}, u32[]{:S(2)}) collective-permute-start(bf16[128,1024]{1,0:T(8,128)(2,1)S(1)} %get-tuple-element.86), channel_id=1, source_target_pairs={{0,4},{4,0},{8,12},{12,8},{16,20},{20,16},{24,28},{28,24},{1,5},{5... | collective-permute-start | bytes 786440 | tf_op jit(solution)/shard_map/ppermute | solution.py:29
  66.7 12.8 %collective-permute-start.22 = (bf16[128,1024]{1,0:T(8,128)(2,1)S(1)}, bf16[128,1024]{1,0:T(8,128)(2,1)S(1)}, u32[]{:S(2)}, u32[]{:S(2)}) collective-permute-start(bf16[128,1024]{1,0:T(8,128)(2,1)S(1)} %get-tuple-element.84), channel_id=1, source_target_pairs={{0,4},{4,0},{8,12},{12,8},{16,20},{20,16},{24,28},{28,24},{1,5},{5... | collective-permute-start | bytes 786440 | tf_op jit(solution)/shard_map/ppermute | solution.py:29
  67.6 11.3 %all-to-all-start = ((f32[32,1,128]{2,1,0:T(1,128)}), f32[32,1,128]{2,1,0:T(1,128)S(1)}, u32[]{:S(2)}, u32[]{:S(2)}) async-start(f32[32,1,128]{2,1,0:T(1,128)} %bitcast.9), calls=%async_computation | async-start | bytes 32768 | tf_op jit(solution)/shard_map/all_to_all | solution.py:416
  (10 other events, 45.4 us)

commit v4 on v3

--- a/solution.py
+++ b/solution.py
@@ -18,10 +18,10 @@
 BF16 = jnp.bfloat16
 F32 = jnp.float32
 PARAMS = pltpu.CompilerParams(vmem_limit_bytes=40 * 1024 * 1024)
-FRONT = 63
-COSTS = {"gather": 0.3, "unpack_values": 1, "gate": 1}
+COSTS = {"gather": 0.3, "gate": 1, "place_keys": 0.5, "router": 1}
 VMEM = pl.BlockSpec(memory_space=pltpu.VMEM)
 ANY = pl.BlockSpec(memory_space=pl.ANY)
+HBM = pl.BlockSpec(memory_space=pltpu.HBM)
 SMEM = pl.BlockSpec(memory_space=pltpu.SMEM)
 
 
@@ -106,34 +106,41 @@
 
 
 def front_kernel(groups, counts, pos_ref, v_ref, k_ref, q_ref, *refs):
-    outs, (out_ref, table_ref, v_buffer, kq_buffer, sems) = refs[:groups], refs[groups:]
+    outs, out_ref, table_ref = refs[:groups], refs[groups], refs[groups + 1]
+    pos, v_buffer, kq_buffer, sems = refs[groups + 2:]
     cap, half = out_ref.shape[1:]
     wide = outs[0].shape[2]
     heads = half // HEAD_DIM
-    parity, group, _ = own_place(counts)
-    copies = [pltpu.make_async_copy(v_ref, v_buffer, sems.at[0])]
-    for t, ref in enumerate((k_ref, q_ref)):
-        copies.append(pltpu.make_async_copy(ref.at[:, lanes(1 - parity, half)], kq_buffer.at[t], sems.at[1 + t]))
-    for copy in copies:
+    index = lax.axis_index("seq")
+    parity, group = index & 1, index >> 1
+    small = [pltpu.make_async_copy(pos_ref, pos, sems.at[1])]
+    large = [
+        pltpu.make_async_copy(ref.at[:, lanes(1 - parity, half)], kq_buffer.at[t], sems.at[2 + t])
+        for t, ref in enumerate((k_ref, q_ref))
+    ]
+    large.append(pltpu.make_async_copy(v_ref, v_buffer, sems.at[4]))
+    for copy in small + large:
         copy.start()
+    for copy in small:
+        copy.wait()
     own_hot, _ = places(counts, cap)
     row, column = grid_of(cap)
-    position = (lax.axis_index("seq") * TOK_DEV + pos_ref[0:1, :]).astype(F32)
+    position = (index * TOK_DEV + pos[0:1, :]).astype(F32)
     position = jnp.sum(jnp.where(row == column, position, 0.0), axis=1, keepdims=True)
     lane = lax.broadcasted_iota(jnp.int32, (cap, HEAD_DIM), 1)
     feature = jnp.where(lane < HALF_DIM, lane, lane - HALF_DIM).astype(F32)
     angle = position * jnp.exp(feature * (-2.0 / HEAD_DIM * math.log(THETA)))
     table_ref[0] = jnp.cos(angle)
     table_ref[1] = jnp.where(lane < HALF_DIM, -1.0, 1.0) * jnp.sin(angle)
-    copies[0].wait()
+    for t in range(2):
+        large[t].wait()
+        for h in range(heads):
+            out_ref[t, :, lanes(h)] = put(own_hot, rotated(kq_buffer[t, :, lanes(h)], table_ref, 1))
+    large[2].wait()
     for m in range(groups):
         for side in range(2):
             block = (parity ^ side) * groups + (group ^ m)
             outs[m][side] = put(own_hot, v_buffer[:, lanes(block, wide)])
-    for t in range(2):
-        copies[1 + t].wait()
-        for h in range(heads):
-            out_ref[t, :, lanes(h)] = put(own_hot, rotated(kq_buffer[t, :, lanes(h)], table_ref, 1))
 
 
 def gate_kernel(counts, weight_ref, input_ref, g_ref, out_ref, gate_ref):
@@ -198,7 +205,8 @@
 
 
 def probabilities_kernel(groups, counts, kqv_ref, *refs):
-    g_refs, outs, (ds_ref, delta_ref, g_ref, sum_ref) = refs[:groups], refs[groups:2 * groups], refs[2 * groups:]
+    g_refs, (dv_ref, ds_ref, delta_ref, g_ref, sum_ref) = refs[:groups], refs[groups:]
+    total = ds_ref.shape[2]
     cap, wide = g_refs[0].shape
     for i in range(groups):
         g_ref[block_of(groups - 1 - i, cap), :] = g_refs[i][...]
@@ -222,12 +230,28 @@
             p16 = p.astype(BF16)
             ds_ref[c, i, :upto, :] = (p16.astype(F32) * (dp - delta) * SCALE).astype(BF16)
             sum_ref[:upto, :] += dot(p16, g, ((1,), (0,)))
-        for m in range(groups):
-            outs[m][:, lanes(c)] = sum_ref[block_of(m, cap), :].astype(BF16)
+        dv_ref[:total, lanes(c)] = sum_ref[...].astype(BF16)
+    extra = dv_ref.shape[0] - total
+    line = lax.broadcasted_iota(jnp.int32, (extra, cap), 0)
+    rows = jnp.zeros((extra, cap), F32)
+    for i in range(groups):
+        delta = delta_ref[i][0:1, :]
+        coarse = delta.astype(BF16).astype(F32)
+        rows = jnp.where(line == 2 * i, coarse, jnp.where(line == 2 * i + 1, delta - coarse, rows))
+    for c in range(wide // HEAD_DIM):
+        dv_ref[total:, lanes(c)] = rows.astype(BF16)
+
+
+def part_values_kernel(groups, counts, dv_ref, dv_in_ref, *outs):
+    cap = outs[0].shape[1]
+    for m in range(groups):
+        block = block_of(m, cap)
+        outs[m][0] = dv_ref[block, :]
+        outs[m][1] = dv_in_ref[block, :]
 
 
 def grad_keys_kernel(groups, counts, kqv_ref, ds_ref, *refs):
-    deltas, outs, sum_ref = refs[:-groups - 1], refs[-groups - 1:-1], refs[-1]
+    outs, sum_ref = refs[:groups], refs[groups]
     heads, _, total, cap = ds_ref.shape
     for c in range(heads):
         sum_ref[...] = jnp.zeros_like(sum_ref)
@@ -235,19 +259,10 @@
             upto = (i + 1) * cap
             sum_ref[:upto, :] += dot(ds_ref[c, i, :upto, :], kqv_ref[1, i * cap:upto, lanes(c)], ((1,), (0,)))
         for m in range(groups):
-            outs[m][0:cap, lanes(c)] = sum_ref[block_of(m, cap), :].astype(BF16)
-    line = lax.broadcasted_iota(jnp.int32, (8, cap), 0)
-    for m in range(groups):
-        group = own_place(counts)[1] ^ m
-        delta = sum(ref[group] for ref in deltas)
-        coarse = delta.astype(BF16).astype(F32)
-        rows = jnp.where(line == 0, coarse, jnp.where(line == 1, delta - coarse, 0.0))
-        rows = jnp.concatenate([rows, jnp.zeros_like(rows)], axis=0).astype(BF16)
-        for c in range(heads):
-            outs[m][cap:, lanes(c)] = rows
-
-
-def grad_queries_kernel(groups, counts, kqv_ref, ds_ref, *refs):
+            outs[m][:, lanes(c)] = sum_ref[block_of(m, cap), :].astype(BF16)
+
+
+def grad_queries_kernel(groups, counts, kqv_ref, ds_ref, dv_ref, dv_in_ref, *refs):
     outs, sum_ref = refs[:groups], refs[groups]
     heads, _, total, cap = ds_ref.shape
     for c in range(heads):
@@ -255,31 +270,35 @@
             upto = (i + 1) * cap
             sum_ref[i * cap:upto, :] = dot(ds_ref[c, i, :upto, :], kqv_ref[0, :upto, lanes(c)], ((0,), (0,)))
         for m in range(groups):
-            outs[m][:, lanes(c)] = sum_ref[block_of(m, cap), :].astype(BF16)
-
-
-def unpack_kernel(groups, turned, counts, table_ref, *refs):
-    ins, own_ref, send_ref, token_ref = refs[:groups], refs[groups], refs[groups + 1], refs[groups + 2]
+            outs[m][0:cap, lanes(c)] = sum_ref[block_of(m, cap), :].astype(BF16)
+    both = dv_ref[total:, 0:HEAD_DIM].astype(F32) + dv_in_ref[total:, 0:HEAD_DIM].astype(F32)
+    line = lax.broadcasted_iota(jnp.int32, both.shape, 0)
+    out_line = lax.broadcasted_iota(jnp.int32, (16, cap), 0)
+    for m in range(groups):
+        group = own_place(counts)[1] ^ m
+        delta = jnp.sum(jnp.where((line >> 1) == group, both, 0.0), axis=0, keepdims=True)
+        coarse = delta.astype(BF16).astype(F32)
+        rows = jnp.where(out_line == 0, coarse, jnp.where(out_line == 1, delta - coarse, 0.0)).astype(BF16)
+        for c in range(heads):
+            outs[m][cap:, lanes(c)] = rows
+
+
+def unpack_kernel(groups, counts, table_ref, *refs):
+    ins, own_ref, send_ref, delta_ref = refs[:groups], refs[groups], refs[groups + 1], refs[groups + 2]
     cap = own_ref.shape[0]
     wide = ins[0].shape[1]
     heads = wide // HEAD_DIM
     own_hot, in_hot = places(counts, cap)
-    for i in range(groups):
+    delta = jnp.zeros((16, HEAD_DIM), F32)
+    for i in range(groups):
+        if ins[0].shape[0] > cap:
+            delta += ins[i][cap:, 0:HEAD_DIM].astype(F32)
         group = own_place(counts)[1] ^ (groups - 1 - i)
         send_ref[:, lanes(group, wide)] = taken(in_hot, ins[i][0:cap, :])
         for c in range(heads):
             own = dot(own_hot, ins[i][0:cap, lanes(c)], ((0,), (0,)))
-            own_ref[:, lanes(group * heads + c)] = rotated(own, table_ref, -1) if turned else own.astype(BF16)
-    token_ref[...] = jnp.zeros_like(token_ref)
-
-
-def delta_kernel(*refs):
-    ins, out_ref = refs[:-1], refs[-1]
-    rows = ins[0].shape[0]
-    total = ins[0][rows - 16:, 0:HEAD_DIM].astype(F32)
-    for ref in ins[1:]:
-        total += ref[rows - 16:, 0:HEAD_DIM].astype(F32)
-    out_ref[...] = jnp.broadcast_to(total[0:1, :] + total[1:2, :], out_ref.shape)
+            own_ref[:, lanes(group * heads + c)] = rotated(own, table_ref, -1)
+    delta_ref[...] = jnp.broadcast_to(delta[0:1, :] + delta[1:2, :], delta_ref.shape)
 
 
 def router_kernel(counts, gate_ref, input_ref, *refs):
@@ -298,15 +317,24 @@
     out_ref[...] = jnp.sum(in_ref[...], axis=0, keepdims=True)
 
 
-def place_kernel(turned, counts, table_ref, own_ref, in_ref, out_ref, token_ref):
+def place_values_kernel(groups, counts, *refs):
+    ins, out_ref, token_ref = refs[:groups], refs[groups], refs[groups + 1]
+    cap, wide = ins[0].shape[1:]
+    parity, group, _ = own_place(counts)
+    own_hot, _ = places(counts, cap)
+    token_ref[...] = jnp.zeros_like(token_ref)
+    for i in range(groups):
+        for side in range(2):
+            block = (parity ^ side) * groups + (group ^ (groups - 1 - i))
+            out_ref[:, lanes(block, wide)] = taken(own_hot, ins[i][side])
+
+
+def place_kernel(counts, table_ref, own_ref, in_ref, out_ref, token_ref):
     half = own_ref.shape[1]
     heads = half // HEAD_DIM
     parity = own_place(counts)[0]
     out_ref[:, lanes(parity, half)] = own_ref[...]
     token_ref[...] = jnp.zeros_like(token_ref)
-    if not turned:
-        out_ref[:, lanes(1 - parity, half)] = in_ref[...]
-        return
     for h in range(heads):
         out_ref[:, lanes((1 - parity) * heads + h)] = rotated(in_ref[:, lanes(h)], table_ref, -1)
 
@@ -326,14 +354,17 @@
 
     *values, sent, table = pl.pallas_call(
         kernel(front_kernel),
-        in_specs=[SMEM, VMEM] + [ANY] * 3,
+        in_specs=[SMEM] + [HBM] * 4,
         out_specs=[VMEM] * (groups + 2),
         out_shape=[jax.ShapeDtypeStruct((2, cap, wide), BF16)] * groups
         + [jax.ShapeDtypeStruct((2, cap, half), BF16), jax.ShapeDtypeStruct((2, cap, HEAD_DIM), F32)],
         scratch_shapes=[
-            pltpu.VMEM((cap, width), BF16), pltpu.VMEM((2, cap, half), BF16), pltpu.SemaphoreType.DMA((3,)),
+            pltpu.VMEM((1, cap), jnp.int32),
+            pltpu.VMEM((cap, width), BF16),
+            pltpu.VMEM((2, cap, half), BF16),
+            pltpu.SemaphoreType.DMA((5,)),
         ],
-        compiler_params=pltpu.CompilerParams(vmem_limit_bytes=FRONT * 1024 * 1024),
+        compiler_params=pltpu.CompilerParams(vmem_limit_bytes=63 * 1024 * 1024),
         cost_estimate=cost("front"),
         name="front",
     )(counts, picked_pos, value_own, key_own, query_own)
@@ -365,56 +396,58 @@
     )[0]
 
     piece = ((cap, wide), BF16)
-    *pieces, ds, delta = call(
+    extra = 16 * ((2 * groups + 15) // 16)
+    dv, ds = call(
         kernel(probabilities_kernel),
         "probabilities",
-        [piece] * groups + [((heads, groups, total, cap), BF16), ((groups, 8, cap), F32)],
+        [((total + extra, wide), BF16), ((heads, groups, total, cap), BF16)],
         counts, kqv, *gated,
-        scratch_shapes=[pltpu.VMEM((total, wide), BF16), pltpu.VMEM((total, HEAD_DIM), F32)],
-    )
-    v_pieces = spread(pieces)
+        scratch_shapes=[
+            pltpu.VMEM((groups, 8, cap), F32), pltpu.VMEM((total, wide), BF16), pltpu.VMEM((total, HEAD_DIM), F32),
+        ],
+    )
+    dv_in = swapped(dv)
     k_pieces = spread(call(
         kernel(grad_keys_kernel),
         "grad_keys",
-        [((cap + 16, wide), BF16)] * groups,
-        counts, kqv, ds, delta,
+        [piece] * groups,
+        counts, kqv, ds,
         scratch_shapes=[pltpu.VMEM((total, HEAD_DIM), F32)],
     ))
 
-    def unpacked(name, turned, pieces, wait=()):
+    def unpacked(name, pieces, wait):
         shapes = [((cap, half), BF16)] * 2 + [((8, cap), F32)]
-        return call(functools.partial(unpack_kernel, groups, turned), name, shapes, counts, table, *pieces, wait=wait)
-
-    def placed(name, turned, own, other, wait):
-        body = functools.partial(place_kernel, turned)
-        return call(body, name, [((cap, width), BF16), ((8, HEAD_DIM), F32)], counts, table, own, other, wait=wait)
-
-    v_own, sent, token = unpacked("unpack_values", False, v_pieces, k_pieces[-1:])
-    v_in = swapped(sent)
-    grad_v, token_v = placed("place_values", False, v_own, v_in, [])
+        return call(kernel(unpack_kernel), name, shapes, counts, table, *pieces, wait=wait)
+
+    def placed(name, own, other, wait):
+        return call(place_kernel, name, [((cap, width), BF16), ((8, HEAD_DIM), F32)], counts, table, own, other, wait=wait)
+
     q_pieces = spread(call(
         kernel(grad_queries_kernel),
         "grad_queries",
-        [piece] * groups,
-        counts, kqv, ds,
-        wait=[token],
+        [((cap + 16, wide), BF16)] * groups,
+        counts, kqv, ds, dv, dv_in,
+        wait=k_pieces[-1:],
         scratch_shapes=[pltpu.VMEM((total, HEAD_DIM), F32)],
     ))
-    (delta,) = call(delta_kernel, "delta", [((8, cap), F32)], *k_pieces)
-    delta_in = swapped(delta)
-    k_own, sent, token_k = unpacked("unpack_keys", True, k_pieces, q_pieces[:1])
+    parts = call(
+        kernel(part_values_kernel), "part_values", [((2, cap, wide), BF16)] * groups, counts, dv, dv_in, wait=q_pieces[-1:]
+    )
+    v_pieces = spread(parts)
+    k_own, sent, token_k = unpacked("unpack_keys", k_pieces, parts[:1])
     k_in = swapped(sent)
+    q_own, sent, delta = unpacked("unpack_queries", q_pieces, [token_k])
+    q_in = swapped(sent)
     (part,) = call(
-        router_kernel, "router", [((input_own.shape[1] // HEAD_DIM, HEAD_DIM), F32)], counts, gate, input_own, delta, delta_in,
-        wait=[token_k],
-    )
-    q_own, sent, _ = unpacked("unpack_queries", True, q_pieces, [part])
-    q_in = swapped(sent)
-    grad_k, token_k = placed("place_keys", True, k_own, k_in, [token_v])
-    grad_q, _ = placed("place_queries", True, q_own, q_in, [token_k])
+        router_kernel, "router", [((input_own.shape[1] // HEAD_DIM, HEAD_DIM), F32)], counts, gate, input_own, delta
+    )
+    shape = [((cap, width), BF16), ((8, HEAD_DIM), F32)]
+    grad_v, token_v = call(kernel(place_values_kernel), "place_values", shape, counts, *v_pieces)
+    grad_k, token_k = placed("place_keys", k_own, k_in, [token_v])
+    grad_q, token_q = placed("place_queries", q_own, q_in, [token_k])
     devices = seq_size * lax.axis_size("fsdp")
     shares = lax.all_to_all(part.reshape(devices, -1), ("seq", "fsdp"), 0, 0, tiled=True)
-    grad_router = call(total_kernel, "total", [((1, shares.shape[1]), F32)], shares, wait=[token_k])[0][0]
+    grad_router = call(total_kernel, "total", [((1, shares.shape[1]), F32)], shares, wait=[token_q])[0][0]
     return grad_q[None], grad_k[None], grad_v[None], grad_router
 
 

time: 80.7 us -> 79.3 us (0.983)
  Pallas kernels: 13.1 us -> 11.9 us
    all_to_all x1, waiting for transfers between devices: 5.01 us -> 3.83 us  [per_device(): lax.all_to_all(part.reshape(devices, -1), ('seq', 'fsdp'), 0, 0, tiled=True)]
    ppermute x18, waiting for transfers between devices: 8.35 us -> 9.32 us  [spread(): lax.ppermute(pieces[m], 'seq', [(i, i ^ 2 * m) for i in range(size)])]
    pallas_call x17 -> x16, Pallas kernels: 9.57 us -> 8.99 us  [call(): pl.pallas_call(body, in_specs=[SMEM if a.shape == (1, 1) else VMEM for a...]
    ppermute x7 -> x6, starting transfers between devices: 7.89 us -> 7.59 us  [swapped(): lax.ppermute(array, 'seq', [(i, i ^ 1) for i in range(lax.axis_size('seq'...]
    ppermute x7 -> x6, waiting for transfers between devices: 1.85 us -> 1.85 us  [swapped(): lax.ppermute(array, 'seq', [(i, i ^ 1) for i in range(lax.axis_size('seq'...]
  transfers between devices with their start and end apart: 26 -> 25, of which waited for: 11 -> 11; matrix products, arithmetic and copies ran while one was open for 0% -> 0% of each run, Pallas kernels for 9% -> 9%
where the time goes in v4:
time: 79.3 us; the launch traced here: 79.1 us
  starting transfers between devices  44.3 us (56%)
  waiting for transfers between devices  15 us (19%)
  Pallas kernels  11.9 us (15%)
  blocking collectives  5.15 us (6%)
  between operations  1.48 us (2%)
  local copies, waits for them, and re-layouts  1.26 us (2%)
    ppermute x18, starting transfers between devices, spread(): lax.ppermute(pieces[m], 'seq', [(i, i ^ 2 * m) for i in range(size)])  32.1 us
    ppermute x18, waiting for transfers between devices, spread(): lax.ppermute(pieces[m], 'seq', [(i, i ^ 2 * m) for i in range(size)])  9.32 us
    pallas_call x16, Pallas kernels, call(): pl.pallas_call(body, in_specs=[SMEM if a.shape == (1, 1) else VMEM for a...  8.99 us
    ppermute x6, starting transfers between devices, swapped(): lax.ppermute(array, 'seq', [(i, i ^ 1) for i in range(lax.axis_size('seq'...  7.59 us
    all_gather x1, blocking collectives, per_device(): router_full = lax.all_gather(router_weight, 'fsdp', axis=0, tiled=True)  5.15 us
    all_to_all x1, starting transfers between devices, per_device(): lax.all_to_all(part.reshape(devices, -1), ('seq', 'fsdp'), 0, 0, tiled=True)  4.67 us
    all_to_all x1, waiting for transfers between devices, per_device(): lax.all_to_all(part.reshape(devices, -1), ('seq', 'fsdp'), 0, 0, tiled=True)  3.83 us
    pallas_call x1, Pallas kernels, per_device(): pl.pallas_call(kernel(front_kernel), in_specs=[SMEM] + [HBM] * 4, out_spe...  2.9 us
  transfers between devices with their start and end apart: 25, of which 11 were waited for; matrix products, arithmetic and copies ran while one was open for 0% of the time, Pallas kernels for 9%

profile of v4, /device:TPU:0, one launch (start us, length us, event | category | flops | bytes accessed | tf_op | source)
XLA Modules:
  0.0 79.1 jit_solution(5386628457743047670)
XLA Ops:
  1.3 2.9 %front.1 = (bf16[2,128,256]{2,1,0:T(8,128)(2,1)}, bf16[2,128,256]{2,1,0:T(8,128)(2,1)}, bf16[2,128,256]{2,1,0:T(8,128)(2,1)}, bf16[2,128,256]{2,1,0:T(8,128)(2,1...) custom-call(s32[1,1]{1,0:T(1,128)S(6)} %copy.13.counts.refs_0_, s32[1,128]{1,0:T(1,128)} %pos_ref.1, ...), custom_call_target="tpu_custom_call" | custom-call | flops 1000000 | bytes 65536 | tf_op jit(solution)/shard_map/front/pallas_call | solution.py:355
  4.2 3.0 %collective-permute-start.3 = (bf16[2,128,1024]{2,1,0:T(8,128)(2,1)}, bf16[2,128,1024]{2,1,0:T(8,128)(2,1)S(1)}, u32[]{:S(2)}, u32[]{:S(2)}) collective-permute-start(bf16[2,128,1024]{2,1,0:T(8,128)(2,1)} %get-tuple-element.53), channel_id=1, source_target_pairs={{0,4},{4,0},{8,12},{12,8},{16,20},{20,16},{24,28},{28,24},{1,5},{5... | collective-permute-start | bytes 1572872 | tf_op jit(solution)/shard_map/ppermute | solution.py:29
  7.2 3.6 %collective-permute-start = (bf16[2,128,256]{2,1,0:T(8,128)(2,1)}, bf16[2,128,256]{2,1,0:T(8,128)(2,1)S(1)}, u32[]{:S(2)}, u32[]{:S(2)}) collective-permute-start(bf16[2,128,256]{2,1,0:T(8,128)(2,1)} %get-tuple-element.49), channel_id=1, source_target_pairs={{0,24},{4,28},{8,16},{12,20},{16,8},{20,12},{24,0},{28,4},{1,25},{... | collective-permute-start | bytes 393224 | tf_op jit(solution)/shard_map/ppermute | solution.py:35
  11.6 5.2 %all_gather.3 = bf16[4096]{0:T(1024)(128)(2,1)S(1)} all-gather(bf16[1024]{0:T(1024)(128)(2,1)S(1)} %copy-done.7), channel_id=1, replica_groups=mesh['seq'=8,'fsdp'=4] {'fsdp'}, dimensions={0}, use_global_device_ids=true | all-gather | bytes 10240 | tf_op jit(solution)/shard_map/all_gather | solution.py:373
  16.8 1.2 %copy-done.5 = bf16[1,128,4096]{2,1,0:T(8,128)(2,1)S(1)} copy-done((bf16[1,128,4096]{2,1,0:T(8,128)(2,1)S(1)}, bf16[1,128,4096]{2,1,0:T(8,128)(2,1)}, u32[]{:S(2)}) %copy-start.5) | copy-done | bytes 1048600
  19.9 1.9 %collective-permute-done.1.refs_2_ = bf16[2,128,256]{2,1,0:T(8,128)(2,1)S(1)} collective-permute-done((bf16[2,128,256]{2,1,0:T(8,128)(2,1)}, bf16[2,128,256]{2,1,0:T(8,128)(2,1)S(1)}, u32[]{:S(2)}, u32[]{:S(2)}) %collective-permute-start.1) | collective-permute-done | bytes 131104 | tf_op jit(solution)/shard_map/ppermute | solution.py:35
  22.5 3.3 %collective-permute-start.5 = (bf16[2,128,256]{2,1,0:T(8,128)(2,1)S(1)}, bf16[2,128,256]{2,1,0:T(8,128)(2,1)S(1)}, u32[]{:S(2)}, u32[]{:S(2)}) collective-permute-start(bf16[2,128,256]{2,1,0:T(8,128)(2,1)S(1)} %get-tuple-element.57), channel_id=1, source_target_pairs={{0,24},{4,28},{8,16},{12,20},{16,8},{20,12},{24,0},{28,4},{1,25},{... | collective-permute-start | bytes 393224 | tf_op jit(solution)/shard_map/ppermute | solution.py:35
  28.0 3.7 %collective-permute-start.9 = (bf16[128,256]{1,0:T(8,128)(2,1)S(1)}, bf16[128,256]{1,0:T(8,128)(2,1)S(1)}, u32[]{:S(2)}, u32[]{:S(2)}) collective-permute-start(bf16[128,256]{1,0:T(8,128)(2,1)S(1)} %get-tuple-element.62), channel_id=1, source_target_pairs={{0,24},{4,28},{8,16},{12,20},{16,8},{20,12},{24,0},{28,4},{1,25},{... | collective-permute-start | bytes 196616 | tf_op jit(solution)/shard_map/ppermute | solution.py:35
  31.7 6.3 %collective-permute-start.10 = (bf16[128,256]{1,0:T(8,128)(2,1)S(1)}, bf16[128,256]{1,0:T(8,128)(2,1)S(1)}, u32[]{:S(2)}, u32[]{:S(2)}) collective-permute-start(bf16[128,256]{1,0:T(8,128)(2,1)S(1)} %get-tuple-element.63), channel_id=1, source_target_pairs={{0,16},{4,20},{8,24},{12,28},{16,0},{20,4},{24,8},{28,12},{1,17},{... | collective-permute-start | bytes 196616 | tf_op jit(solution)/shard_map/ppermute | solution.py:35
  38.0 1.4 %collective-permute-done.6.refs_4_ = bf16[2,128,256]{2,1,0:T(8,128)(2,1)S(1)} collective-permute-done((bf16[2,128,256]{2,1,0:T(8,128)(2,1)S(1)}, bf16[2,128,256]{2,1,0:T(8,128)(2,1)S(1)}, u32[]{:S(2)}, u32[]{:S(2)}) %collective-permute-start.6) | collective-permute-done | bytes 131104 | tf_op jit(solution)/shard_map/ppermute | solution.py:35
  39.5 1.4 %collective-permute-done.10.refs_3_ = bf16[128,256]{1,0:T(8,128)(2,1)S(1)} collective-permute-done((bf16[128,256]{1,0:T(8,128)(2,1)S(1)}, bf16[128,256]{1,0:T(8,128)(2,1)S(1)}, u32[]{:S(2)}, u32[]{:S(2)}) %collective-permute-start.10) | collective-permute-done | bytes 65568 | tf_op jit(solution)/shard_map/ppermute | solution.py:35
  40.9 2.8 %collective-permute-done.11.refs_4_ = bf16[128,256]{1,0:T(8,128)(2,1)S(1)} collective-permute-done((bf16[128,256]{1,0:T(8,128)(2,1)S(1)}, bf16[128,256]{1,0:T(8,128)(2,1)S(1)}, u32[]{:S(2)}, u32[]{:S(2)}) %collective-permute-start.11) | collective-permute-done | bytes 65568 | tf_op jit(solution)/shard_map/ppermute | solution.py:35
  43.7 1.3 %probabilities.1 = (bf16[528,256]{1,0:T(8,128)(2,1)S(1)}, bf16[2,4,512,128]{3,2,1,0:T(8,128)(2,1)S(1)}) custom-call(s32[1,1]{1,0:T(1,128)S(6)} %copy.13.counts.refs_0_, bf16[3,512,256]{2,1,0:T(8,128)(2,1)S(1)} %gather.1.refs_1_, bf16[128,256]{1,0:T(8,128)(2,1)S(1)} %collective-permute-done.9.refs_2_, bf16[128,256]{1,0:T(8,128)(2,1)S(1)} %collective-permute-done.10.refs_3_, ...), custom_call_target="tpu_custom_call" | custom-call | flops 1000000 | bytes 65536 | tf_op jit(solution)/shard_map/probabilities/pallas_call | solution.py:50
  46.5 2.5 %collective-permute-start.16 = (bf16[128,256]{1,0:T(8,128)(2,1)S(1)}, bf16[128,256]{1,0:T(8,128)(2,1)S(1)}, u32[]{:S(2)}, u32[]{:S(2)}) collective-permute-start(bf16[128,256]{1,0:T(8,128)(2,1)S(1)} %get-tuple-element.73), channel_id=1, source_target_pairs={{0,24},{4,28},{8,16},{12,20},{16,8},{20,12},{24,0},{28,4},{1,25},{... | collective-permute-start | bytes 196616 | tf_op jit(solution)/shard_map/ppermute | solution.py:35
  49.0 2.0 %collective-permute-start.18 = (bf16[128,256]{1,0:T(8,128)(2,1)S(1)}, bf16[128,256]{1,0:T(8,128)(2,1)S(1)}, u32[]{:S(2)}, u32[]{:S(2)}) collective-permute-start(bf16[128,256]{1,0:T(8,128)(2,1)S(1)} %get-tuple-element.75), channel_id=1, source_target_pairs={{0,8},{4,12},{8,0},{12,4},{16,24},{20,28},{24,16},{28,20},{1,9},{5... | collective-permute-start | bytes 196616 | tf_op jit(solution)/shard_map/ppermute | solution.py:35
  51.9 2.6 %collective-permute-start.13 = (bf16[144,256]{1,0:T(8,128)(2,1)S(1)}, bf16[144,256]{1,0:T(8,128)(2,1)S(1)}, u32[]{:S(2)}, u32[]{:S(2)}) collective-permute-start(bf16[144,256]{1,0:T(8,128)(2,1)S(1)} %get-tuple-element.69), channel_id=1, source_target_pairs={{0,24},{4,28},{8,16},{12,20},{16,8},{20,12},{24,0},{28,4},{1,25},{... | collective-permute-start | bytes 221192 | tf_op jit(solution)/shard_map/ppermute | solution.py:35
  54.5 1.9 %collective-permute-start.15 = (bf16[144,256]{1,0:T(8,128)(2,1)S(1)}, bf16[144,256]{1,0:T(8,128)(2,1)S(1)}, u32[]{:S(2)}, u32[]{:S(2)}) collective-permute-start(bf16[144,256]{1,0:T(8,128)(2,1)S(1)} %get-tuple-element.71), channel_id=1, source_target_pairs={{0,8},{4,12},{8,0},{12,4},{16,24},{20,28},{24,16},{28,20},{1,9},{5... | collective-permute-start | bytes 221192 | tf_op jit(solution)/shard_map/ppermute | solution.py:35
  56.9 1.2 %collective-permute-start.20 = (bf16[128,1024]{1,0:T(8,128)(2,1)S(1)}, bf16[128,1024]{1,0:T(8,128)(2,1)S(1)}, u32[]{:S(2)}, u32[]{:S(2)}) collective-permute-start(bf16[128,1024]{1,0:T(8,128)(2,1)S(1)} %get-tuple-element.81), channel_id=1, source_target_pairs={{0,4},{4,0},{8,12},{12,8},{16,20},{20,16},{24,28},{28,24},{1,5},{5... | collective-permute-start | bytes 786440 | tf_op jit(solution)/shard_map/ppermute | solution.py:29
  58.2 1.6 %collective-permute-done.14.refs_3_ = bf16[144,256]{1,0:T(8,128)(2,1)S(1)} collective-permute-done((bf16[144,256]{1,0:T(8,128)(2,1)S(1)}, bf16[144,256]{1,0:T(8,128)(2,1)S(1)}, u32[]{:S(2)}, u32[]{:S(2)}) %collective-permute-start.14) | collective-permute-done | bytes 73760 | tf_op jit(solution)/shard_map/ppermute | solution.py:35
  60.2 1.3 %collective-permute-start.19 = (bf16[128,1024]{1,0:T(8,128)(2,1)S(1)}, bf16[128,1024]{1,0:T(8,128)(2,1)S(1)}, u32[]{:S(2)}, u32[]{:S(2)}) collective-permute-start(bf16[128,1024]{1,0:T(8,128)(2,1)S(1)} %get-tuple-element.79), channel_id=1, source_target_pairs={{0,4},{4,0},{8,12},{12,8},{16,20},{20,16},{24,28},{28,24},{1,5},{5... | collective-permute-start | bytes 786440 | tf_op jit(solution)/shard_map/ppermute | solution.py:29
  61.5 2.8 %collective-permute-start.21 = (bf16[2,128,256]{2,1,0:T(8,128)(2,1)S(1)}, bf16[2,128,256]{2,1,0:T(8,128)(2,1)S(1)}, u32[]{:S(2)}, u32[]{:S(2)}) collective-permute-start(bf16[2,128,256]{2,1,0:T(8,128)(2,1)S(1)} %get-tuple-element.82), channel_id=1, source_target_pairs={{0,24},{4,28},{8,16},{12,20},{16,8},{20,12},{24,0},{28,4},{1,25},{... | collective-permute-start | bytes 393224 | tf_op jit(solution)/shard_map/ppermute | solution.py:35
  64.2 1.6 %collective-permute-start.23 = (bf16[2,128,256]{2,1,0:T(8,128)(2,1)S(1)}, bf16[2,128,256]{2,1,0:T(8,128)(2,1)S(1)}, u32[]{:S(2)}, u32[]{:S(2)}) collective-permute-start(bf16[2,128,256]{2,1,0:T(8,128)(2,1)S(1)} %get-tuple-element.84), channel_id=1, source_target_pairs={{0,8},{4,12},{8,0},{12,4},{16,24},{20,28},{24,16},{28,20},{1,9},{5... | collective-permute-start | bytes 393224 | tf_op jit(solution)/shard_map/ppermute | solution.py:35
  66.8 4.7 %all-to-all-start = ((f32[32,1,128]{2,1,0:T(1,128)}), f32[32,1,128]{2,1,0:T(1,128)S(1)}, u32[]{:S(2)}, u32[]{:S(2)}) async-start(f32[32,1,128]{2,1,0:T(1,128)} %bitcast.9), calls=%async_computation | async-start | bytes 32768 | tf_op jit(solution)/shard_map/all_to_all | solution.py:449
  74.8 3.8 %all-to-all-done = f32[32,1,128]{2,1,0:T(1,128)S(1)} async-done(((f32[32,1,128]{2,1,0:T(1,128)}), f32[32,1,128]{2,1,0:T(1,128)S(1)}, u32[]{:S(2)}, u32[]{:S(2)}) %all-to-all-start) | async-done | bytes 16416 | tf_op jit(solution)/shard_map/all_to_all | solution.py:449
  (61 shorter events, 13.9 us)
Async XLA Ops:
  4.2 15.2 %collective-permute-start.3 = (bf16[2,128,1024]{2,1,0:T(8,128)(2,1)}, bf16[2,128,1024]{2,1,0:T(8,128)(2,1)S(1)}, u32[]{:S(2)}, u32[]{:S(2)}) collective-permute-start(bf16[2,128,1024]{2,1,0:T(8,128)(2,1)} %get-tuple-element.53), channel_id=1, source_target_pairs={{0,4},{4,0},{8,12},{12,8},{16,20},{20,16},{24,28},{28,24},{1,5},{5... | collective-permute-start | bytes 1572872 | tf_op jit(solution)/shard_map/ppermute | solution.py:29
  7.2 12.7 %collective-permute-start = (bf16[2,128,256]{2,1,0:T(8,128)(2,1)}, bf16[2,128,256]{2,1,0:T(8,128)(2,1)S(1)}, u32[]{:S(2)}, u32[]{:S(2)}) collective-permute-start(bf16[2,128,256]{2,1,0:T(8,128)(2,1)} %get-tuple-element.49), channel_id=1, source_target_pairs={{0,24},{4,28},{8,16},{12,20},{16,8},{20,12},{24,0},{28,4},{1,25},{... | collective-permute-start | bytes 393224 | tf_op jit(solution)/shard_map/ppermute | solution.py:35
  10.8 11.0 %collective-permute-start.1 = (bf16[2,128,256]{2,1,0:T(8,128)(2,1)}, bf16[2,128,256]{2,1,0:T(8,128)(2,1)S(1)}, u32[]{:S(2)}, u32[]{:S(2)}) collective-permute-start(bf16[2,128,256]{2,1,0:T(8,128)(2,1)} %get-tuple-element.50), channel_id=1, source_target_pairs={{0,16},{4,20},{8,24},{12,28},{16,0},{20,4},{24,8},{28,12},{1,17},{... | collective-permute-start | bytes 393224 | tf_op jit(solution)/shard_map/ppermute | solution.py:35
  10.8 11.0 %collective-permute-start.2 = (bf16[2,128,256]{2,1,0:T(8,128)(2,1)}, bf16[2,128,256]{2,1,0:T(8,128)(2,1)S(1)}, u32[]{:S(2)}, u32[]{:S(2)}) collective-permute-start(bf16[2,128,256]{2,1,0:T(8,128)(2,1)} %get-tuple-element.51), channel_id=1, source_target_pairs={{0,8},{4,12},{8,0},{12,4},{16,24},{20,28},{24,16},{28,20},{1,9},{5... | collective-permute-start | bytes 393224 | tf_op jit(solution)/shard_map/ppermute | solution.py:35
  18.6 9.2 %collective-permute-start.8 = (bf16[128,1024]{1,0:T(8,128)(2,1)S(1)}, bf16[128,1024]{1,0:T(8,128)(2,1)S(1)}, u32[]{:S(2)}, u32[]{:S(2)}) collective-permute-start(bf16[128,1024]{1,0:T(8,128)(2,1)S(1)} %get-tuple-element.61), channel_id=1, source_target_pairs={{0,4},{4,0},{8,12},{12,8},{16,20},{20,16},{24,28},{28,24},{1,5},{5... | collective-permute-start | bytes 786440 | tf_op jit(solution)/shard_map/ppermute | solution.py:29
  21.9 17.5 %collective-permute-start.4 = (bf16[512,256]{1,0:T(8,128)(2,1)S(1)}, bf16[512,256]{1,0:T(8,128)(2,1)S(1)}, u32[]{:S(2)}, u32[]{:S(2)}) collective-permute-start(bf16[512,256]{1,0:T(8,128)(2,1)S(1)} %get-tuple-element.56), channel_id=1, source_target_pairs={{0,4},{4,0},{8,12},{12,8},{16,20},{20,16},{24,28},{28,24},{1,5},{5... | collective-permute-start | bytes 786440 | tf_op jit(solution)/shard_map/ppermute | solution.py:29
  22.5 9.2 %collective-permute-start.5 = (bf16[2,128,256]{2,1,0:T(8,128)(2,1)S(1)}, bf16[2,128,256]{2,1,0:T(8,128)(2,1)S(1)}, u32[]{:S(2)}, u32[]{:S(2)}) collective-permute-start(bf16[2,128,256]{2,1,0:T(8,128)(2,1)S(1)} %get-tuple-element.57), channel_id=1, source_target_pairs={{0,24},{4,28},{8,16},{12,20},{16,8},{20,12},{24,0},{28,4},{1,25},{... | collective-permute-start | bytes 393224 | tf_op jit(solution)/shard_map/ppermute | solution.py:35
  25.7 13.6 %collective-permute-start.6 = (bf16[2,128,256]{2,1,0:T(8,128)(2,1)S(1)}, bf16[2,128,256]{2,1,0:T(8,128)(2,1)S(1)}, u32[]{:S(2)}, u32[]{:S(2)}) collective-permute-start(bf16[2,128,256]{2,1,0:T(8,128)(2,1)S(1)} %get-tuple-element.58), channel_id=1, source_target_pairs={{0,16},{4,20},{8,24},{12,28},{16,0},{20,4},{24,8},{28,12},{1,17},{... | collective-permute-start | bytes 393224 | tf_op jit(solution)/shard_map/ppermute | solution.py:35
  25.7 13.7 %collective-permute-start.7 = (bf16[2,128,256]{2,1,0:T(8,128)(2,1)S(1)}, bf16[2,128,256]{2,1,0:T(8,128)(2,1)S(1)}, u32[]{:S(2)}, u32[]{:S(2)}) collective-permute-start(bf16[2,128,256]{2,1,0:T(8,128)(2,1)S(1)} %get-tuple-element.59), channel_id=1, source_target_pairs={{0,8},{4,12},{8,0},{12,4},{16,24},{20,28},{24,16},{28,20},{1,9},{5... | collective-permute-start | bytes 393224 | tf_op jit(solution)/shard_map/ppermute | solution.py:35
  28.0 11.5 %collective-permute-start.9 = (bf16[128,256]{1,0:T(8,128)(2,1)S(1)}, bf16[128,256]{1,0:T(8,128)(2,1)S(1)}, u32[]{:S(2)}, u32[]{:S(2)}) collective-permute-start(bf16[128,256]{1,0:T(8,128)(2,1)S(1)} %get-tuple-element.62), channel_id=1, source_target_pairs={{0,24},{4,28},{8,16},{12,20},{16,8},{20,12},{24,0},{28,4},{1,25},{... | collective-permute-start | bytes 196616 | tf_op jit(solution)/shard_map/ppermute | solution.py:35
  31.7 9.2 %collective-permute-start.10 = (bf16[128,256]{1,0:T(8,128)(2,1)S(1)}, bf16[128,256]{1,0:T(8,128)(2,1)S(1)}, u32[]{:S(2)}, u32[]{:S(2)}) collective-permute-start(bf16[128,256]{1,0:T(8,128)(2,1)S(1)} %get-tuple-element.63), channel_id=1, source_target_pairs={{0,16},{4,20},{8,24},{12,28},{16,0},{20,4},{24,8},{28,12},{1,17},{... | collective-permute-start | bytes 196616 | tf_op jit(solution)/shard_map/ppermute | solution.py:35
  45.0 6.5 %collective-permute-start.12 = (bf16[528,256]{1,0:T(8,128)(2,1)S(1)}, bf16[528,256]{1,0:T(8,128)(2,1)S(1)}, u32[]{:S(2)}, u32[]{:S(2)}) collective-permute-start(bf16[528,256]{1,0:T(8,128)(2,1)S(1)} %get-tuple-element.67.refs_3_.refs_1_), channel_id=1, source_target_pairs={{0,4},{4,0},{8,12},{12,8},{16,20},{20,16},{24,28},{28,24},{1,5},{5... | collective-permute-start | bytes 811016 | tf_op jit(solution)/shard_map/ppermute | solution.py:29
  46.5 8.0 %collective-permute-start.16 = (bf16[128,256]{1,0:T(8,128)(2,1)S(1)}, bf16[128,256]{1,0:T(8,128)(2,1)S(1)}, u32[]{:S(2)}, u32[]{:S(2)}) collective-permute-start(bf16[128,256]{1,0:T(8,128)(2,1)S(1)} %get-tuple-element.73), channel_id=1, source_target_pairs={{0,24},{4,28},{8,16},{12,20},{16,8},{20,12},{24,0},{28,4},{1,25},{... | collective-permute-start | bytes 196616 | tf_op jit(solution)/shard_map/ppermute | solution.py:35
  49.0 7.4 %collective-permute-start.17 = (bf16[128,256]{1,0:T(8,128)(2,1)S(1)}, bf16[128,256]{1,0:T(8,128)(2,1)S(1)}, u32[]{:S(2)}, u32[]{:S(2)}) collective-permute-start(bf16[128,256]{1,0:T(8,128)(2,1)S(1)} %get-tuple-element.74), channel_id=1, source_target_pairs={{0,16},{4,20},{8,24},{12,28},{16,0},{20,4},{24,8},{28,12},{1,17},{... | collective-permute-start | bytes 196616 | tf_op jit(solution)/shard_map/ppermute | solution.py:35
  49.0 7.4 %collective-permute-start.18 = (bf16[128,256]{1,0:T(8,128)(2,1)S(1)}, bf16[128,256]{1,0:T(8,128)(2,1)S(1)}, u32[]{:S(2)}, u32[]{:S(2)}) collective-permute-start(bf16[128,256]{1,0:T(8,128)(2,1)S(1)} %get-tuple-element.75), channel_id=1, source_target_pairs={{0,8},{4,12},{8,0},{12,4},{16,24},{20,28},{24,16},{28,20},{1,9},{5... | collective-permute-start | bytes 196616 | tf_op jit(solution)/shard_map/ppermute | solution.py:35
  51.9 6.2 %collective-permute-start.13 = (bf16[144,256]{1,0:T(8,128)(2,1)S(1)}, bf16[144,256]{1,0:T(8,128)(2,1)S(1)}, u32[]{:S(2)}, u32[]{:S(2)}) collective-permute-start(bf16[144,256]{1,0:T(8,128)(2,1)S(1)} %get-tuple-element.69), channel_id=1, source_target_pairs={{0,24},{4,28},{8,16},{12,20},{16,8},{20,12},{24,0},{28,4},{1,25},{... | collective-permute-start | bytes 221192 | tf_op jit(solution)/shard_map/ppermute | solution.py:35
  54.5 5.3 %collective-permute-start.14 = (bf16[144,256]{1,0:T(8,128)(2,1)S(1)}, bf16[144,256]{1,0:T(8,128)(2,1)S(1)}, u32[]{:S(2)}, u32[]{:S(2)}) collective-permute-start(bf16[144,256]{1,0:T(8,128)(2,1)S(1)} %get-tuple-element.70), channel_id=1, source_target_pairs={{0,16},{4,20},{8,24},{12,28},{16,0},{20,4},{24,8},{28,12},{1,17},{... | collective-permute-start | bytes 221192 | tf_op jit(solution)/shard_map/ppermute | solution.py:35
  54.5 5.2 %collective-permute-start.15 = (bf16[144,256]{1,0:T(8,128)(2,1)S(1)}, bf16[144,256]{1,0:T(8,128)(2,1)S(1)}, u32[]{:S(2)}, u32[]{:S(2)}) collective-permute-start(bf16[144,256]{1,0:T(8,128)(2,1)S(1)} %get-tuple-element.71), channel_id=1, source_target_pairs={{0,8},{4,12},{8,0},{12,4},{16,24},{20,28},{24,16},{28,20},{1,9},{5... | collective-permute-start | bytes 221192 | tf_op jit(solution)/shard_map/ppermute | solution.py:35
  56.9 15.9 %collective-permute-start.20 = (bf16[128,1024]{1,0:T(8,128)(2,1)S(1)}, bf16[128,1024]{1,0:T(8,128)(2,1)S(1)}, u32[]{:S(2)}, u32[]{:S(2)}) collective-permute-start(bf16[128,1024]{1,0:T(8,128)(2,1)S(1)} %get-tuple-element.81), channel_id=1, source_target_pairs={{0,4},{4,0},{8,12},{12,8},{16,20},{20,16},{24,28},{28,24},{1,5},{5... | collective-permute-start | bytes 786440 | tf_op jit(solution)/shard_map/ppermute | solution.py:29
  60.2 13.6 %collective-permute-start.19 = (bf16[128,1024]{1,0:T(8,128)(2,1)S(1)}, bf16[128,1024]{1,0:T(8,128)(2,1)S(1)}, u32[]{:S(2)}, u32[]{:S(2)}) collective-permute-start(bf16[128,1024]{1,0:T(8,128)(2,1)S(1)} %get-tuple-element.79), channel_id=1, source_target_pairs={{0,4},{4,0},{8,12},{12,8},{16,20},{20,16},{24,28},{28,24},{1,5},{5... | collective-permute-start | bytes 786440 | tf_op jit(solution)/shard_map/ppermute | solution.py:29
  61.5 10.0 %collective-permute-start.21 = (bf16[2,128,256]{2,1,0:T(8,128)(2,1)S(1)}, bf16[2,128,256]{2,1,0:T(8,128)(2,1)S(1)}, u32[]{:S(2)}, u32[]{:S(2)}) collective-permute-start(bf16[2,128,256]{2,1,0:T(8,128)(2,1)S(1)} %get-tuple-element.82), channel_id=1, source_target_pairs={{0,24},{4,28},{8,16},{12,20},{16,8},{20,12},{24,0},{28,4},{1,25},{... | collective-permute-start | bytes 393224 | tf_op jit(solution)/shard_map/ppermute | solution.py:35
  64.2 7.4 %collective-permute-start.22 = (bf16[2,128,256]{2,1,0:T(8,128)(2,1)S(1)}, bf16[2,128,256]{2,1,0:T(8,128)(2,1)S(1)}, u32[]{:S(2)}, u32[]{:S(2)}) collective-permute-start(bf16[2,128,256]{2,1,0:T(8,128)(2,1)S(1)} %get-tuple-element.83), channel_id=1, source_target_pairs={{0,16},{4,20},{8,24},{12,28},{16,0},{20,4},{24,8},{28,12},{1,17},{... | collective-permute-start | bytes 393224 | tf_op jit(solution)/shard_map/ppermute | solution.py:35
  64.2 7.4 %collective-permute-start.23 = (bf16[2,128,256]{2,1,0:T(8,128)(2,1)S(1)}, bf16[2,128,256]{2,1,0:T(8,128)(2,1)S(1)}, u32[]{:S(2)}, u32[]{:S(2)}) collective-permute-start(bf16[2,128,256]{2,1,0:T(8,128)(2,1)S(1)} %get-tuple-element.84), channel_id=1, source_target_pairs={{0,8},{4,12},{8,0},{12,4},{16,24},{20,28},{24,16},{28,20},{1,9},{5... | collective-permute-start | bytes 393224 | tf_op jit(solution)/shard_map/ppermute | solution.py:35
  66.8 11.8 %all-to-all-start = ((f32[32,1,128]{2,1,0:T(1,128)}), f32[32,1,128]{2,1,0:T(1,128)S(1)}, u32[]{:S(2)}, u32[]{:S(2)}) async-start(f32[32,1,128]{2,1,0:T(1,128)} %bitcast.9), calls=%async_computation | async-start | bytes 32768 | tf_op jit(solution)/shard_map/all_to_all | solution.py:449
  (9 other events, 45.8 us)

commit v5 on v4

--- a/solution.py
+++ b/solution.py
@@ -18,7 +18,7 @@
 BF16 = jnp.bfloat16
 F32 = jnp.float32
 PARAMS = pltpu.CompilerParams(vmem_limit_bytes=40 * 1024 * 1024)
-COSTS = {"gather": 0.3, "gate": 1, "place_keys": 0.5, "router": 1}
+COSTS = {"place_keys": 0.5, "router": 1}
 VMEM = pl.BlockSpec(memory_space=pltpu.VMEM)
 ANY = pl.BlockSpec(memory_space=pl.ANY)
 HBM = pl.BlockSpec(memory_space=pltpu.HBM)
@@ -382,7 +382,7 @@
         counts, table, key_own, query_own, kq_in,
     ))
     v_own, sent = call(
-        kernel(gather_values_kernel), "gather_values", [((total, wide), BF16)] * 2, counts, *values, wait=kq[-1:]
+        kernel(gather_values_kernel), "gather_values", [((total, wide), BF16)] * 2, counts, *values
     )
     v_in = swapped(sent)
     gated = spread(call(

time: 79.3 us -> 78.3 us (0.987)
  starting transfers between devices: 44.3 us -> 40.9 us
  waiting for transfers between devices: 15 us -> 16.5 us
    ppermute x18, waiting for transfers between devices: 9.32 us -> 12.3 us  [spread(): lax.ppermute(pieces[m], 'seq', [(i, i ^ 2 * m) for i in range(size)])]
    all_to_all x1, waiting for transfers between devices: 3.83 us -> 1.24 us  [per_device(): lax.all_to_all(part.reshape(devices, -1), ('seq', 'fsdp'), 0, 0, tiled=True)]
    ppermute x18, starting transfers between devices: 32.1 us -> 29.9 us  [spread(): lax.ppermute(pieces[m], 'seq', [(i, i ^ 2 * m) for i in range(size)])]
    ppermute x6, waiting for transfers between devices: 1.85 us -> 2.93 us  [swapped(): lax.ppermute(array, 'seq', [(i, i ^ 1) for i in range(lax.axis_size('seq'...]
  transfers between devices with their start and end apart: 25 -> 25, of which waited for: 11 -> 9; matrix products, arithmetic and copies ran while one was open for 0% -> 0% of each run, Pallas kernels for 9% -> 10%
where the time goes in v5:
time: 78.3 us; the launch traced here: 78.1 us
  starting transfers between devices  40.9 us (52%)
  waiting for transfers between devices  16.5 us (21%)
  Pallas kernels  12.6 us (16%)
  blocking collectives  5.15 us (7%)
  local copies, waits for them, and re-layouts  1.52 us (2%)
  between operations  1.44 us (2%)
    ppermute x18, starting transfers between devices, spread(): lax.ppermute(pieces[m], 'seq', [(i, i ^ 2 * m) for i in range(size)])  29.9 us
    ppermute x18, waiting for transfers between devices, spread(): lax.ppermute(pieces[m], 'seq', [(i, i ^ 2 * m) for i in range(size)])  12.3 us
    pallas_call x16, Pallas kernels, call(): pl.pallas_call(body, in_specs=[SMEM if a.shape == (1, 1) else VMEM for a...  9.67 us
    ppermute x6, starting transfers between devices, swapped(): lax.ppermute(array, 'seq', [(i, i ^ 1) for i in range(lax.axis_size('seq'...  6.91 us
    all_gather x1, blocking collectives, per_device(): router_full = lax.all_gather(router_weight, 'fsdp', axis=0, tiled=True)  5.15 us
    all_to_all x1, starting transfers between devices, per_device(): lax.all_to_all(part.reshape(devices, -1), ('seq', 'fsdp'), 0, 0, tiled=True)  4.05 us
    ppermute x6, waiting for transfers between devices, swapped(): lax.ppermute(array, 'seq', [(i, i ^ 1) for i in range(lax.axis_size('seq'...  2.93 us
    pallas_call x1, Pallas kernels, per_device(): pl.pallas_call(kernel(front_kernel), in_specs=[SMEM] + [HBM] * 4, out_spe...  2.9 us
  transfers between devices with their start and end apart: 25, of which 9 were waited for; matrix products, arithmetic and copies ran while one was open for 0% of the time, Pallas kernels for 10%

profile of v5, /device:TPU:0, one launch (start us, length us, event | category | flops | bytes accessed | tf_op | source)
XLA Modules:
  0.0 78.1 jit_solution(16942923276417763107)
XLA Ops:
  1.3 2.9 %front.1 = (bf16[2,128,256]{2,1,0:T(8,128)(2,1)}, bf16[2,128,256]{2,1,0:T(8,128)(2,1)}, bf16[2,128,256]{2,1,0:T(8,128)(2,1)}, bf16[2,128,256]{2,1,0:T(8,128)(2,1...) custom-call(s32[1,1]{1,0:T(1,128)S(6)} %copy.13.counts.refs_0_, s32[1,128]{1,0:T(1,128)} %pos_ref.1, ...), custom_call_target="tpu_custom_call" | custom-call | flops 1000000 | bytes 65536 | tf_op jit(solution)/shard_map/front/pallas_call | solution.py:355
  4.2 3.0 %collective-permute-start.4 = (bf16[2,128,1024]{2,1,0:T(8,128)(2,1)}, bf16[2,128,1024]{2,1,0:T(8,128)(2,1)S(1)}, u32[]{:S(2)}, u32[]{:S(2)}) collective-permute-start(bf16[2,128,1024]{2,1,0:T(8,128)(2,1)} %get-tuple-element.55), channel_id=1, source_target_pairs={{0,4},{4,0},{8,12},{12,8},{16,20},{20,16},{24,28},{28,24},{1,5},{5... | collective-permute-start | bytes 1572872 | tf_op jit(solution)/shard_map/ppermute | solution.py:29
  7.2 3.6 %collective-permute-start = (bf16[2,128,256]{2,1,0:T(8,128)(2,1)}, bf16[2,128,256]{2,1,0:T(8,128)(2,1)S(1)}, u32[]{:S(2)}, u32[]{:S(2)}) collective-permute-start(bf16[2,128,256]{2,1,0:T(8,128)(2,1)} %get-tuple-element.49), channel_id=1, source_target_pairs={{0,24},{4,28},{8,16},{12,20},{16,8},{20,12},{24,0},{28,4},{1,25},{... | collective-permute-start | bytes 393224 | tf_op jit(solution)/shard_map/ppermute | solution.py:35
  11.6 5.2 %all_gather.3 = bf16[4096]{0:T(1024)(128)(2,1)S(1)} all-gather(bf16[1024]{0:T(1024)(128)(2,1)S(1)} %copy-done.6), channel_id=1, replica_groups=mesh['seq'=8,'fsdp'=4] {'fsdp'}, dimensions={0}, use_global_device_ids=true | all-gather | bytes 10240 | tf_op jit(solution)/shard_map/all_gather | solution.py:373
  18.9 2.9 %collective-permute-done.1.refs_2_ = bf16[2,128,256]{2,1,0:T(8,128)(2,1)S(1)} collective-permute-done((bf16[2,128,256]{2,1,0:T(8,128)(2,1)}, bf16[2,128,256]{2,1,0:T(8,128)(2,1)S(1)}, u32[]{:S(2)}, u32[]{:S(2)}) %collective-permute-start.1) | collective-permute-done | bytes 131104 | tf_op jit(solution)/shard_map/ppermute | solution.py:35
  23.3 2.5 %collective-permute-start.5 = (bf16[2,128,256]{2,1,0:T(8,128)(2,1)S(1)}, bf16[2,128,256]{2,1,0:T(8,128)(2,1)S(1)}, u32[]{:S(2)}, u32[]{:S(2)}) collective-permute-start(bf16[2,128,256]{2,1,0:T(8,128)(2,1)S(1)} %get-tuple-element.56), channel_id=1, source_target_pairs={{0,24},{4,28},{8,16},{12,20},{16,8},{20,12},{24,0},{28,4},{1,25},{... | collective-permute-start | bytes 393224 | tf_op jit(solution)/shard_map/ppermute | solution.py:35
  25.8 1.9 %collective-permute-start.7 = (bf16[2,128,256]{2,1,0:T(8,128)(2,1)S(1)}, bf16[2,128,256]{2,1,0:T(8,128)(2,1)S(1)}, u32[]{:S(2)}, u32[]{:S(2)}) collective-permute-start(bf16[2,128,256]{2,1,0:T(8,128)(2,1)S(1)} %get-tuple-element.58), channel_id=1, source_target_pairs={{0,8},{4,12},{8,0},{12,4},{16,24},{20,28},{24,16},{28,20},{1,9},{5... | collective-permute-start | bytes 393224 | tf_op jit(solution)/shard_map/ppermute | solution.py:35
  28.0 3.7 %collective-permute-start.9 = (bf16[128,256]{1,0:T(8,128)(2,1)S(1)}, bf16[128,256]{1,0:T(8,128)(2,1)S(1)}, u32[]{:S(2)}, u32[]{:S(2)}) collective-permute-start(bf16[128,256]{1,0:T(8,128)(2,1)S(1)} %get-tuple-element.62), channel_id=1, source_target_pairs={{0,24},{4,28},{8,16},{12,20},{16,8},{20,12},{24,0},{28,4},{1,25},{... | collective-permute-start | bytes 196616 | tf_op jit(solution)/shard_map/ppermute | solution.py:35
  32.8 2.1 %collective-permute-start.10 = (bf16[128,256]{1,0:T(8,128)(2,1)S(1)}, bf16[128,256]{1,0:T(8,128)(2,1)S(1)}, u32[]{:S(2)}, u32[]{:S(2)}) collective-permute-start(bf16[128,256]{1,0:T(8,128)(2,1)S(1)} %get-tuple-element.63), channel_id=1, source_target_pairs={{0,16},{4,20},{8,24},{12,28},{16,0},{20,4},{24,8},{28,12},{1,17},{... | collective-permute-start | bytes 196616 | tf_op jit(solution)/shard_map/ppermute | solution.py:35
  34.9 2.0 %collective-permute-start.11 = (bf16[128,256]{1,0:T(8,128)(2,1)S(1)}, bf16[128,256]{1,0:T(8,128)(2,1)S(1)}, u32[]{:S(2)}, u32[]{:S(2)}) collective-permute-start(bf16[128,256]{1,0:T(8,128)(2,1)S(1)} %get-tuple-element.64), channel_id=1, source_target_pairs={{0,8},{4,12},{8,0},{12,4},{16,24},{20,28},{24,16},{28,20},{1,9},{5... | collective-permute-start | bytes 196616 | tf_op jit(solution)/shard_map/ppermute | solution.py:35
  36.9 2.5 %collective-permute-done.6.refs_4_ = bf16[2,128,256]{2,1,0:T(8,128)(2,1)S(1)} collective-permute-done((bf16[2,128,256]{2,1,0:T(8,128)(2,1)S(1)}, bf16[2,128,256]{2,1,0:T(8,128)(2,1)S(1)}, u32[]{:S(2)}, u32[]{:S(2)}) %collective-permute-start.6) | collective-permute-done | bytes 131104 | tf_op jit(solution)/shard_map/ppermute | solution.py:35
  39.5 2.2 %collective-permute-done.10.refs_3_ = bf16[128,256]{1,0:T(8,128)(2,1)S(1)} collective-permute-done((bf16[128,256]{1,0:T(8,128)(2,1)S(1)}, bf16[128,256]{1,0:T(8,128)(2,1)S(1)}, u32[]{:S(2)}, u32[]{:S(2)}) %collective-permute-start.10) | collective-permute-done | bytes 65568 | tf_op jit(solution)/shard_map/ppermute | solution.py:35
  41.6 1.3 %probabilities.1 = (bf16[528,256]{1,0:T(8,128)(2,1)S(1)}, bf16[2,4,512,128]{3,2,1,0:T(8,128)(2,1)S(1)}) custom-call(s32[1,1]{1,0:T(1,128)S(6)} %copy.13.counts.refs_0_, bf16[3,512,256]{2,1,0:T(8,128)(2,1)S(1)} %gather.1.refs_1_, bf16[128,256]{1,0:T(8,128)(2,1)S(1)} %collective-permute-done.9.refs_2_, bf16[128,256]{1,0:T(8,128)(2,1)S(1)} %collective-permute-done.10.refs_3_, ...), custom_call_target="tpu_custom_call" | custom-call | flops 1000000 | bytes 65536 | tf_op jit(solution)/shard_map/probabilities/pallas_call | solution.py:50
  42.9 1.3 %collective-permute-start.12 = (bf16[528,256]{1,0:T(8,128)(2,1)S(1)}, bf16[528,256]{1,0:T(8,128)(2,1)S(1)}, u32[]{:S(2)}, u32[]{:S(2)}) collective-permute-start(bf16[528,256]{1,0:T(8,128)(2,1)S(1)} %get-tuple-element.67.refs_3_.refs_1_), channel_id=1, source_target_pairs={{0,4},{4,0},{8,12},{12,8},{16,20},{20,16},{24,28},{28,24},{1,5},{5... | collective-permute-start | bytes 811016 | tf_op jit(solution)/shard_map/ppermute | solution.py:29
  44.7 1.9 %collective-permute-start.16 = (bf16[128,256]{1,0:T(8,128)(2,1)S(1)}, bf16[128,256]{1,0:T(8,128)(2,1)S(1)}, u32[]{:S(2)}, u32[]{:S(2)}) collective-permute-start(bf16[128,256]{1,0:T(8,128)(2,1)S(1)} %get-tuple-element.73), channel_id=1, source_target_pairs={{0,24},{4,28},{8,16},{12,20},{16,8},{20,12},{24,0},{28,4},{1,25},{... | collective-permute-start | bytes 196616 | tf_op jit(solution)/shard_map/ppermute | solution.py:35
  46.6 2.5 %collective-permute-start.18 = (bf16[128,256]{1,0:T(8,128)(2,1)S(1)}, bf16[128,256]{1,0:T(8,128)(2,1)S(1)}, u32[]{:S(2)}, u32[]{:S(2)}) collective-permute-start(bf16[128,256]{1,0:T(8,128)(2,1)S(1)} %get-tuple-element.75), channel_id=1, source_target_pairs={{0,8},{4,12},{8,0},{12,4},{16,24},{20,28},{24,16},{28,20},{1,9},{5... | collective-permute-start | bytes 196616 | tf_op jit(solution)/shard_map/ppermute | solution.py:35
  49.1 1.8 %collective-permute-done.12.refs_4_.refs_2_ = bf16[528,256]{1,0:T(8,128)(2,1)S(1)} collective-permute-done((bf16[528,256]{1,0:T(8,128)(2,1)S(1)}, bf16[528,256]{1,0:T(8,128)(2,1)S(1)}, u32[]{:S(2)}, u32[]{:S(2)}) %collective-permute-start.12) | collective-permute-done | bytes 270368 | tf_op jit(solution)/shard_map/ppermute | solution.py:29
  51.4 2.4 %collective-permute-start.13 = (bf16[144,256]{1,0:T(8,128)(2,1)S(1)}, bf16[144,256]{1,0:T(8,128)(2,1)S(1)}, u32[]{:S(2)}, u32[]{:S(2)}) collective-permute-start(bf16[144,256]{1,0:T(8,128)(2,1)S(1)} %get-tuple-element.69), channel_id=1, source_target_pairs={{0,24},{4,28},{8,16},{12,20},{16,8},{20,12},{24,0},{28,4},{1,25},{... | collective-permute-start | bytes 221192 | tf_op jit(solution)/shard_map/ppermute | solution.py:35
  53.8 2.1 %collective-permute-start.15 = (bf16[144,256]{1,0:T(8,128)(2,1)S(1)}, bf16[144,256]{1,0:T(8,128)(2,1)S(1)}, u32[]{:S(2)}, u32[]{:S(2)}) collective-permute-start(bf16[144,256]{1,0:T(8,128)(2,1)S(1)} %get-tuple-element.71), channel_id=1, source_target_pairs={{0,8},{4,12},{8,0},{12,4},{16,24},{20,28},{24,16},{28,20},{1,9},{5... | collective-permute-start | bytes 221192 | tf_op jit(solution)/shard_map/ppermute | solution.py:35
  58.1 1.6 %collective-permute-done.14.refs_3_ = bf16[144,256]{1,0:T(8,128)(2,1)S(1)} collective-permute-done((bf16[144,256]{1,0:T(8,128)(2,1)S(1)}, bf16[144,256]{1,0:T(8,128)(2,1)S(1)}, u32[]{:S(2)}, u32[]{:S(2)}) %collective-permute-start.14) | collective-permute-done | bytes 73760 | tf_op jit(solution)/shard_map/ppermute | solution.py:35
  61.0 2.1 %collective-permute-start.21 = (bf16[2,128,256]{2,1,0:T(8,128)(2,1)}, bf16[2,128,256]{2,1,0:T(8,128)(2,1)S(1)}, u32[]{:S(2)}, u32[]{:S(2)}) collective-permute-start(bf16[2,128,256]{2,1,0:T(8,128)(2,1)} %get-tuple-element.82), channel_id=1, source_target_pairs={{0,24},{4,28},{8,16},{12,20},{16,8},{20,12},{24,0},{28,4},{1,25},{... | collective-permute-start | bytes 393224 | tf_op jit(solution)/shard_map/ppermute | solution.py:35
  63.2 2.2 %collective-permute-start.23 = (bf16[2,128,256]{2,1,0:T(8,128)(2,1)S(1)}, bf16[2,128,256]{2,1,0:T(8,128)(2,1)S(1)}, u32[]{:S(2)}, u32[]{:S(2)}) collective-permute-start(bf16[2,128,256]{2,1,0:T(8,128)(2,1)S(1)} %get-tuple-element.84), channel_id=1, source_target_pairs={{0,8},{4,12},{8,0},{12,4},{16,24},{20,28},{24,16},{28,20},{1,9},{5... | collective-permute-start | bytes 393224 | tf_op jit(solution)/shard_map/ppermute | solution.py:35
  66.4 4.0 %all-to-all-start = ((f32[32,1,128]{2,1,0:T(1,128)}), f32[32,1,128]{2,1,0:T(1,128)S(1)}, u32[]{:S(2)}, u32[]{:S(2)}) async-start(f32[32,1,128]{2,1,0:T(1,128)} %bitcast.9), calls=%async_computation | async-start | bytes 32768 | tf_op jit(solution)/shard_map/all_to_all | solution.py:449
  70.4 2.8 %collective-permute-done.22.refs_2_ = bf16[2,128,256]{2,1,0:T(8,128)(2,1)S(1)} collective-permute-done((bf16[2,128,256]{2,1,0:T(8,128)(2,1)}, bf16[2,128,256]{2,1,0:T(8,128)(2,1)S(1)}, u32[]{:S(2)}, u32[]{:S(2)}) %collective-permute-start.22) | collective-permute-done | bytes 131104 | tf_op jit(solution)/shard_map/ppermute | solution.py:35
  (59 shorter events, 15.9 us)
Async XLA Ops:
  4.2 18.3 %collective-permute-start.4 = (bf16[2,128,1024]{2,1,0:T(8,128)(2,1)}, bf16[2,128,1024]{2,1,0:T(8,128)(2,1)S(1)}, u32[]{:S(2)}, u32[]{:S(2)}) collective-permute-start(bf16[2,128,1024]{2,1,0:T(8,128)(2,1)} %get-tuple-element.55), channel_id=1, source_target_pairs={{0,4},{4,0},{8,12},{12,8},{16,20},{20,16},{24,28},{28,24},{1,5},{5... | collective-permute-start | bytes 1572872 | tf_op jit(solution)/shard_map/ppermute | solution.py:29
  7.2 11.7 %collective-permute-start = (bf16[2,128,256]{2,1,0:T(8,128)(2,1)}, bf16[2,128,256]{2,1,0:T(8,128)(2,1)S(1)}, u32[]{:S(2)}, u32[]{:S(2)}) collective-permute-start(bf16[2,128,256]{2,1,0:T(8,128)(2,1)} %get-tuple-element.49), channel_id=1, source_target_pairs={{0,24},{4,28},{8,16},{12,20},{16,8},{20,12},{24,0},{28,4},{1,25},{... | collective-permute-start | bytes 393224 | tf_op jit(solution)/shard_map/ppermute | solution.py:35
  10.8 11.0 %collective-permute-start.1 = (bf16[2,128,256]{2,1,0:T(8,128)(2,1)}, bf16[2,128,256]{2,1,0:T(8,128)(2,1)S(1)}, u32[]{:S(2)}, u32[]{:S(2)}) collective-permute-start(bf16[2,128,256]{2,1,0:T(8,128)(2,1)} %get-tuple-element.50), channel_id=1, source_target_pairs={{0,16},{4,20},{8,24},{12,28},{16,0},{20,4},{24,8},{28,12},{1,17},{... | collective-permute-start | bytes 393224 | tf_op jit(solution)/shard_map/ppermute | solution.py:35
  10.8 11.0 %collective-permute-start.2 = (bf16[2,128,256]{2,1,0:T(8,128)(2,1)}, bf16[2,128,256]{2,1,0:T(8,128)(2,1)S(1)}, u32[]{:S(2)}, u32[]{:S(2)}) collective-permute-start(bf16[2,128,256]{2,1,0:T(8,128)(2,1)} %get-tuple-element.51), channel_id=1, source_target_pairs={{0,8},{4,12},{8,0},{12,4},{16,24},{20,28},{24,16},{28,20},{1,9},{5... | collective-permute-start | bytes 393224 | tf_op jit(solution)/shard_map/ppermute | solution.py:35
  18.6 9.2 %collective-permute-start.8 = (bf16[128,1024]{1,0:T(8,128)(2,1)S(1)}, bf16[128,1024]{1,0:T(8,128)(2,1)S(1)}, u32[]{:S(2)}, u32[]{:S(2)}) collective-permute-start(bf16[128,1024]{1,0:T(8,128)(2,1)S(1)} %get-tuple-element.61), channel_id=1, source_target_pairs={{0,4},{4,0},{8,12},{12,8},{16,20},{20,16},{24,28},{28,24},{1,5},{5... | collective-permute-start | bytes 786440 | tf_op jit(solution)/shard_map/ppermute | solution.py:29
  21.9 10.8 %collective-permute-start.3 = (bf16[512,256]{1,0:T(8,128)(2,1)S(1)}, bf16[512,256]{1,0:T(8,128)(2,1)S(1)}, u32[]{:S(2)}, u32[]{:S(2)}) collective-permute-start(bf16[512,256]{1,0:T(8,128)(2,1)S(1)} %get-tuple-element.54), channel_id=1, source_target_pairs={{0,4},{4,0},{8,12},{12,8},{16,20},{20,16},{24,28},{28,24},{1,5},{5... | collective-permute-start | bytes 786440 | tf_op jit(solution)/shard_map/ppermute | solution.py:29
  23.3 11.6 %collective-permute-start.5 = (bf16[2,128,256]{2,1,0:T(8,128)(2,1)S(1)}, bf16[2,128,256]{2,1,0:T(8,128)(2,1)S(1)}, u32[]{:S(2)}, u32[]{:S(2)}) collective-permute-start(bf16[2,128,256]{2,1,0:T(8,128)(2,1)S(1)} %get-tuple-element.56), channel_id=1, source_target_pairs={{0,24},{4,28},{8,16},{12,20},{16,8},{20,12},{24,0},{28,4},{1,25},{... | collective-permute-start | bytes 393224 | tf_op jit(solution)/shard_map/ppermute | solution.py:35
  25.8 13.5 %collective-permute-start.6 = (bf16[2,128,256]{2,1,0:T(8,128)(2,1)S(1)}, bf16[2,128,256]{2,1,0:T(8,128)(2,1)S(1)}, u32[]{:S(2)}, u32[]{:S(2)}) collective-permute-start(bf16[2,128,256]{2,1,0:T(8,128)(2,1)S(1)} %get-tuple-element.57), channel_id=1, source_target_pairs={{0,16},{4,20},{8,24},{12,28},{16,0},{20,4},{24,8},{28,12},{1,17},{... | collective-permute-start | bytes 393224 | tf_op jit(solution)/shard_map/ppermute | solution.py:35
  25.8 13.5 %collective-permute-start.7 = (bf16[2,128,256]{2,1,0:T(8,128)(2,1)S(1)}, bf16[2,128,256]{2,1,0:T(8,128)(2,1)S(1)}, u32[]{:S(2)}, u32[]{:S(2)}) collective-permute-start(bf16[2,128,256]{2,1,0:T(8,128)(2,1)S(1)} %get-tuple-element.58), channel_id=1, source_target_pairs={{0,8},{4,12},{8,0},{12,4},{16,24},{20,28},{24,16},{28,20},{1,9},{5... | collective-permute-start | bytes 393224 | tf_op jit(solution)/shard_map/ppermute | solution.py:35
  28.0 11.4 %collective-permute-start.9 = (bf16[128,256]{1,0:T(8,128)(2,1)S(1)}, bf16[128,256]{1,0:T(8,128)(2,1)S(1)}, u32[]{:S(2)}, u32[]{:S(2)}) collective-permute-start(bf16[128,256]{1,0:T(8,128)(2,1)S(1)} %get-tuple-element.62), channel_id=1, source_target_pairs={{0,24},{4,28},{8,16},{12,20},{16,8},{20,12},{24,0},{28,4},{1,25},{... | collective-permute-start | bytes 196616 | tf_op jit(solution)/shard_map/ppermute | solution.py:35
  32.8 8.9 %collective-permute-start.10 = (bf16[128,256]{1,0:T(8,128)(2,1)S(1)}, bf16[128,256]{1,0:T(8,128)(2,1)S(1)}, u32[]{:S(2)}, u32[]{:S(2)}) collective-permute-start(bf16[128,256]{1,0:T(8,128)(2,1)S(1)} %get-tuple-element.63), channel_id=1, source_target_pairs={{0,16},{4,20},{8,24},{12,28},{16,0},{20,4},{24,8},{28,12},{1,17},{... | collective-permute-start | bytes 196616 | tf_op jit(solution)/shard_map/ppermute | solution.py:35
  34.9 6.7 %collective-permute-start.11 = (bf16[128,256]{1,0:T(8,128)(2,1)S(1)}, bf16[128,256]{1,0:T(8,128)(2,1)S(1)}, u32[]{:S(2)}, u32[]{:S(2)}) collective-permute-start(bf16[128,256]{1,0:T(8,128)(2,1)S(1)} %get-tuple-element.64), channel_id=1, source_target_pairs={{0,8},{4,12},{8,0},{12,4},{16,24},{20,28},{24,16},{28,20},{1,9},{5... | collective-permute-start | bytes 196616 | tf_op jit(solution)/shard_map/ppermute | solution.py:35
  42.9 8.0 %collective-permute-start.12 = (bf16[528,256]{1,0:T(8,128)(2,1)S(1)}, bf16[528,256]{1,0:T(8,128)(2,1)S(1)}, u32[]{:S(2)}, u32[]{:S(2)}) collective-permute-start(bf16[528,256]{1,0:T(8,128)(2,1)S(1)} %get-tuple-element.67.refs_3_.refs_1_), channel_id=1, source_target_pairs={{0,4},{4,0},{8,12},{12,8},{16,20},{20,16},{24,28},{28,24},{1,5},{5... | collective-permute-start | bytes 811016 | tf_op jit(solution)/shard_map/ppermute | solution.py:29
  44.7 9.1 %collective-permute-start.16 = (bf16[128,256]{1,0:T(8,128)(2,1)S(1)}, bf16[128,256]{1,0:T(8,128)(2,1)S(1)}, u32[]{:S(2)}, u32[]{:S(2)}) collective-permute-start(bf16[128,256]{1,0:T(8,128)(2,1)S(1)} %get-tuple-element.73), channel_id=1, source_target_pairs={{0,24},{4,28},{8,16},{12,20},{16,8},{20,12},{24,0},{28,4},{1,25},{... | collective-permute-start | bytes 196616 | tf_op jit(solution)/shard_map/ppermute | solution.py:35
  46.6 10.0 %collective-permute-start.17 = (bf16[128,256]{1,0:T(8,128)(2,1)S(1)}, bf16[128,256]{1,0:T(8,128)(2,1)S(1)}, u32[]{:S(2)}, u32[]{:S(2)}) collective-permute-start(bf16[128,256]{1,0:T(8,128)(2,1)S(1)} %get-tuple-element.74), channel_id=1, source_target_pairs={{0,16},{4,20},{8,24},{12,28},{16,0},{20,4},{24,8},{28,12},{1,17},{... | collective-permute-start | bytes 196616 | tf_op jit(solution)/shard_map/ppermute | solution.py:35
  46.6 10.0 %collective-permute-start.18 = (bf16[128,256]{1,0:T(8,128)(2,1)S(1)}, bf16[128,256]{1,0:T(8,128)(2,1)S(1)}, u32[]{:S(2)}, u32[]{:S(2)}) collective-permute-start(bf16[128,256]{1,0:T(8,128)(2,1)S(1)} %get-tuple-element.75), channel_id=1, source_target_pairs={{0,8},{4,12},{8,0},{12,4},{16,24},{20,28},{24,16},{28,20},{1,9},{5... | collective-permute-start | bytes 196616 | tf_op jit(solution)/shard_map/ppermute | solution.py:35
  51.4 6.7 %collective-permute-start.13 = (bf16[144,256]{1,0:T(8,128)(2,1)S(1)}, bf16[144,256]{1,0:T(8,128)(2,1)S(1)}, u32[]{:S(2)}, u32[]{:S(2)}) collective-permute-start(bf16[144,256]{1,0:T(8,128)(2,1)S(1)} %get-tuple-element.69), channel_id=1, source_target_pairs={{0,24},{4,28},{8,16},{12,20},{16,8},{20,12},{24,0},{28,4},{1,25},{... | collective-permute-start | bytes 221192 | tf_op jit(solution)/shard_map/ppermute | solution.py:35
  53.8 6.0 %collective-permute-start.14 = (bf16[144,256]{1,0:T(8,128)(2,1)S(1)}, bf16[144,256]{1,0:T(8,128)(2,1)S(1)}, u32[]{:S(2)}, u32[]{:S(2)}) collective-permute-start(bf16[144,256]{1,0:T(8,128)(2,1)S(1)} %get-tuple-element.70), channel_id=1, source_target_pairs={{0,16},{4,20},{8,24},{12,28},{16,0},{20,4},{24,8},{28,12},{1,17},{... | collective-permute-start | bytes 221192 | tf_op jit(solution)/shard_map/ppermute | solution.py:35
  57.0 17.3 %collective-permute-start.20 = (bf16[128,1024]{1,0:T(8,128)(2,1)S(1)}, bf16[128,1024]{1,0:T(8,128)(2,1)S(1)}, u32[]{:S(2)}, u32[]{:S(2)}) collective-permute-start(bf16[128,1024]{1,0:T(8,128)(2,1)S(1)} %get-tuple-element.81), channel_id=1, source_target_pairs={{0,4},{4,0},{8,12},{12,8},{16,20},{20,16},{24,28},{28,24},{1,5},{5... | collective-permute-start | bytes 786440 | tf_op jit(solution)/shard_map/ppermute | solution.py:29
  60.2 15.1 %collective-permute-start.19 = (bf16[128,1024]{1,0:T(8,128)(2,1)S(1)}, bf16[128,1024]{1,0:T(8,128)(2,1)S(1)}, u32[]{:S(2)}, u32[]{:S(2)}) collective-permute-start(bf16[128,1024]{1,0:T(8,128)(2,1)S(1)} %get-tuple-element.79), channel_id=1, source_target_pairs={{0,4},{4,0},{8,12},{12,8},{16,20},{20,16},{24,28},{28,24},{1,5},{5... | collective-permute-start | bytes 786440 | tf_op jit(solution)/shard_map/ppermute | solution.py:29
  61.0 9.4 %collective-permute-start.21 = (bf16[2,128,256]{2,1,0:T(8,128)(2,1)}, bf16[2,128,256]{2,1,0:T(8,128)(2,1)S(1)}, u32[]{:S(2)}, u32[]{:S(2)}) collective-permute-start(bf16[2,128,256]{2,1,0:T(8,128)(2,1)} %get-tuple-element.82), channel_id=1, source_target_pairs={{0,24},{4,28},{8,16},{12,20},{16,8},{20,12},{24,0},{28,4},{1,25},{... | collective-permute-start | bytes 393224 | tf_op jit(solution)/shard_map/ppermute | solution.py:35
  63.2 10.0 %collective-permute-start.22 = (bf16[2,128,256]{2,1,0:T(8,128)(2,1)}, bf16[2,128,256]{2,1,0:T(8,128)(2,1)S(1)}, u32[]{:S(2)}, u32[]{:S(2)}) collective-permute-start(bf16[2,128,256]{2,1,0:T(8,128)(2,1)} %get-tuple-element.83), channel_id=1, source_target_pairs={{0,16},{4,20},{8,24},{12,28},{16,0},{20,4},{24,8},{28,12},{1,17},{... | collective-permute-start | bytes 393224 | tf_op jit(solution)/shard_map/ppermute | solution.py:35
  63.2 10.0 %collective-permute-start.23 = (bf16[2,128,256]{2,1,0:T(8,128)(2,1)S(1)}, bf16[2,128,256]{2,1,0:T(8,128)(2,1)S(1)}, u32[]{:S(2)}, u32[]{:S(2)}) collective-permute-start(bf16[2,128,256]{2,1,0:T(8,128)(2,1)S(1)} %get-tuple-element.84), channel_id=1, source_target_pairs={{0,8},{4,12},{8,0},{12,4},{16,24},{20,28},{24,16},{28,20},{1,9},{5... | collective-permute-start | bytes 393224 | tf_op jit(solution)/shard_map/ppermute | solution.py:35
  66.4 11.2 %all-to-all-start = ((f32[32,1,128]{2,1,0:T(1,128)}), f32[32,1,128]{2,1,0:T(1,128)S(1)}, u32[]{:S(2)}, u32[]{:S(2)}) async-start(f32[32,1,128]{2,1,0:T(1,128)} %bitcast.9), calls=%async_computation | async-start | bytes 32768 | tf_op jit(solution)/shard_map/all_to_all | solution.py:449
  (8 other events, 40.7 us)
